TPU v7x, 512 devices: a whole 4x4x16 slice. The times are simulated.
512 devices in a mesh: bx: 16 (over x, z_lo), by: 32 (over z_hi, y, core).
Axes of the slice: x: 4, y: 4, z: 16 (z_hi: 4, z_lo: 4; z = z_hi * 4 + z_lo), core: 2. Of those that a mesh axis runs over, the one named last changes fastest.
Arguments:
- cells_in: float32 [2048, 5, 4096], P(('bx', 'by')), may hold values from -0.5 to 2, as said below
- block_levels: int32 [2048], P(('bx', 'by')), may hold values from 0 to 2
- send_x: int32 [512, 1], P(('bx', 'by')), may hold values from 0 to 3, as said below
- send_y: int32 [512, 1], P(('bx', 'by')), may hold values from 0 to 3, as said below
- layout: int32 [512, 3], P(('bx', 'by')), may hold values from -1 to 5, as said below
- face_out: int32 [512, 4, 4], P(('bx', 'by')), may hold values from 0 to 23, as said below
- ghost_src: int32 [512, 4, 6], P(('bx', 'by')), may hold values from 0 to 39
Outputs:
- cells_out: float32 [1536, 5, 4096], P(('bx', 'by'))
Inputs may be any that keep to these rules, and one draw needn't show every extreme that they name: `cells_in`: fields 0 and 4 (density, pressure) lie in 1 to 2, fields 1 to 3 (velocities) in -0.5 to 0.5. Per device, send_x and send_y together name 2 distinct slots. Per device, send_x and send_y together name 2 distinct slots. `layout`: each device's codes name each of 4 to 5 once, at most 1 distinct own slots that neither send list names, and -1 for empty slots; some device keeps 1 own slots and some keeps none. `face_out`: entries are face numbers slot * 6 + face of the sending device, distinct within one device and direction.
All inputs are finite; a program needn't handle non-finite values.
Results may differ from a plain program's by a relative error of at most 0.0003.
Values sent between devices are 32-bit elements; how exact they have to be, the bound alone decides.
No kernel may reach another device: no remote copies, remote signals or barrier semaphores. Data moves between devices by JAX's collectives and lax.ppermute only.
A program may use at most 64 MiB of HBM per device.

v0:
```python
import jax
import jax.numpy as jnp
from jax import lax
from jax.sharding import PartitionSpec as P

B = 16


gamma_gas = 1.4
step_base = 0.05


def extended_2(cells, sides, width):
    for axis, dim in sides:
        count = lax.axis_size(axis)
        head = lax.slice_in_dim(cells, 0, width, axis=dim)
        tail = lax.slice_in_dim(cells, cells.shape[dim] - width, cells.shape[dim], axis=dim)
        cells = jnp.concatenate(
            [
                lax.ppermute(tail, axis, [(i, (i + 1) % count) for i in range(count)]),
                cells,
                lax.ppermute(head, axis, [((i + 1) % count, i) for i in range(count)]),
            ],
            axis=dim,
        )
    return cells


def from_partner(shard, axis, distance):
    return lax.ppermute(shard, axis, [(i, i ^ 1 << distance) for i in range(lax.axis_size(axis))])


def face_table(blocks):
    number = blocks.shape[0]
    cube_cells = blocks.reshape(number, 5, B, B, B)
    layer_pairs = [
        (cube_cells[:, :, 0], cube_cells[:, :, 1]),
        (cube_cells[:, :, B - 1], cube_cells[:, :, B - 2]),
        (cube_cells[:, :, :, 0], cube_cells[:, :, :, 1]),
        (cube_cells[:, :, :, B - 1], cube_cells[:, :, :, B - 2]),
        (cube_cells[:, :, :, :, 0], cube_cells[:, :, :, :, 1]),
        (cube_cells[:, :, :, :, B - 1], cube_cells[:, :, :, :, B - 2]),
    ]
    face_set = jnp.stack([jnp.stack(layer_pair, axis=2) for layer_pair in layer_pairs], axis=1)
    return face_set.reshape(number * 6, 5, 2 * B * B)


def minmod_slope(left_diff, right_diff):
    return (
        0.5
        * (jnp.sign(left_diff) + jnp.sign(right_diff))
        * jnp.minimum(jnp.abs(left_diff), jnp.abs(right_diff))
    )


def euler_flux(states, normal):
    density = states[0]
    pressure = states[4]
    normal_vel = states[normal]
    kinetic = (
        0.5 * density * (states[1] * states[1] + states[2] * states[2] + states[3] * states[3])
    )
    energy = pressure / (gamma_gas - 1.0) + kinetic
    cons_rows = [density] + [density * states[column] for column in range(1, 4)] + [energy]
    flux_rows = [density * normal_vel]
    for column in range(1, 4):
        update_term = density * states[column] * normal_vel
        if column == normal:
            update_term = update_term + pressure
        flux_rows.append(update_term)
    flux_rows.append(normal_vel * (energy + pressure))
    signal = jnp.abs(normal_vel) + jnp.sqrt(gamma_gas * pressure / density)
    return (jnp.stack(flux_rows), jnp.stack(cons_rows), signal)


def sweep(extended, normal, ratio_dt):
    length = extended.shape[1] - 4
    deltas = extended[:, 1:] - extended[:, :-1]
    slopes = minmod_slope(deltas[:, :-1], deltas[:, 1:])
    centre = extended[:, 1 : length + 3]
    density = centre[0]
    normal_vel = centre[normal]
    pressure = centre[4]
    advance = [-(normal_vel * slopes[0] + density * slopes[normal])]
    for column in range(1, 4):
        update_term = normal_vel * slopes[column]
        if column == normal:
            update_term = update_term + slopes[4] / density
        advance.append(-update_term)
    advance.append(-(normal_vel * slopes[4] + gamma_gas * pressure * slopes[normal]))
    half_step = 0.5 * ratio_dt * jnp.stack(advance)
    lower_face = centre - 0.5 * slopes + half_step
    upper_face = centre + 0.5 * slopes + half_step
    left_flux, left_cons, left_signal = euler_flux(upper_face[:, : length + 1], normal)
    right_flux, right_cons, right_signal = euler_flux(lower_face[:, 1 : length + 2], normal)
    face_flux = 0.5 * (left_flux + right_flux) - 0.5 * jnp.maximum(left_signal, right_signal) * (
        right_cons - left_cons
    )
    return face_flux[:, 1:] - face_flux[:, :-1]


def extend_cells(interior, low_side, high_side):
    return jnp.concatenate(
        [low_side[:, 1:2], low_side[:, 0:1], interior, high_side[:, 0:1], high_side[:, 1:2]], axis=1
    )


def update_block(cells, ghosts, ratio_dt):
    cube_cells = cells.reshape(5, B, B, B)
    ghost_cube = ghosts.reshape(6, 5, 2, B, B)
    along_x = extend_cells(cube_cells, ghost_cube[0], ghost_cube[1]).reshape(5, B + 4, B * B)
    along_y = extend_cells(cube_cells.transpose(0, 2, 1, 3), ghost_cube[2], ghost_cube[3]).reshape(
        5, B + 4, B * B
    )
    along_z = extend_cells(cube_cells.transpose(0, 3, 1, 2), ghost_cube[4], ghost_cube[5]).reshape(
        5, B + 4, B * B
    )
    change_x = sweep(along_x, 1, ratio_dt).reshape(5, B, B, B)
    change_y = sweep(along_y, 2, ratio_dt).reshape(5, B, B, B).transpose(0, 2, 1, 3)
    change_z = sweep(along_z, 3, ratio_dt).reshape(5, B, B, B).transpose(0, 2, 3, 1)
    flat = cube_cells.reshape(5, B * B * B)
    density = flat[0]
    kinetic = 0.5 * density * (flat[1] * flat[1] + flat[2] * flat[2] + flat[3] * flat[3])
    initial = jnp.stack(
        [
            density,
            density * flat[1],
            density * flat[2],
            density * flat[3],
            flat[4] / (gamma_gas - 1.0) + kinetic,
        ]
    )
    total = (change_x + change_y + change_z).reshape(5, B * B * B)
    return initial - ratio_dt * total


def update_many(operands):
    return update_block(operands[0], operands[1], operands[2])


def on_device(cells_in, block_levels, send_x, send_y, layout, face_out, ghost_src):
    slots = cells_in.shape[0]
    face_set = face_table(cells_in)
    outgoing = face_set[face_out[0]]
    across_x = extended_2(jnp.stack([outgoing[1], outgoing[0]]), (("bx", 0),), 1)
    across_y = extended_2(jnp.stack([outgoing[3], outgoing[2]]), (("by", 0),), 1)
    ghost_table = jnp.concatenate(
        [face_set, across_x[0], across_x[3], across_y[0], across_y[3]], axis=0
    )
    ghosts = ghost_table[ghost_src[0].reshape(-1)].reshape(slots, 6, 5, 2 * B * B)
    step_sizes = step_base * jnp.exp2(block_levels.astype(jnp.float32))
    slot_codes = layout[0]
    filled = slot_codes >= 0
    chosen = jnp.maximum(slot_codes, 0)
    bit_x = lax.axis_size("bx").bit_length() - 2
    bit_y = lax.axis_size("by").bit_length() - 2
    list_x = send_x[0]
    list_y = send_y[0]
    moved_x = from_partner((cells_in[list_x], ghosts[list_x], step_sizes[list_x]), "bx", bit_x)
    moved_y = from_partner((cells_in[list_y], ghosts[list_y], step_sizes[list_y]), "by", bit_y)
    pool_cells = jnp.concatenate([cells_in, moved_x[0], moved_y[0]], axis=0)
    pool_ghosts = jnp.concatenate([ghosts, moved_x[1], moved_y[1]], axis=0)
    pool_steps = jnp.concatenate([step_sizes, moved_x[2], moved_y[2]], axis=0)
    result = lax.map(update_many, (pool_cells[chosen], pool_ghosts[chosen], pool_steps[chosen]))
    return jnp.where(filled[:, None, None], result, jnp.zeros_like(result))


def solution(mesh):
    return jax.shard_map(
        on_device,
        mesh=mesh,
        in_specs=(
            P(("bx", "by"), None, None),
            P(("bx", "by")),
            P(("bx", "by"), None),
            P(("bx", "by"), None),
            P(("bx", "by"), None),
            P(("bx", "by"), None, None),
            P(("bx", "by"), None, None),
        ),
        out_specs=P(("bx", "by"), None, None),
        check_vma=False,
    )
```

profile of v0, /device:TPU:2, one launch (start us, length us, event | category | flops | bytes accessed | tf_op | source)
XLA Modules:
  0.0 153.3 jit_solution(15105479052091290197)
XLA Ops:
  0.0 2.0 %reshape.252 = f32[4,5,16,16,16]{4,3,2,0,1:T(8,128)S(1)} reshape(f32[4,5,4096]{2,0,1:T(4,128)} %param.9) | data formatting | bytes 655360 | tf_op jit(solution)/shard_map/reshape | solution.py:35
  4.0 6.2 %fusion.34 = (f32[4,5,16,16,1]{4,3,2,0,1:T(8,128)}, f32[4,5,16,16,1]{4,3,2,0,1:T(8,128)}, f32[4,5,16,16,1]{4,3,2,0,1:T(8,128)}, f32[4,5,16,16,1]{4,3,2,0,1:T(8,128)}) fusion(f32[4,5,16,16,16]{4,3,2,0,1:T(8,128)S(1)} %reshape.252), kind=kLoop, calls=%fused_computation.230 | loop fusion | bytes 163840 | tf_op jit(solution)/shard_map/slice | solution.py:42
  10.2 4.5 %copy.166 = f32[4,5,16,16,1]{3,2,1,0,4:T(8,128)} copy(f32[4,5,16,16,1]{4,3,2,0,1:T(8,128)} %get-tuple-element.215) | data formatting | bytes 40960 | tf_op jit(solution)/shard_map/slice | solution.py:41
  14.6 2.6 %copy.167 = f32[4,5,16,16,1]{3,2,1,0,4:T(8,128)} copy(f32[4,5,16,16,1]{4,3,2,0,1:T(8,128)S(1)} %copy-done.1) | data formatting | bytes 40960 | tf_op jit(solution)/shard_map/slice | solution.py:41
  17.2 4.5 %copy.170 = f32[4,5,16,16,1]{3,2,1,0,4:T(8,128)} copy(f32[4,5,16,16,1]{4,3,2,0,1:T(8,128)} %get-tuple-element.213) | data formatting | bytes 40960 | tf_op jit(solution)/shard_map/slice | solution.py:42
  21.7 2.6 %copy.171 = f32[4,5,16,16,1]{3,2,1,0,4:T(8,128)} copy(f32[4,5,16,16,1]{4,3,2,0,1:T(8,128)S(1)} %copy-done) | data formatting | bytes 40960 | tf_op jit(solution)/shard_map/slice | solution.py:42
  24.3 1.7 %fusion.26 = f32[4,6,5,2,16,16]{5,4,0,2,3,1:T(8,128)} fusion(f32[4,6,5,2,16,16]{5,4,0,2,3,1:T(8,128)} %fusion.29, f32[4,5,1,16,16]{4,3,0,1,2:T(8,128)} %get-tuple-element.222, f32[4,5,1,16,16]{4,3,0,1,2:T(8,128)S(1)} %get-tuple-element.221), kind=kLoop, calls=%fused_computation.190 | loop fusion | flops 10240 | bytes 512000
  28.3 0.8 bitcast_dynamic-update-slice_fusion
  29.1 1.8 %copy.189 = f32[4,6,5,2,16,16]{5,4,3,2,1,0:T(8,128)S(1)} copy(f32[4,6,5,2,16,16]{5,4,0,2,3,1:T(8,128)} %bitcast_dynamic-update-slice_fusion) | data formatting | bytes 491520 | tf_op jit(solution)/shard_map/reshape | solution.py:45
  31.0 1.2 reshape.433
  32.9 3.8 %collective-permute-start.4 = (f32[1,4,5,512]{3,2,1,0:T(8,128)S(1)}, f32[1,4,5,512]{3,2,1,0:T(8,128)S(1)}, u32[]{:S(2)}, u32[]{:S(2)}) collective-permute-start(f32[1,4,5,512]{3,2,1,0:T(8,128)S(1)} %get-tuple-element.230), channel_id=1, source_target_pairs={{0,32},{32,64},{64,96},{96,128},{128,160},{160,192},{192,224},{224... | collective-permute-start | bytes 122888 | tf_op jit(solution)/shard_map/ppermute | solution.py:20
  36.7 4.7 %collective-permute-start.5 = (f32[1,4,5,512]{3,2,1,0:T(8,128)S(1)}, f32[1,4,5,512]{3,2,1,0:T(8,128)S(1)}, u32[]{:S(2)}, u32[]{:S(2)}) collective-permute-start(f32[1,4,5,512]{3,2,1,0:T(8,128)S(1)} %get-tuple-element.229), channel_id=1, source_target_pairs={{32,0},{64,32},{96,64},{128,96},{160,128},{192,160},{224,192},{256... | collective-permute-start | bytes 122888 | tf_op jit(solution)/shard_map/ppermute | solution.py:22
  41.4 1.9 %collective-permute-start.6 = (f32[1,4,5,512]{3,2,1,0:T(8,128)S(1)}, f32[1,4,5,512]{3,2,1,0:T(8,128)S(1)}, u32[]{:S(2)}, u32[]{:S(2)}) collective-permute-start(f32[1,4,5,512]{3,2,1,0:T(8,128)S(1)} %get-tuple-element.228), channel_id=1, source_target_pairs={{0,1},{1,2},{2,3},{3,4},{4,5},{5,6},{6,7},{7,8},{8,9},{9,10},{10,1... | collective-permute-start | bytes 122888 | tf_op jit(solution)/shard_map/ppermute | solution.py:20
  43.4 14.1 %collective-permute-start.7 = (f32[1,4,5,512]{3,2,1,0:T(8,128)S(1)}, f32[1,4,5,512]{3,2,1,0:T(8,128)S(1)}, u32[]{:S(2)}, u32[]{:S(2)}) collective-permute-start(f32[1,4,5,512]{3,2,1,0:T(8,128)S(1)} %get-tuple-element.227), channel_id=1, source_target_pairs={{1,0},{2,1},{3,2},{4,3},{5,4},{6,5},{7,6},{8,7},{9,8},{10,9},{11,1... | collective-permute-start | bytes 122888 | tf_op jit(solution)/shard_map/ppermute | solution.py:22
  59.4 4.0 %collective-permute-start.2 = (f32[1]{0:T(128)}, f32[1]{0:T(128)}, u32[]{:S(2)}, u32[]{:S(2)}) collective-permute-start(f32[1]{0:T(128)} %get-tuple-element.231), channel_id=1, source_target_pairs={{0,256},{32,288},{64,320},{96,352},{128,384},{160,416},{192,448},{... | collective-permute-start | bytes 20 | tf_op jit(solution)/shard_map/ppermute | solution.py:30
  63.9 2.6 %collective-permute-done.2 = f32[1]{0:T(128)} collective-permute-done((f32[1]{0:T(128)}, f32[1]{0:T(128)}, u32[]{:S(2)}, u32[]{:S(2)}) %collective-permute-start.2) | collective-permute-done | bytes 36 | tf_op jit(solution)/shard_map/ppermute | solution.py:30
  66.5 11.3 %collective-permute-start.3 = (f32[1]{0:T(128)}, f32[1]{0:T(128)}, u32[]{:S(2)}, u32[]{:S(2)}) collective-permute-start(f32[1]{0:T(128)} %get-tuple-element.232), channel_id=1, source_target_pairs={{0,16},{1,17},{2,18},{3,19},{4,20},{5,21},{6,22},{7,23},{8,24},{9,... | collective-permute-start | bytes 20 | tf_op jit(solution)/shard_map/ppermute | solution.py:30
  77.8 2.8 %collective-permute-done.3 = f32[1]{0:T(128)} collective-permute-done((f32[1]{0:T(128)}, f32[1]{0:T(128)}, u32[]{:S(2)}, u32[]{:S(2)}) %collective-permute-start.3) | collective-permute-done | bytes 36 | tf_op jit(solution)/shard_map/ppermute | solution.py:30
  80.7 4.0 %collective-permute-start = (f32[1,5,4096]{2,1,0:T(8,128)S(1)}, f32[1,5,4096]{2,1,0:T(8,128)S(1)}, u32[]{:S(2)}, u32[]{:S(2)}) collective-permute-start(f32[1,5,4096]{2,1,0:T(8,128)S(1)} %get-tuple-element.223), channel_id=1, source_target_pairs={{0,256},{32,288},{64,320},{96,352},{128,384},{160,416},{192,448},{... | collective-permute-start | bytes 245768 | tf_op jit(solution)/shard_map/ppermute | solution.py:30
  84.7 1.4 pad_maximum_fusion.16
  86.7 11.3 %collective-permute-start.1 = (f32[1,5,4096]{2,1,0:T(8,128)S(1)}, f32[1,5,4096]{2,1,0:T(8,128)S(1)}, u32[]{:S(2)}, u32[]{:S(2)}) collective-permute-start(f32[1,5,4096]{2,1,0:T(8,128)S(1)} %get-tuple-element.224), channel_id=1, source_target_pairs={{0,16},{1,17},{2,18},{3,19},{4,20},{5,21},{6,22},{7,23},{8,24},{9,... | collective-permute-start | bytes 245768 | tf_op jit(solution)/shard_map/ppermute | solution.py:30
  98.9 3.3 %collective-permute-start.8 = (f32[1,6,5,512]{3,1,2,0:T(8,128)S(1)}, f32[1,6,5,512]{3,1,2,0:T(8,128)S(1)}, u32[]{:S(2)}, u32[]{:S(2)}) collective-permute-start(f32[1,6,5,512]{3,1,2,0:T(8,128)S(1)} %get-tuple-element.225), channel_id=1, source_target_pairs={{0,256},{32,288},{64,320},{96,352},{128,384},{160,416},{192,448},{... | collective-permute-start | bytes 184328 | tf_op jit(solution)/shard_map/ppermute | solution.py:30
  102.2 3.4 %collective-permute-start.9 = (f32[1,6,5,512]{3,1,2,0:T(8,128)S(1)}, f32[1,6,5,512]{3,1,2,0:T(8,128)S(1)}, u32[]{:S(2)}, u32[]{:S(2)}) collective-permute-start(f32[1,6,5,512]{3,1,2,0:T(8,128)S(1)} %get-tuple-element.226), channel_id=1, source_target_pairs={{0,16},{1,17},{2,18},{3,19},{4,20},{5,21},{6,22},{7,23},{8,24},{9,... | collective-permute-start | bytes 184328 | tf_op jit(solution)/shard_map/ppermute | solution.py:30
  106.7 10.5 %collective-permute-done.9 = f32[1,6,5,512]{3,1,2,0:T(8,128)S(1)} collective-permute-done((f32[1,6,5,512]{3,1,2,0:T(8,128)S(1)}, f32[1,6,5,512]{3,1,2,0:T(8,128)S(1)}, u32[]{:S(2)}, u32[]{:S(2)}) %collective-permute-start.9) | collective-permute-done | bytes 61472 | tf_op jit(solution)/shard_map/ppermute | solution.py:30
  117.9 33.5 %while.17 = (s32[]{:T(128)}, f32[3,5,4096]{2,0,1:T(4,128)}, f32[3,5,4096]{2,1,0:T(8,128)S(1)}, f32[3]{0:T(128)S(1)}, f32[3,6,5,512]{3,1,2,0:T(8,128)S(1)}) while((s32[]{:T(128)}, f32[3,5,4096]{2,0,1:T(4,128)}, f32[3,5,4096]{2,1,0:T(8,128)S(1)}, f32[3]{0:T(128)S(1)}, f32[3,6,5,512]{3,1,2,0:T(8,128)S(1)}) %tuple.181), condition=%wide.region_1.2_spmd.clone, body=%wide.region_0.1_spmd.sunk.clone | while | flops 3417337 | bytes 15378641 | solution.py:164
  124.6 0.9 fusion.61
  126.4 2.7 %dynamic_update_slice.6 = f32[3,5,4096]{2,0,1:T(4,128)} dynamic-update-slice(f32[3,5,4096]{2,0,1:T(4,128)} %get-tuple-element.487, f32[1,5,4096]{2,0,1:T(1,128)S(1)} %copy.244, s32[]{:T(128)} %get-tuple-element.486, s32[]{:T(128)} %constant.20.clone.1..sunk.1, s32[]{:T(128)} %constant.20.clone.1..sunk.1) | dynamic-update-slice | bytes 163844 | tf_op jit(solution)/shard_map/while/body/jit(dynamic_update_index_in_dim)/dynamic_update_slice | solution.py:164
  135.7 0.9 fusion.61
  137.5 2.7 %dynamic_update_slice.6 = f32[3,5,4096]{2,0,1:T(4,128)} dynamic-update-slice(f32[3,5,4096]{2,0,1:T(4,128)} %get-tuple-element.487, f32[1,5,4096]{2,0,1:T(1,128)S(1)} %copy.244, s32[]{:T(128)} %get-tuple-element.486, s32[]{:T(128)} %constant.20.clone.1..sunk.1, s32[]{:T(128)} %constant.20.clone.1..sunk.1) | dynamic-update-slice | bytes 163844 | tf_op jit(solution)/shard_map/while/body/jit(dynamic_update_index_in_dim)/dynamic_update_slice | solution.py:164
  146.9 0.9 fusion.61
  148.7 2.7 %dynamic_update_slice.6 = f32[3,5,4096]{2,0,1:T(4,128)} dynamic-update-slice(f32[3,5,4096]{2,0,1:T(4,128)} %get-tuple-element.487, f32[1,5,4096]{2,0,1:T(1,128)S(1)} %copy.244, s32[]{:T(128)} %get-tuple-element.486, s32[]{:T(128)} %constant.20.clone.1..sunk.1, s32[]{:T(128)} %constant.20.clone.1..sunk.1) | dynamic-update-slice | bytes 163844 | tf_op jit(solution)/shard_map/while/body/jit(dynamic_update_index_in_dim)/dynamic_update_slice | solution.py:164
  151.4 1.8 %broadcast_select_fusion = f32[3,5,4096]{2,0,1:T(4,128)} fusion(f32[3,5,4096]{2,0,1:T(4,128)} %get-tuple-element.32, pred[3]{0:T(512)(128)(4,1)S(1)} %compare_bitcast_fusion), kind=kLoop, calls=%fused_computation.203 | loop fusion | flops 61440 | bytes 491523 | tf_op jit(solution)/shard_map/jit(_where)/select_n | solution.py:165
  (385 shorter events, 27.9 us)
Async XLA Ops:
  10.2 4.5 %copy-start.1 = (f32[4,5,16,16,1]{4,3,2,0,1:T(8,128)S(1)}, f32[4,5,16,16,1]{4,3,2,0,1:T(8,128)}, u32[]{:S(2)}) copy-start(f32[4,5,16,16,1]{4,3,2,0,1:T(8,128)} %get-tuple-element.214) | copy-start | bytes 61444
  17.2 4.5 %copy-start = (f32[4,5,16,16,1]{4,3,2,0,1:T(8,128)S(1)}, f32[4,5,16,16,1]{4,3,2,0,1:T(8,128)}, u32[]{:S(2)}) copy-start(f32[4,5,16,16,1]{4,3,2,0,1:T(8,128)} %get-tuple-element.216) | copy-start | bytes 61444
  24.3 3.2 %copy-start.3 = (f32[4,5,16,16,1]{3,2,1,0,4:T(8,128)S(1)}, f32[4,5,16,16,1]{3,2,1,0,4:T(8,128)}, u32[]{:S(2)}) copy-start(f32[4,5,16,16,1]{3,2,1,0,4:T(8,128)} %copy.166) | copy-start | bytes 61444
  24.3 3.2 %copy-start.5 = (f32[4,5,16,16,1]{3,2,1,0,4:T(8,128)S(1)}, f32[4,5,16,16,1]{3,2,1,0,4:T(8,128)}, u32[]{:S(2)}) copy-start(f32[4,5,16,16,1]{3,2,1,0,4:T(8,128)} %copy.167) | copy-start | bytes 61444
  24.3 4.0 %copy-start.4 = (f32[4,5,16,16,1]{3,2,1,0,4:T(8,128)S(1)}, f32[4,5,16,16,1]{3,2,1,0,4:T(8,128)}, u32[]{:S(2)}) copy-start(f32[4,5,16,16,1]{3,2,1,0,4:T(8,128)} %copy.170) | copy-start | bytes 61444
  24.3 4.0 %copy-start.6 = (f32[4,5,16,16,1]{3,2,1,0,4:T(8,128)S(1)}, f32[4,5,16,16,1]{3,2,1,0,4:T(8,128)}, u32[]{:S(2)}) copy-start(f32[4,5,16,16,1]{3,2,1,0,4:T(8,128)} %copy.171) | copy-start | bytes 61444
  31.0 1.2 copy-start.8
  31.0 27.8 %copy-start.9 = (s32[4]{0:T(128)S(1)}, s32[4]{0:T(128)}, u32[]{:S(2)}) copy-start(s32[4]{0:T(128)} %param.10) | copy-start | bytes 52
  31.0 32.5 %copy-start.2 = (f32[4,5,4096]{2,0,1:T(4,128)S(1)}, f32[4,5,4096]{2,0,1:T(4,128)}, u32[]{:S(2)}) copy-start(f32[4,5,4096]{2,0,1:T(4,128)} %param.9) | copy-start | bytes 983044
  31.0 32.7 %copy-start.10 = (s32[1,3]{1,0:T(1,128)S(1)}, s32[1,3]{1,0:T(1,128)}, u32[]{:S(2)}) copy-start(s32[1,3]{1,0:T(1,128)} %param.13) | copy-start | bytes 40
  31.0 32.8 %copy-start.7 = (s32[1,4,6]{2,1,0:T(4,128)S(1)}, s32[1,4,6]{2,1,0:T(4,128)}, u32[]{:S(2)}) copy-start(s32[1,4,6]{2,1,0:T(4,128)} %param.15) | copy-start | bytes 292
  32.9 53.8 %collective-permute-start.4 = (f32[1,4,5,512]{3,2,1,0:T(8,128)S(1)}, f32[1,4,5,512]{3,2,1,0:T(8,128)S(1)}, u32[]{:S(2)}, u32[]{:S(2)}) collective-permute-start(f32[1,4,5,512]{3,2,1,0:T(8,128)S(1)} %get-tuple-element.230), channel_id=1, source_target_pairs={{0,32},{32,64},{64,96},{96,128},{128,160},{160,192},{192,224},{224... | collective-permute-start | bytes 122888 | tf_op jit(solution)/shard_map/ppermute | solution.py:20
  36.7 61.3 %collective-permute-start.5 = (f32[1,4,5,512]{3,2,1,0:T(8,128)S(1)}, f32[1,4,5,512]{3,2,1,0:T(8,128)S(1)}, u32[]{:S(2)}, u32[]{:S(2)}) collective-permute-start(f32[1,4,5,512]{3,2,1,0:T(8,128)S(1)} %get-tuple-element.229), channel_id=1, source_target_pairs={{32,0},{64,32},{96,64},{128,96},{160,128},{192,160},{224,192},{256... | collective-permute-start | bytes 122888 | tf_op jit(solution)/shard_map/ppermute | solution.py:22
  41.4 56.6 %collective-permute-start.6 = (f32[1,4,5,512]{3,2,1,0:T(8,128)S(1)}, f32[1,4,5,512]{3,2,1,0:T(8,128)S(1)}, u32[]{:S(2)}, u32[]{:S(2)}) collective-permute-start(f32[1,4,5,512]{3,2,1,0:T(8,128)S(1)} %get-tuple-element.228), channel_id=1, source_target_pairs={{0,1},{1,2},{2,3},{3,4},{4,5},{5,6},{6,7},{7,8},{8,9},{9,10},{10,1... | collective-permute-start | bytes 122888 | tf_op jit(solution)/shard_map/ppermute | solution.py:20
  43.4 54.7 %collective-permute-start.7 = (f32[1,4,5,512]{3,2,1,0:T(8,128)S(1)}, f32[1,4,5,512]{3,2,1,0:T(8,128)S(1)}, u32[]{:S(2)}, u32[]{:S(2)}) collective-permute-start(f32[1,4,5,512]{3,2,1,0:T(8,128)S(1)} %get-tuple-element.227), channel_id=1, source_target_pairs={{1,0},{2,1},{3,2},{4,3},{5,4},{6,5},{7,6},{8,7},{9,8},{10,9},{11,1... | collective-permute-start | bytes 122888 | tf_op jit(solution)/shard_map/ppermute | solution.py:22
  59.4 7.1 %collective-permute-start.2 = (f32[1]{0:T(128)}, f32[1]{0:T(128)}, u32[]{:S(2)}, u32[]{:S(2)}) collective-permute-start(f32[1]{0:T(128)} %get-tuple-element.231), channel_id=1, source_target_pairs={{0,256},{32,288},{64,320},{96,352},{128,384},{160,416},{192,448},{... | collective-permute-start | bytes 20 | tf_op jit(solution)/shard_map/ppermute | solution.py:30
  66.5 14.1 %collective-permute-start.3 = (f32[1]{0:T(128)}, f32[1]{0:T(128)}, u32[]{:S(2)}, u32[]{:S(2)}) collective-permute-start(f32[1]{0:T(128)} %get-tuple-element.232), channel_id=1, source_target_pairs={{0,16},{1,17},{2,18},{3,19},{4,20},{5,21},{6,22},{7,23},{8,24},{9,... | collective-permute-start | bytes 20 | tf_op jit(solution)/shard_map/ppermute | solution.py:30
  80.7 25.0 %collective-permute-start = (f32[1,5,4096]{2,1,0:T(8,128)S(1)}, f32[1,5,4096]{2,1,0:T(8,128)S(1)}, u32[]{:S(2)}, u32[]{:S(2)}) collective-permute-start(f32[1,5,4096]{2,1,0:T(8,128)S(1)} %get-tuple-element.223), channel_id=1, source_target_pairs={{0,256},{32,288},{64,320},{96,352},{128,384},{160,416},{192,448},{... | collective-permute-start | bytes 245768 | tf_op jit(solution)/shard_map/ppermute | solution.py:30
  86.7 18.9 %collective-permute-start.1 = (f32[1,5,4096]{2,1,0:T(8,128)S(1)}, f32[1,5,4096]{2,1,0:T(8,128)S(1)}, u32[]{:S(2)}, u32[]{:S(2)}) collective-permute-start(f32[1,5,4096]{2,1,0:T(8,128)S(1)} %get-tuple-element.224), channel_id=1, source_target_pairs={{0,16},{1,17},{2,18},{3,19},{4,20},{5,21},{6,22},{7,23},{8,24},{9,... | collective-permute-start | bytes 245768 | tf_op jit(solution)/shard_map/ppermute | solution.py:30
  98.9 7.8 %collective-permute-start.8 = (f32[1,6,5,512]{3,1,2,0:T(8,128)S(1)}, f32[1,6,5,512]{3,1,2,0:T(8,128)S(1)}, u32[]{:S(2)}, u32[]{:S(2)}) collective-permute-start(f32[1,6,5,512]{3,1,2,0:T(8,128)S(1)} %get-tuple-element.225), channel_id=1, source_target_pairs={{0,256},{32,288},{64,320},{96,352},{128,384},{160,416},{192,448},{... | collective-permute-start | bytes 184328 | tf_op jit(solution)/shard_map/ppermute | solution.py:30
  102.2 15.0 %collective-permute-start.9 = (f32[1,6,5,512]{3,1,2,0:T(8,128)S(1)}, f32[1,6,5,512]{3,1,2,0:T(8,128)S(1)}, u32[]{:S(2)}, u32[]{:S(2)}) collective-permute-start(f32[1,6,5,512]{3,1,2,0:T(8,128)S(1)} %get-tuple-element.226), channel_id=1, source_target_pairs={{0,16},{1,17},{2,18},{3,19},{4,20},{5,21},{6,22},{7,23},{8,24},{9,... | collective-permute-start | bytes 184328 | tf_op jit(solution)/shard_map/ppermute | solution.py:30
where the time goes:
time: 154 us; the launch traced here: 153 us
  starting transfers between devices  61.9 us (40%)
  local copies, waits for them, and re-layouts  53.2 us (35%)
  waiting for transfers between devices  16.4 us (11%)
  other arithmetic  16.1 us (10%)
  loops' own time  3.97 us (3%)
  between operations  1.71 us (1%)
    ppermute x6, starting transfers between devices, from_partner(): lax.ppermute(shard, axis, [(i, i ^ 1 << distance) for i in range(lax.axis...  37.4 us
    ppermute x2, starting transfers between devices, extended_2(): lax.ppermute(head, axis, [((i + 1) % count, i) for i in range(count)])  18.8 us
    ppermute x6, waiting for transfers between devices, from_partner(): lax.ppermute(shard, axis, [(i, i ^ 1 << distance) for i in range(lax.axis...  16.4 us
    slice x2, local copies, waits for them, and re-layouts, face_table(): cube_cells[:, :, :, :, B - 1]  10.7 us
    dynamic_update_slice x6, local copies, waits for them, and re-layouts, on_device(): lax.map(update_many, (pool_cells[chosen], pool_ghosts[chosen], pool_steps...  8.48 us
    ppermute x2, starting transfers between devices, extended_2(): lax.ppermute(tail, axis, [(i, (i + 1) % count) for i in range(count)])  5.75 us
    slice x1, local copies, waits for them, and re-layouts, face_table(): cube_cells[:, :, :, :, 0]  4.47 us
    unnamed x4, other arithmetic  3.99 us
  transfers between devices with their start and end apart: 10, of which 4 were waited for; matrix products, arithmetic and copies ran while one was open for 3% of the time, Pallas kernels for 0%

commit v1 on v0

v1 whole, which is shorter than its diff:
```python
import functools

import jax
import jax.numpy as jnp
from jax import lax
from jax.experimental import pallas as pl
from jax.experimental.pallas import tpu as pltpu
from jax.sharding import PartitionSpec as P

B = 16
GAMMA = 1.4
STEP = 0.05
HALF = 8
FIELD_ROWS = B * 8
SWEEP_ROWS = 5 * FIELD_ROWS
BLOCK_ROWS = 5 * 2 * B
FACE_ROWS = 24
GHOST_ROWS = 4 * 8


def slot_of(field, direction):
    if field == 1:
        return 1 + direction
    if field == 1 + direction:
        return 1
    return field


def lanes(shape=(8, 128)):
    return lax.broadcasted_iota(jnp.int32, shape, 1)


def rows(shape=(8, 128)):
    return lax.broadcasted_iota(jnp.int32, shape, 0)


def take(values, index, axis):
    return jnp.take_along_axis(values, index, axis=axis, mode="promise_in_bounds")


class Turns:
    def __init__(self):
        lane, row = lanes(), rows()
        group, inner = lane // 16, lane % 16
        self.low = inner < 8
        self.skew = ((group + row) % 8) * 16 + inner
        self.shift = (row - group) % 8
        self.back = ((row - group) % 8) * 16 + inner
        source_group = (group + row) % 8
        self.skew_z = (inner % 8) * 16 + (inner // 8) * 8 + source_group
        z_low, z_high = inner % 8, inner // 8
        self.back_z = ((row - z_low) % 8) * 16 + z_high * 8 + group

    def turn(self, v):
        return take(take(take(v, self.skew, 1), self.shift, 0), self.back, 1)

    def to_z(self, v0, v1):
        t0 = take(take(take(v0, self.skew_z, 1), self.shift, 0), self.back, 1)
        t1 = take(take(take(v1, self.skew_z, 1), self.shift, 0), self.back, 1)
        first = jnp.where(self.low, t0, pltpu.roll(t1, 8, 1))
        second = jnp.where(self.low, pltpu.roll(t0, 120, 1), t1)
        return first, second

    def from_z(self, first, second):
        t0 = jnp.where(self.low, first, pltpu.roll(second, 8, 1))
        t1 = jnp.where(self.low, pltpu.roll(first, 120, 1), second)
        return tuple(
            take(take(take(t, self.skew, 1), self.shift, 0), self.back_z, 1) for t in (t0, t1)
        )


def pack_kernel(face_out, lists, cells, sweep, table, *messages):
    turns = Turns()
    for s in range(4):
        for t in range(2 * B):
            x, h = t // 2, t % 2
            sweep[s, pl.ds(x * 8 + h, 5, stride=FIELD_ROWS), :] = cells[
                s, :, t * 128 : (t + 1) * 128
            ]
        for field in range(5):
            base = field * FIELD_ROWS
            to_y = slot_of(field, 1) * FIELD_ROWS
            to_z = slot_of(field, 2) * FIELD_ROWS
            for xh in range(2):
                v = [
                    sweep[s, pl.ds(base + HALF * xh * 8 + h, 8, stride=8), :] for h in range(2)
                ]
                for h in range(2):
                    start = to_y + HALF * h * 8 + 2 + xh
                    sweep[s, pl.ds(start, 8, stride=8), :] = turns.turn(v[h])
                for zh, value in enumerate(turns.to_z(v[0], v[1])):
                    start = to_z + HALF * zh * 8 + 4 + xh
                    sweep[s, pl.ds(start, 8, stride=8), :] = value
        for face in range(6):
            direction, high = face // 2, face % 2
            for layer in range(2):
                i = B - 1 - layer if high else layer
                for h in range(2):
                    row = i * 8 + direction * 2 + h
                    to = (layer * 2 + h) * 5
                    table[s * 6 + face, to : to + 5, :] = sweep[
                        s, pl.ds(row, 5, stride=FIELD_ROWS), :
                    ]
                    if direction:
                        for field, slot in ((1, 1 + direction), (1 + direction, 1)):
                            table[s * 6 + face, to + field : to + field + 1, :] = sweep[
                                s, pl.ds(slot * FIELD_ROWS + row, 1), :
                            ]
    for m in range(4):
        listed = lists[m]
        for k in range(4):
            messages[m][k] = table[face_out[0, listed, k]]


def limited(left, right):
    return jnp.maximum(jnp.minimum(left, right), 0.0) + jnp.minimum(jnp.maximum(left, right), 0.0)


def fluxes_of(q):
    density, normal, second, third, pressure = q
    mass = density * normal
    kinetic = 0.5 * density * (normal * normal + second * second + third * third)
    energy = pressure * (1.0 / (GAMMA - 1.0)) + kinetic
    cons = (density, mass, density * second, density * third, energy)
    flux = (mass, mass * normal + pressure, mass * second, mass * third, normal * (energy + pressure))
    scaled = GAMMA * pressure
    signal = jnp.abs(normal) + scaled * lax.rsqrt(scaled * density)
    return cons, flux, signal


def step_of(level):
    return jnp.where(level == 0, STEP, jnp.where(level == 1, STEP * 2, STEP * 4))


def update_kernel(slot, levels, ghost_src, order, sweep, table, r0, r1, r2, r3, out, remote, ghost, change):
    turns = Turns()
    s = slot[0]
    ratio = step_of(levels[s])
    for m, received in enumerate((r0, r1, r2, r3)):
        for k in range(4):
            remote[m * 4 + k] = received[k]
    for face in range(6):
        direction, high = face // 2, face % 2
        code = ghost_src[0, s, face]
        far = jnp.maximum(code - 24, 0)
        far = order[far // 4] * 4 + far % 4
        near = jnp.minimum(code, 23)
        for layer in range(2):
            i = 2 + layer if high else 1 - layer
            for h in range(2):
                row = i * 8 + direction * 2 + h
                at = (layer * 2 + h) * 5
                moves = [(pl.ds(at, 5), pl.ds(row, 5, stride=GHOST_ROWS))]
                if direction:
                    for field, to in ((1, 1 + direction), (1 + direction, 1)):
                        moves.append((pl.ds(at + field, 1), pl.ds(to * GHOST_ROWS + row, 1)))
                for source, target in moves:
                    ghost[target, :] = jnp.where(
                        code < 24, table[near, source, :], remote[far, source, :]
                    )

    def cells_at(i):
        if 0 <= i < B:
            return [sweep[s, pl.ds(f * FIELD_ROWS + i * 8, 8), :] for f in range(5)]
        k = i + 2 if i < 0 else i - B + 2
        return [ghost[pl.ds(f * GHOST_ROWS + k * 8, 8), :] for f in range(5)]

    here, after = cells_at(-2), cells_at(-1)
    right = [b - a for a, b in zip(here, after)]
    left_face = last_flux = None
    for i in range(-1, B + 1):
        here, after, left = after, cells_at(i + 2 - 1), right
        right = [b - a for a, b in zip(here, after)]
        half = [0.5 * limited(a, b) for a, b in zip(left, right)]
        density, normal, _, _, pressure = here
        carried = ratio * normal
        moved = [carried * a for a in half]
        centre = [
            density - (moved[0] + ratio * density * half[1]),
            normal - (moved[1] + ratio * half[4] / density),
            here[2] - moved[2],
            here[3] - moved[3],
            pressure - (moved[4] + (ratio * GAMMA) * pressure * half[1]),
        ]
        if i >= 0:
            cons, flux, signal = fluxes_of([a - b for a, b in zip(centre, half)])
            old_cons, old_flux, old_signal = left_face
            speed = jnp.maximum(signal, old_signal)
            face_flux = [
                (fa + fb) - speed * (ub - ua)
                for fa, fb, ua, ub in zip(old_flux, flux, old_cons, cons)
            ]
            if i >= 1:
                for f in range(5):
                    change[pl.ds(f * FIELD_ROWS + (i - 1) * 8, 8), :] = face_flux[f] - last_flux[f]
            last_flux = face_flux
        if i < B:
            left_face = fluxes_of([a + b for a, b in zip(centre, half)])

    def in_place(ref, start):
        return ref[pl.ds(start, 8, stride=8), :]

    scale = 0.5 * ratio
    for xh in range(2):
        prims = [
            [sweep[s, pl.ds(f * FIELD_ROWS + HALF * xh * 8 + h, 8, stride=8), :] for h in range(2)]
            for f in range(5)
        ]
        for f in range(5):
            along_y = slot_of(f, 1) * FIELD_ROWS
            along_z = slot_of(f, 2) * FIELD_ROWS
            from_z = turns.from_z(
                *[in_place(change, along_z + HALF * zh * 8 + 4 + xh) for zh in range(2)]
            )
            for h in range(2):
                total = (
                    in_place(change, f * FIELD_ROWS + HALF * xh * 8 + h)
                    + turns.turn(in_place(change, along_y + HALF * h * 8 + 2 + xh))
                    + from_z[h]
                )
                density, u, v, w, pressure = (prims[k][h] for k in range(5))
                if f == 0:
                    initial = density
                elif f < 4:
                    initial = density * prims[f][h]
                else:
                    initial = pressure * (1.0 / (GAMMA - 1.0)) + 0.5 * density * (
                        u * u + v * v + w * w
                    )
                row = f * 2 * B + h * B + HALF * xh
                out[row : row + 8, :] = initial - scale * total


def place_kernel(layout, own, from_x, from_y, out):
    codes = [layout[0, j] for j in range(3)]
    at_x = jnp.where(codes[1] == 4, 1, jnp.where(codes[2] == 4, 2, 0))
    at_y = jnp.where(codes[1] == 5, 1, jnp.where(codes[2] == 5, 2, 0))
    at_own = 3 - at_x - at_y
    empty = codes[0] + codes[1] + codes[2] == 8
    for source, at in ((own, at_own), (from_x, at_x), (from_y, at_y)):
        for t in range(2 * B):
            row = (t % 2) * B + t // 2
            v = source[pl.ds(row, 5, stride=2 * B), :]
            if source is own:
                v = jnp.where(empty, 0.0, v)
            out[at, :, t * 128 : (t + 1) * 128] = v


SMEM = pl.BlockSpec(memory_space=pltpu.SMEM)
VMEM = pl.BlockSpec(memory_space=pltpu.VMEM)
LIMIT = 48 << 20


def struct(*shape):
    return jax.ShapeDtypeStruct(shape, jnp.float32)


def pack(face_out, lists, cells):
    return pl.pallas_call(
        pack_kernel,
        out_shape=(struct(4, SWEEP_ROWS, 128), struct(24, FACE_ROWS, 128))
        + (struct(4, FACE_ROWS, 128),) * 4,
        in_specs=[SMEM, SMEM, VMEM],
        out_specs=(VMEM,) * 6,
        compiler_params=pltpu.CompilerParams(vmem_limit_bytes=LIMIT),
        name="pack",
    )(face_out, lists, cells)


def update(name, slot, levels, ghost_src, order, sweep, table, received):
    return pl.pallas_call(
        update_kernel,
        out_shape=struct(BLOCK_ROWS, 128),
        in_specs=[SMEM] * 4 + [VMEM] * 6,
        out_specs=VMEM,
        scratch_shapes=[
            pltpu.VMEM((16, FACE_ROWS, 128), jnp.float32),
            pltpu.VMEM((5 * GHOST_ROWS, 128), jnp.float32),
            pltpu.VMEM((SWEEP_ROWS, 128), jnp.float32),
        ],
        compiler_params=pltpu.CompilerParams(vmem_limit_bytes=LIMIT),
        name=name,
    )(slot, levels, ghost_src, order, sweep, table, *received)


def place(layout, own, from_x, from_y):
    return pl.pallas_call(
        place_kernel,
        out_shape=struct(3, 5, B * B * B),
        in_specs=[SMEM] + [VMEM] * 3,
        out_specs=VMEM,
        compiler_params=pltpu.CompilerParams(vmem_limit_bytes=LIMIT),
        name="place",
    )(layout, own, from_x, from_y)


def with_pair(values, axis, odd):
    count = lax.axis_size(axis)
    mate = [((i + odd) ^ 1) - odd for i in range(count)]
    return lax.ppermute(values, axis, [(i, j % count) for i, j in enumerate(mate)])


def with_partner(values, axis):
    count = lax.axis_size(axis)
    return lax.ppermute(values, axis, [(i, i ^ (count // 2)) for i in range(count)])


def on_device(cells_in, block_levels, send_x, send_y, layout, face_out, ghost_src):
    odd_x = lax.axis_index("bx") % 2
    odd_y = lax.axis_index("by") % 2
    lists = jnp.stack([odd_x, 1 - odd_x, 2 + odd_y, 3 - odd_y]).astype(jnp.int32)
    order = jnp.stack([1 - odd_x, odd_x, 3 - odd_y, 2 + odd_y]).astype(jnp.int32)
    sweep, table, *messages = pack(face_out, lists, cells_in)
    received = [
        with_pair(messages[0], "bx", 0),
        with_pair(messages[1], "bx", 1),
        with_pair(messages[2], "by", 0),
        with_pair(messages[3], "by", 1),
    ]
    own_slot = jnp.max(jnp.where(layout < 4, layout, 0), axis=1)
    common = (block_levels, ghost_src, order, sweep, table, received)
    from_y = with_partner(update("to_y", send_y[0], *common), "by")
    from_x = with_partner(update("to_x", send_x[0], *common), "bx")
    own = update("own", own_slot, *common)
    return place(layout, own, from_x, from_y)


def solution(mesh):
    return jax.shard_map(
        on_device,
        mesh=mesh,
        in_specs=(
            P(("bx", "by"), None, None),
            P(("bx", "by")),
            P(("bx", "by"), None),
            P(("bx", "by"), None),
            P(("bx", "by"), None),
            P(("bx", "by"), None, None),
            P(("bx", "by"), None, None),
        ),
        out_specs=P(("bx", "by"), None, None),
        check_vma=False,
    )
```

time: 154 us -> 56.7 us (0.37)
  the two profiles are of different devices: /device:TPU:2 before, /device:TPU:4 now
where the time goes in v1:
time: 56.7 us; the launch traced here: 56.3 us
  starting transfers between devices  38.2 us (67%)
  Pallas kernels  9.18 us (16%)
  waiting for transfers between devices  3.97 us (7%)
  local copies, waits for them, and re-layouts  2.8 us (5%)
  between operations  1.43 us (3%)
  other arithmetic  0.8 us (1%)
    ppermute x4, starting transfers between devices, with_pair(): lax.ppermute(values, axis, [(i, j % count) for i, j in enumerate(mate)])  23.9 us
    ppermute x2, starting transfers between devices, with_partner(): lax.ppermute(values, axis, [(i, i ^ count // 2) for i in range(count)])  14.2 us
    pallas_call x3, Pallas kernels, update(): pl.pallas_call(update_kernel, out_shape=struct(BLOCK_ROWS, 128), in_specs...  4.36 us
    pallas_call x1, Pallas kernels, pack(): pl.pallas_call(pack_kernel, out_shape=(struct(4, SWEEP_ROWS, 128), struct...  4.11 us
    ppermute x2, waiting for transfers between devices, with_partner(): lax.ppermute(values, axis, [(i, i ^ count // 2) for i in range(count)])  3.12 us
    unnamed x9, local copies, waits for them, and re-layouts  1.9 us
  transfers between devices with their start and end apart: 6, of which 2 were waited for; matrix products, arithmetic and copies ran while one was open for 1% of the time, Pallas kernels for 6%

profile of v1, /device:TPU:4, one launch (start us, length us, event | category | flops | bytes accessed | tf_op | source)
XLA Modules:
  0.0 56.3 jit_solution(11008161614978712074)
XLA Ops:
  0.0 0.0 copy-start.1
  0.0 0.0 copy-start
  0.0 1.2 %copy.8.cells = f32[4,5,4096]{2,1,0:T(8,128)S(1)} copy(f32[4,5,4096]{2,0,1:T(4,128)} %param.7) | data formatting | bytes 655360 | tf_op args[0]
  1.2 0.1 pad_add_fusion.1.lists
  1.3 0.0 copy-start.2
  1.3 0.7 %copy-done.2 = s32[1,4,4]{2,1,0:T(4,128)S(1)} copy-done((s32[1,4,4]{2,1,0:T(4,128)S(1)}, s32[1,4,4]{2,1,0:T(4,128)}, u32[]{:S(2)}) %copy-start.2) | copy-done | bytes 88
  2.0 4.1 %pack.1 = (f32[4,640,128]{2,1,0:T(8,128)S(1)}, f32[24,24,128]{2,1,0:T(8,128)S(1)}, f32[4,24,128]{2,1,0:T(8,128)S(1)}, f32[4,24,128]{2,1,0:T(8,128)S(1)}, f32[4,2...) custom-call(s32[1,4,4]{2,1,0:T(4,128)S(1)} %copy-done.2, s32[4]{0:T(128)S(1)} %pad_add_fusion.1.lists, ...), custom_call_target="tpu_custom_call" | custom-call | tf_op jit(solution)/shard_map/pack/pallas_call | solution.py:259
  6.1 3.8 %collective-permute-start = (f32[4,24,128]{2,1,0:T(8,128)S(1)}, f32[4,24,128]{2,1,0:T(8,128)S(1)}, u32[]{:S(2)}, u32[]{:S(2)}) collective-permute-start(f32[4,24,128]{2,1,0:T(8,128)S(1)} %get-tuple-element.13), channel_id=1, source_target_pairs={{0,32},{32,0},{64,96},{96,64},{128,160},{160,128},{192,224},{224,1... | collective-permute-start | bytes 147464 | tf_op jit(solution)/shard_map/ppermute | solution.py:300
  9.9 4.7 %collective-permute-start.1 = (f32[4,24,128]{2,1,0:T(8,128)S(1)}, f32[4,24,128]{2,1,0:T(8,128)S(1)}, u32[]{:S(2)}, u32[]{:S(2)}) collective-permute-start(f32[4,24,128]{2,1,0:T(8,128)S(1)} %get-tuple-element.14), channel_id=1, source_target_pairs={{0,480},{32,64},{64,32},{96,128},{128,96},{160,192},{192,160},{224... | collective-permute-start | bytes 147464 | tf_op jit(solution)/shard_map/ppermute | solution.py:300
  14.6 1.9 %collective-permute-start.2 = (f32[4,24,128]{2,1,0:T(8,128)S(1)}, f32[4,24,128]{2,1,0:T(8,128)S(1)}, u32[]{:S(2)}, u32[]{:S(2)}) collective-permute-start(f32[4,24,128]{2,1,0:T(8,128)S(1)} %get-tuple-element.15), channel_id=1, source_target_pairs={{0,1},{1,0},{2,3},{3,2},{4,5},{5,4},{6,7},{7,6},{8,9},{9,8},{10,11... | collective-permute-start | bytes 147464 | tf_op jit(solution)/shard_map/ppermute | solution.py:300
  16.6 13.5 %collective-permute-start.3 = (f32[4,24,128]{2,1,0:T(8,128)S(1)}, f32[4,24,128]{2,1,0:T(8,128)S(1)}, u32[]{:S(2)}, u32[]{:S(2)}) collective-permute-start(f32[4,24,128]{2,1,0:T(8,128)S(1)} %get-tuple-element.16), channel_id=1, source_target_pairs={{0,31},{1,2},{2,1},{3,4},{4,3},{5,6},{6,5},{7,8},{8,7},{9,10},{10,... | collective-permute-start | bytes 147464 | tf_op jit(solution)/shard_map/ppermute | solution.py:300
  30.1 0.1 pad_add_fusion.order
  31.4 0.0 collective-permute-done.r0
  31.5 0.0 collective-permute-done.1.r1
  31.5 0.0 collective-permute-done.2.r2
  31.5 0.8 %collective-permute-done.3.r3 = f32[4,24,128]{2,1,0:T(8,128)S(1)} collective-permute-done((f32[4,24,128]{2,1,0:T(8,128)S(1)}, f32[4,24,128]{2,1,0:T(8,128)S(1)}, u32[]{:S(2)}, u32[]{:S(2)}) %collective-permute-start.3) | collective-permute-done | bytes 49184 | tf_op jit(solution)/shard_map/ppermute | solution.py:300
  32.3 0.0 copy-done.1
  32.3 0.0 copy-done
  32.3 1.2 %to_x.1 = f32[160,128]{1,0:T(8,128)S(1)} custom-call(s32[1]{0:T(128)} %bitcast.7.slot, s32[4]{0:T(128)S(1)} %copy-done.1, s32[1,4,6]{2,1,0:T(4,128)S(1)} %copy-done, s32[4]{0:T(128)S(1)} %pad_add_fusion.order, f32[4,640,128]{2,1,0:T(8,128)S(1)} %get-tuple-element.11.sweep, f32[24,24,128]{2,1,0:T(8,128)S(1)} %get-tuple-element.12.table, ...), custom_call_target="tpu_custom_call" | custom-call | tf_op jit(solution)/shard_map/to_x/pallas_call | solution.py:271
  33.6 0.0 copy-start.3
  33.6 4.5 %collective-permute-start.4 = (f32[160,128]{1,0:T(8,128)S(1)}, f32[160,128]{1,0:T(8,128)S(1)}, u32[]{:S(2)}, u32[]{:S(2)}) collective-permute-start(f32[160,128]{1,0:T(8,128)S(1)} %to_x.1), channel_id=1, source_target_pairs={{0,256},{32,288},{64,320},{96,352},{128,384},{160,416},{192,448},{... | collective-permute-start | bytes 245768 | tf_op jit(solution)/shard_map/ppermute | solution.py:305
  38.1 1.2 %to_y.1 = f32[160,128]{1,0:T(8,128)S(1)} custom-call(s32[1]{0:T(128)} %bitcast.8.slot, s32[4]{0:T(128)S(1)} %copy-done.1, s32[1,4,6]{2,1,0:T(4,128)S(1)} %copy-done, s32[4]{0:T(128)S(1)} %pad_add_fusion.order, f32[4,640,128]{2,1,0:T(8,128)S(1)} %get-tuple-element.11.sweep, f32[24,24,128]{2,1,0:T(8,128)S(1)} %get-tuple-element.12.table, ...), custom_call_target="tpu_custom_call" | custom-call | tf_op jit(solution)/shard_map/to_y/pallas_call | solution.py:271
  39.4 9.7 %collective-permute-start.5 = (f32[160,128]{1,0:T(8,128)S(1)}, f32[160,128]{1,0:T(8,128)S(1)}, u32[]{:S(2)}, u32[]{:S(2)}) collective-permute-start(f32[160,128]{1,0:T(8,128)S(1)} %to_y.1), channel_id=1, source_target_pairs={{0,16},{1,17},{2,18},{3,19},{4,20},{5,21},{6,22},{7,23},{8,24},{9,... | collective-permute-start | bytes 245768 | tf_op jit(solution)/shard_map/ppermute | solution.py:305
  49.1 0.0 copy-done.3
  49.1 0.6 %fusion = s32[]{:T(128)} fusion(s32[1,3]{1,0:T(1,128)S(1)} %copy-done.3), kind=kLoop, calls=%fused_computation.1 | loop fusion | flops 8 | bytes 16 | tf_op jit(solution)/shard_map/reduce_max | solution.py:320
  49.7 1.9 %own.1 = f32[160,128]{1,0:T(8,128)S(1)} custom-call(s32[1]{0:T(128)} %bitcast.slot, s32[4]{0:T(128)S(1)} %copy-done.1, s32[1,4,6]{2,1,0:T(4,128)S(1)} %copy-done, s32[4]{0:T(128)S(1)} %pad_add_fusion.order, f32[4,640,128]{2,1,0:T(8,128)S(1)} %get-tuple-element.11.sweep, f32[24,24,128]{2,1,0:T(8,128)S(1)} %get-tuple-element.12.table, ...), custom_call_target="tpu_custom_call" | custom-call | tf_op jit(solution)/shard_map/own/pallas_call | solution.py:271
  51.6 0.0 collective-permute-done.4.from_x
  51.6 3.1 %collective-permute-done.5.from_y = f32[160,128]{1,0:T(8,128)S(1)} collective-permute-done((f32[160,128]{1,0:T(8,128)S(1)}, f32[160,128]{1,0:T(8,128)S(1)}, u32[]{:S(2)}, u32[]{:S(2)}) %collective-permute-start.5) | collective-permute-done | bytes 81952 | tf_op jit(solution)/shard_map/ppermute | solution.py:305
  54.7 0.7 %place.1 = f32[3,5,4096]{2,1,0:T(8,128)S(1)} custom-call(s32[1,3]{1,0:T(1,128)S(1)} %copy-done.3, f32[160,128]{1,0:T(8,128)S(1)} %own.1, f32[160,128]{1,0:T(8,128)S(1)} %collective-permute-done.4.from_x, f32[160,128]{1,0:T(8,128)S(1)} %collective-permute-done.5.from_y), custom_call_target="tpu_custom_call" | custom-call | tf_op jit(solution)/shard_map/place/pallas_call | solution.py:287
  55.4 0.9 %copy.9 = f32[3,5,4096]{2,0,1:T(4,128)} copy(f32[3,5,4096]{2,1,0:T(8,128)S(1)} %place.1) | data formatting | bytes 491520 | tf_op jit(solution)/shard_map/place/pallas_call | solution.py:287
Async XLA Ops:
  0.0 32.3 %copy-start.1 = (s32[4]{0:T(128)S(1)}, s32[4]{0:T(128)}, u32[]{:S(2)}) copy-start(s32[4]{0:T(128)} %levels.5) | copy-start | bytes 52
  0.0 32.3 %copy-start = (s32[1,4,6]{2,1,0:T(4,128)S(1)}, s32[1,4,6]{2,1,0:T(4,128)}, u32[]{:S(2)}) copy-start(s32[1,4,6]{2,1,0:T(4,128)} %ghost_src.5) | copy-start | bytes 292
  1.3 0.7 %copy-start.2 = (s32[1,4,4]{2,1,0:T(4,128)S(1)}, s32[1,4,4]{2,1,0:T(4,128)}, u32[]{:S(2)}) copy-start(s32[1,4,4]{2,1,0:T(4,128)} %face_out.1) | copy-start | bytes 196
  6.1 25.3 %collective-permute-start = (f32[4,24,128]{2,1,0:T(8,128)S(1)}, f32[4,24,128]{2,1,0:T(8,128)S(1)}, u32[]{:S(2)}, u32[]{:S(2)}) collective-permute-start(f32[4,24,128]{2,1,0:T(8,128)S(1)} %get-tuple-element.13), channel_id=1, source_target_pairs={{0,32},{32,0},{64,96},{96,64},{128,160},{160,128},{192,224},{224,1... | collective-permute-start | bytes 147464 | tf_op jit(solution)/shard_map/ppermute | solution.py:300
  9.9 21.5 %collective-permute-start.1 = (f32[4,24,128]{2,1,0:T(8,128)S(1)}, f32[4,24,128]{2,1,0:T(8,128)S(1)}, u32[]{:S(2)}, u32[]{:S(2)}) collective-permute-start(f32[4,24,128]{2,1,0:T(8,128)S(1)} %get-tuple-element.14), channel_id=1, source_target_pairs={{0,480},{32,64},{64,32},{96,128},{128,96},{160,192},{192,160},{224... | collective-permute-start | bytes 147464 | tf_op jit(solution)/shard_map/ppermute | solution.py:300
  14.6 16.8 %collective-permute-start.2 = (f32[4,24,128]{2,1,0:T(8,128)S(1)}, f32[4,24,128]{2,1,0:T(8,128)S(1)}, u32[]{:S(2)}, u32[]{:S(2)}) collective-permute-start(f32[4,24,128]{2,1,0:T(8,128)S(1)} %get-tuple-element.15), channel_id=1, source_target_pairs={{0,1},{1,0},{2,3},{3,2},{4,5},{5,4},{6,7},{7,6},{8,9},{9,8},{10,11... | collective-permute-start | bytes 147464 | tf_op jit(solution)/shard_map/ppermute | solution.py:300
  16.6 15.8 %collective-permute-start.3 = (f32[4,24,128]{2,1,0:T(8,128)S(1)}, f32[4,24,128]{2,1,0:T(8,128)S(1)}, u32[]{:S(2)}, u32[]{:S(2)}) collective-permute-start(f32[4,24,128]{2,1,0:T(8,128)S(1)} %get-tuple-element.16), channel_id=1, source_target_pairs={{0,31},{1,2},{2,1},{3,4},{4,3},{5,6},{6,5},{7,8},{8,7},{9,10},{10,... | collective-permute-start | bytes 147464 | tf_op jit(solution)/shard_map/ppermute | solution.py:300
  33.6 15.5 %copy-start.3 = (s32[1,3]{1,0:T(1,128)S(1)}, s32[1,3]{1,0:T(1,128)}, u32[]{:S(2)}) copy-start(s32[1,3]{1,0:T(1,128)} %layout.1) | copy-start | bytes 40
  33.6 18.0 %collective-permute-start.4 = (f32[160,128]{1,0:T(8,128)S(1)}, f32[160,128]{1,0:T(8,128)S(1)}, u32[]{:S(2)}, u32[]{:S(2)}) collective-permute-start(f32[160,128]{1,0:T(8,128)S(1)} %to_x.1), channel_id=1, source_target_pairs={{0,256},{32,288},{64,320},{96,352},{128,384},{160,416},{192,448},{... | collective-permute-start | bytes 245768 | tf_op jit(solution)/shard_map/ppermute | solution.py:305
  39.4 15.4 %collective-permute-start.5 = (f32[160,128]{1,0:T(8,128)S(1)}, f32[160,128]{1,0:T(8,128)S(1)}, u32[]{:S(2)}, u32[]{:S(2)}) collective-permute-start(f32[160,128]{1,0:T(8,128)S(1)} %to_y.1), channel_id=1, source_target_pairs={{0,16},{1,17},{2,18},{3,19},{4,20},{5,21},{6,22},{7,23},{8,24},{9,... | collective-permute-start | bytes 245768 | tf_op jit(solution)/shard_map/ppermute | solution.py:305

commit v2 on v1

--- a/solution.py
+++ b/solution.py
@@ -46,6 +46,8 @@
         self.skew = ((group + row) % 8) * 16 + inner
         self.shift = (row - group) % 8
         self.back = ((row - group) % 8) * 16 + inner
+        self.skew_half = ((group + row) % 8) * 16 + (inner + 8) % 16
+        self.back_half = ((row - group) % 8) * 16 + (inner + 8) % 16
         source_group = (group + row) % 8
         self.skew_z = (inner % 8) * 16 + (inner // 8) * 8 + source_group
         z_low, z_high = inner % 8, inner // 8
@@ -55,61 +57,99 @@
         return take(take(take(v, self.skew, 1), self.shift, 0), self.back, 1)
 
     def to_z(self, v0, v1):
-        t0 = take(take(take(v0, self.skew_z, 1), self.shift, 0), self.back, 1)
-        t1 = take(take(take(v1, self.skew_z, 1), self.shift, 0), self.back, 1)
-        first = jnp.where(self.low, t0, pltpu.roll(t1, 8, 1))
-        second = jnp.where(self.low, pltpu.roll(t0, 120, 1), t1)
+        t0 = take(take(v0, self.skew_z, 1), self.shift, 0)
+        t1 = take(take(v1, self.skew_z, 1), self.shift, 0)
+        first = jnp.where(self.low, take(t0, self.back, 1), take(t1, self.back_half, 1))
+        second = jnp.where(self.low, take(t0, self.back_half, 1), take(t1, self.back, 1))
         return first, second
 
     def from_z(self, first, second):
-        t0 = jnp.where(self.low, first, pltpu.roll(second, 8, 1))
-        t1 = jnp.where(self.low, pltpu.roll(first, 120, 1), second)
-        return tuple(
-            take(take(take(t, self.skew, 1), self.shift, 0), self.back_z, 1) for t in (t0, t1)
+        t0 = jnp.where(self.low, take(first, self.skew, 1), take(second, self.skew_half, 1))
+        t1 = jnp.where(self.low, take(first, self.skew_half, 1), take(second, self.skew, 1))
+        return tuple(take(take(t, self.shift, 0), self.back_z, 1) for t in (t0, t1))
+
+
+def parities():
+    return lax.axis_index("bx") % 2, lax.axis_index("by") % 2
+
+
+def pack_kernel(
+    send_x, send_y, cells_in, layout_in, levels_in, ghost_src_in, face_out_in, *rest
+):
+    numbers, sweep, table, *messages = rest[:7]
+    cells, layout, levels, ghost_src, face_out, cells_sem, small_sem = rest[7:]
+    odd_x, odd_y = parities()
+    copies = [
+        pltpu.make_async_copy(cells_in.at[f], cells.at[f], cells_sem.at[f]) for f in range(5)
+    ]
+    small = [
+        pltpu.make_async_copy(source, target, small_sem.at[i])
+        for i, (source, target) in enumerate(
+            (
+                (face_out_in, face_out),
+                (layout_in, layout),
+                (levels_in, levels),
+                (ghost_src_in, ghost_src),
+            )
         )
-
-
-def pack_kernel(face_out, lists, cells, sweep, table, *messages):
+    ]
+    for copy in copies + small:
+        copy.start()
     turns = Turns()
-    for s in range(4):
+    for field in range(5):
+        base = field * FIELD_ROWS
+        to_y = slot_of(field, 1) * FIELD_ROWS
+        to_z = slot_of(field, 2) * FIELD_ROWS
+        copies[field].wait()
         for t in range(2 * B):
-            x, h = t // 2, t % 2
-            sweep[s, pl.ds(x * 8 + h, 5, stride=FIELD_ROWS), :] = cells[
-                s, :, t * 128 : (t + 1) * 128
+            row = base + (t // 2) * 8 + t % 2
+            sweep[pl.ds(row, 4, stride=SWEEP_ROWS), :] = cells[
+                field, :, t * 128 : (t + 1) * 128
             ]
-        for field in range(5):
-            base = field * FIELD_ROWS
-            to_y = slot_of(field, 1) * FIELD_ROWS
-            to_z = slot_of(field, 2) * FIELD_ROWS
+        for first in range(0, 4 * SWEEP_ROWS, SWEEP_ROWS):
             for xh in range(2):
                 v = [
-                    sweep[s, pl.ds(base + HALF * xh * 8 + h, 8, stride=8), :] for h in range(2)
+                    sweep[pl.ds(first + base + HALF * xh * 8 + h, 8, stride=8), :]
+                    for h in range(2)
                 ]
                 for h in range(2):
-                    start = to_y + HALF * h * 8 + 2 + xh
-                    sweep[s, pl.ds(start, 8, stride=8), :] = turns.turn(v[h])
+                    start = first + to_y + HALF * h * 8 + 2 + xh
+                    sweep[pl.ds(start, 8, stride=8), :] = turns.turn(v[h])
                 for zh, value in enumerate(turns.to_z(v[0], v[1])):
-                    start = to_z + HALF * zh * 8 + 4 + xh
-                    sweep[s, pl.ds(start, 8, stride=8), :] = value
+                    start = first + to_z + HALF * zh * 8 + 4 + xh
+                    sweep[pl.ds(start, 8, stride=8), :] = value
+    for s in range(4):
         for face in range(6):
             direction, high = face // 2, face % 2
             for layer in range(2):
                 i = B - 1 - layer if high else layer
                 for h in range(2):
-                    row = i * 8 + direction * 2 + h
+                    row = s * SWEEP_ROWS + i * 8 + direction * 2 + h
                     to = (layer * 2 + h) * 5
                     table[s * 6 + face, to : to + 5, :] = sweep[
-                        s, pl.ds(row, 5, stride=FIELD_ROWS), :
+                        pl.ds(row, 5, stride=FIELD_ROWS), :
                     ]
                     if direction:
                         for field, slot in ((1, 1 + direction), (1 + direction, 1)):
                             table[s * 6 + face, to + field : to + field + 1, :] = sweep[
-                                s, pl.ds(slot * FIELD_ROWS + row, 1), :
+                                pl.ds(slot * FIELD_ROWS + row, 1), :
                             ]
-    for m in range(4):
-        listed = lists[m]
+    for copy in small:
+        copy.wait()
+    for m, one_list in enumerate((2 + (1 - odd_y), 1 - odd_x, odd_x, 2 + odd_y)):
         for k in range(4):
-            messages[m][k] = table[face_out[0, listed, k]]
+            messages[m][k] = table[face_out[0, one_list, k]]
+    codes = [layout[0, j] for j in range(3)]
+    kept = functools.reduce(jnp.maximum, [jnp.where(c < 4, c, 0) for c in codes])
+    listed = {0: send_x[0, 0], 1: send_y[0, 0], 2: kept}
+    listed.update({3 + j: codes[j] for j in range(3)})
+    listed.update({8 + j: levels[j] for j in range(4)})
+    listed.update({12 + s * 6 + f: ghost_src[0, s, f] for s in range(4) for f in range(6)})
+    lane = lanes((1, 128))
+    row = jnp.zeros((1, 128), jnp.int32)
+    for i, number in listed.items():
+        row = jnp.where(lane == i, number, row)
+    numbers[...] = row
 
 
 def limited(left, right):
@@ -132,18 +172,23 @@
     return jnp.where(level == 0, STEP, jnp.where(level == 1, STEP * 2, STEP * 4))
 
 
-def update_kernel(slot, levels, ghost_src, order, sweep, table, r0, r1, r2, r3, out, remote, ghost, change):
+def update_kernel(which_block, more, numbers, sweep, table, r0, r1, r2, r3, *rest):
+    out, remote, ghost, change = rest[-4:]
     turns = Turns()
-    s = slot[0]
-    ratio = step_of(levels[s])
+    odd_x, odd_y = parities()
+    s = numbers[0, which_block]
+    ratio = step_of(numbers[0, 8 + s])
     for m, received in enumerate((r0, r1, r2, r3)):
         for k in range(4):
             remote[m * 4 + k] = received[k]
     for face in range(6):
         direction, high = face // 2, face % 2
-        code = ghost_src[0, s, face]
+        code = numbers[0, 12 + s * 6 + face]
         far = jnp.maximum(code - 24, 0)
-        far = order[far // 4] * 4 + far % 4
+        which = far // 4
+        along_x = jnp.where(which == odd_x, 1, 2)
+        along_y = jnp.where(which - 2 == odd_y, 0, 3)
+        far = jnp.where(which < 2, along_x, along_y) * 4 + far % 4
         near = jnp.minimum(code, 23)
         for layer in range(2):
             i = 2 + layer if high else 1 - layer
@@ -197,6 +242,9 @@
         if i < B:
             left_face = fluxes_of([a + b for a, b in zip(centre, half)])
 
+    if more:
+        out[BLOCK_ROWS : BLOCK_ROWS + 8, :] = jnp.zeros((8, 128), jnp.float32)
+
     def in_place(ref, start):
         return ref[pl.ds(start, 8, stride=8), :]
 
@@ -231,23 +279,32 @@
                 out[row : row + 8, :] = initial - scale * total
 
 
-def place_kernel(layout, own, from_x, from_y, out):
-    codes = [layout[0, j] for j in range(3)]
+def place_kernel(numbers, from_y, from_x, own, out, slots, staged, sems):
+    codes = [numbers[0, 3 + j] for j in range(3)]
     at_x = jnp.where(codes[1] == 4, 1, jnp.where(codes[2] == 4, 2, 0))
     at_y = jnp.where(codes[1] == 5, 1, jnp.where(codes[2] == 5, 2, 0))
     at_own = 3 - at_x - at_y
     empty = codes[0] + codes[1] + codes[2] == 8
-    for source, at in ((own, at_own), (from_x, at_x), (from_y, at_y)):
-        for t in range(2 * B):
-            row = (t % 2) * B + t // 2
-            v = source[pl.ds(row, 5, stride=2 * B), :]
+    copies = []
+    for f in range(5):
+        for source, at in ((own, at_own), (from_x, at_x), (from_y, at_y)):
+            v = source[f * 2 * B : (f + 1) * 2 * B, :]
             if source is own:
                 v = jnp.where(empty, 0.0, v)
-            out[at, :, t * 128 : (t + 1) * 128] = v
+            slots[pl.ds(pl.multiple_of(at * BLOCK_ROWS + f * 2 * B, 2 * B), 2 * B), :] = v
+        for t in range(2 * B):
+            row = f * 2 * B + (t % 2) * B + t // 2
+            staged[f, :, t * 128 : (t + 1) * 128] = slots[pl.ds(row, 3, stride=BLOCK_ROWS), :]
+        copies.append(pltpu.make_async_copy(staged.at[f], out.at[f], sems.at[f]))
+        copies[-1].start()
+    for copy in copies:
+        copy.wait()
 
 
 SMEM = pl.BlockSpec(memory_space=pltpu.SMEM)
 VMEM = pl.BlockSpec(memory_space=pltpu.VMEM)
+HBM = pl.BlockSpec(memory_space=pltpu.HBM)
+ANY = pl.BlockSpec(memory_space=pl.ANY)
 LIMIT = 48 << 20
 
 
@@ -255,23 +312,37 @@
     return jax.ShapeDtypeStruct(shape, jnp.float32)
 
 
-def pack(face_out, lists, cells):
+def in_hbm(array):
+    return pltpu.with_memory_space_constraint(array, pltpu.HBM)
+
+
+def pack(send_x, send_y, cells, *small):
     return pl.pallas_call(
         pack_kernel,
-        out_shape=(struct(4, SWEEP_ROWS, 128), struct(24, FACE_ROWS, 128))
+        out_shape=(
+            jax.ShapeDtypeStruct((1, 128), jnp.int32),
+            struct(4 * SWEEP_ROWS, 128),
+            struct(24, FACE_ROWS, 128),
+        )
         + (struct(4, FACE_ROWS, 128),) * 4,
-        in_specs=[SMEM, SMEM, VMEM],
-        out_specs=(VMEM,) * 6,
+        in_specs=[SMEM, SMEM, HBM] + [HBM] * len(small),
+        out_specs=(VMEM,) * 7,
+        scratch_shapes=[
+            pltpu.VMEM(cells.shape, jnp.float32),
+            *[pltpu.SMEM(array.shape, jnp.int32) for array in small],
+            pltpu.SemaphoreType.DMA((5,)),
+            pltpu.SemaphoreType.DMA((len(small),)),
+        ],
         compiler_params=pltpu.CompilerParams(vmem_limit_bytes=LIMIT),
         name="pack",
-    )(face_out, lists, cells)
-
-
-def update(name, slot, levels, ghost_src, order, sweep, table, received):
+    )(send_x, send_y, *[in_hbm(array) for array in (cells, *small)])
+
+
+def update(name, which_block, more, numbers, sweep, table, received, *after):
     return pl.pallas_call(
-        update_kernel,
-        out_shape=struct(BLOCK_ROWS, 128),
-        in_specs=[SMEM] * 4 + [VMEM] * 6,
+        functools.partial(update_kernel, which_block, more),
+        out_shape=struct(BLOCK_ROWS + (8 if more else 0), 128),
+        in_specs=[SMEM] + [VMEM] * 6 + [ANY] * len(after),
         out_specs=VMEM,
         scratch_shapes=[
             pltpu.VMEM((16, FACE_ROWS, 128), jnp.float32),
@@ -279,19 +350,25 @@
             pltpu.VMEM((SWEEP_ROWS, 128), jnp.float32),
         ],
         compiler_params=pltpu.CompilerParams(vmem_limit_bytes=LIMIT),
+        cost_estimate=pl.CostEstimate(flops=2_000_000, bytes_accessed=4_000_000, transcendentals=40_000),
         name=name,
-    )(slot, levels, ghost_src, order, sweep, table, *received)
-
-
-def place(layout, own, from_x, from_y):
+    )(numbers, sweep.reshape(4, SWEEP_ROWS, 128), table, *received, *after)
+
+
+def place(numbers, from_y, from_x, own):
     return pl.pallas_call(
         place_kernel,
-        out_shape=struct(3, 5, B * B * B),
+        out_shape=struct(5, 3, B * B * B),
         in_specs=[SMEM] + [VMEM] * 3,
-        out_specs=VMEM,
+        out_specs=HBM,
+        scratch_shapes=[
+            pltpu.VMEM((3 * BLOCK_ROWS, 128), jnp.float32),
+            pltpu.VMEM((5, 3, B * B * B), jnp.float32),
+            pltpu.SemaphoreType.DMA((5,)),
+        ],
         compiler_params=pltpu.CompilerParams(vmem_limit_bytes=LIMIT),
         name="place",
-    )(layout, own, from_x, from_y)
+    )(numbers, from_y, from_x, own)
 
 
 def with_pair(values, axis, odd):
@@ -306,23 +383,22 @@
 
 
 def on_device(cells_in, block_levels, send_x, send_y, layout, face_out, ghost_src):
-    odd_x = lax.axis_index("bx") % 2
-    odd_y = lax.axis_index("by") % 2
-    lists = jnp.stack([odd_x, 1 - odd_x, 2 + odd_y, 3 - odd_y]).astype(jnp.int32)
-    order = jnp.stack([1 - odd_x, odd_x, 3 - odd_y, 2 + odd_y]).astype(jnp.int32)
-    sweep, table, *messages = pack(face_out, lists, cells_in)
+    numbers, sweep, table, *messages = pack(
+        send_x, send_y, cells_in.transpose(1, 0, 2), layout, block_levels, ghost_src, face_out
+    )
     received = [
-        with_pair(messages[0], "bx", 0),
+        with_pair(messages[0], "by", 1),
         with_pair(messages[1], "bx", 1),
-        with_pair(messages[2], "by", 0),
-        with_pair(messages[3], "by", 1),
+        with_pair(messages[2], "bx", 0),
+        with_pair(messages[3], "by", 0),
     ]
-    own_slot = jnp.max(jnp.where(layout < 4, layout, 0), axis=1)
-    common = (block_levels, ghost_src, order, sweep, table, received)
-    from_y = with_partner(update("to_y", send_y[0], *common), "by")
-    from_x = with_partner(update("to_x", send_x[0], *common), "bx")
-    own = update("own", own_slot, *common)
-    return place(layout, own, from_x, from_y)
+    common = (numbers, sweep, table, received)
+    to_y = update("to_y", 1, True, *common)
+    from_y = with_partner(to_y, "by")
+    to_x = update("to_x", 0, False, *common, to_y)
+    from_x = with_partner(to_x, "bx")
+    own = update("own", 2, False, *common, to_x)
+    return place(numbers, from_y, from_x, own).transpose(1, 0, 2)
 
 
 def solution(mesh):

time: 56.7 us -> 53 us (0.935)
  the two profiles are of different devices: /device:TPU:4 before, /device:TPU:1 now
where the time goes in v2:
time: 53 us; the launch traced here: 52.7 us
  starting transfers between devices  34.5 us (65%)
  waiting for transfers between devices  9.32 us (18%)
  Pallas kernels  7.49 us (14%)
  between operations  1.4 us (3%)
    ppermute x4, starting transfers between devices, with_pair(): lax.ppermute(values, axis, [(i, j % count) for i, j in enumerate(mate)])  26 us
    ppermute x2, starting transfers between devices, with_partner(): lax.ppermute(values, axis, [(i, i ^ count // 2) for i in range(count)])  8.49 us
    ppermute x2, waiting for transfers between devices, with_partner(): lax.ppermute(values, axis, [(i, i ^ count // 2) for i in range(count)])  8.48 us
    pallas_call x3, Pallas kernels, update(): pl.pallas_call(functools.partial(update_kernel, which_block, more), out_s...  3.57 us
    pallas_call x1, Pallas kernels, pack(): pl.pallas_call(pack_kernel, out_shape=(jax.ShapeDtypeStruct((1, 128), jnp...  2.47 us
    pallas_call x1, Pallas kernels, place(): pl.pallas_call(place_kernel, out_shape=struct(5, 3, B * B * B), in_specs=...  1.44 us
  transfers between devices with their start and end apart: 6, of which 3 were waited for; matrix products, arithmetic and copies ran while one was open for 0% of the time, Pallas kernels for 5%

profile of v2, /device:TPU:1, one launch (start us, length us, event | category | flops | bytes accessed | tf_op | source)
XLA Modules:
  0.0 52.7 jit_solution(15215991504571873185)
XLA Ops:
  1.3 2.5 %pack.1 = (s32[1,128]{1,0:T(1,128)S(1)}, f32[2560,128]{1,0:T(8,128)S(1)}, f32[24,24,128]{2,1,0:T(8,128)S(1)}, f32[4,24,128]{2,1,0:T(8,128)S(1)}, f32[4,24,128]{2...) custom-call(s32[1,1]{1,0:T(1,128)S(6)} %copy.8.send_x, s32[1,1]{1,0:T(1,128)S(6)} %copy.9.send_y, ...), custom_call_target="tpu_custom_call" | custom-call | tf_op jit(solution)/shard_map/pack/pallas_call | solution.py:320
  3.8 4.6 %collective-permute-start = (f32[4,24,128]{2,1,0:T(8,128)S(1)}, f32[4,24,128]{2,1,0:T(8,128)S(1)}, u32[]{:S(2)}, u32[]{:S(2)}) collective-permute-start(f32[4,24,128]{2,1,0:T(8,128)S(1)} %get-tuple-element.15), channel_id=1, source_target_pairs={{0,31},{1,2},{2,1},{3,4},{4,3},{5,6},{6,5},{7,8},{8,7},{9,10},{10,... | collective-permute-start | bytes 147464 | tf_op jit(solution)/shard_map/ppermute | solution.py:377
  8.4 8.4 %collective-permute-start.1 = (f32[4,24,128]{2,1,0:T(8,128)S(1)}, f32[4,24,128]{2,1,0:T(8,128)S(1)}, u32[]{:S(2)}, u32[]{:S(2)}) collective-permute-start(f32[4,24,128]{2,1,0:T(8,128)S(1)} %get-tuple-element.16), channel_id=1, source_target_pairs={{0,480},{32,64},{64,32},{96,128},{128,96},{160,192},{192,160},{224... | collective-permute-start | bytes 147464 | tf_op jit(solution)/shard_map/ppermute | solution.py:377
  16.8 1.9 %collective-permute-start.2 = (f32[4,24,128]{2,1,0:T(8,128)S(1)}, f32[4,24,128]{2,1,0:T(8,128)S(1)}, u32[]{:S(2)}, u32[]{:S(2)}) collective-permute-start(f32[4,24,128]{2,1,0:T(8,128)S(1)} %get-tuple-element.17), channel_id=1, source_target_pairs={{0,32},{32,0},{64,96},{96,64},{128,160},{160,128},{192,224},{224,1... | collective-permute-start | bytes 147464 | tf_op jit(solution)/shard_map/ppermute | solution.py:377
  18.8 11.0 %collective-permute-start.3 = (f32[4,24,128]{2,1,0:T(8,128)S(1)}, f32[4,24,128]{2,1,0:T(8,128)S(1)}, u32[]{:S(2)}, u32[]{:S(2)}) collective-permute-start(f32[4,24,128]{2,1,0:T(8,128)S(1)} %get-tuple-element.18), channel_id=1, source_target_pairs={{0,1},{1,0},{2,3},{3,2},{4,5},{5,4},{6,7},{7,6},{8,9},{9,8},{10,11... | collective-permute-start | bytes 147464 | tf_op jit(solution)/shard_map/ppermute | solution.py:377
  29.8 0.0 collective-permute-done.r0
  29.8 0.0 collective-permute-done.1.r1
  29.8 0.0 collective-permute-done.2.r2
  29.8 0.8 %collective-permute-done.3.r3 = f32[4,24,128]{2,1,0:T(8,128)S(1)} collective-permute-done((f32[4,24,128]{2,1,0:T(8,128)S(1)}, f32[4,24,128]{2,1,0:T(8,128)S(1)}, u32[]{:S(2)}, u32[]{:S(2)}) %collective-permute-start.3) | collective-permute-done | bytes 49184 | tf_op jit(solution)/shard_map/ppermute | solution.py:377
  30.7 1.2 %to_y.1.rest_0_ = f32[168,128]{1,0:T(8,128)S(1)} custom-call(s32[1,128]{1,0:T(1,128)S(1)} %get-tuple-element.12.numbers, f32[4,640,128]{2,1,0:T(8,128)S(1)} %bitcast.3, f32[24,24,128]{2,1,0:T(8,128)S(1)} %get-tuple-element.14.table, f32[4,24,128]{2,1,0:T(8,128)S(1)} %collective-permute-done.r0, f32[4,24,128]{2,1,0:T(8,128)S(1)} %collective-permute-done.1.r1, ...), custom_call_target="tpu_custom_call" | custom-call | flops 2000000 | bytes 4000000 | tf_op jit(solution)/shard_map/to_y/pallas_call | solution.py:342
  31.9 6.1 %collective-permute-start.4 = (f32[168,128]{1,0:T(8,128)S(1)}, f32[168,128]{1,0:T(8,128)S(1)}, u32[]{:S(2)}, u32[]{:S(2)}) collective-permute-start(f32[168,128]{1,0:T(8,128)S(1)} %to_y.1.rest_0_), channel_id=1, source_target_pairs={{0,16},{1,17},{2,18},{3,19},{4,20},{5,21},{6,22},{7,23},{8,24},{9,... | collective-permute-start | bytes 258056 | tf_op jit(solution)/shard_map/ppermute | solution.py:382
  37.9 1.2 %to_x.1.rest_0_ = f32[160,128]{1,0:T(8,128)S(1)} custom-call(s32[1,128]{1,0:T(1,128)S(1)} %get-tuple-element.12.numbers, f32[4,640,128]{2,1,0:T(8,128)S(1)} %bitcast.4, f32[24,24,128]{2,1,0:T(8,128)S(1)} %get-tuple-element.14.table, f32[4,24,128]{2,1,0:T(8,128)S(1)} %collective-permute-done.r0, f32[4,24,128]{2,1,0:T(8,128)S(1)} %collective-permute-done.1.r1, ...), custom_call_target="tpu_custom_call" | custom-call | flops 2000000 | bytes 4000000 | tf_op jit(solution)/shard_map/to_x/pallas_call | solution.py:342
  39.1 2.4 %collective-permute-start.5 = (f32[160,128]{1,0:T(8,128)S(1)}, f32[160,128]{1,0:T(8,128)S(1)}, u32[]{:S(2)}, u32[]{:S(2)}) collective-permute-start(f32[160,128]{1,0:T(8,128)S(1)} %to_x.1.rest_0_), channel_id=1, source_target_pairs={{0,256},{32,288},{64,320},{96,352},{128,384},{160,416},{192,448},{... | collective-permute-start | bytes 245768 | tf_op jit(solution)/shard_map/ppermute | solution.py:382
  41.6 1.2 %own.1 = f32[160,128]{1,0:T(8,128)S(1)} custom-call(s32[1,128]{1,0:T(1,128)S(1)} %get-tuple-element.12.numbers, f32[4,640,128]{2,1,0:T(8,128)S(1)} %bitcast.5, f32[24,24,128]{2,1,0:T(8,128)S(1)} %get-tuple-element.14.table, f32[4,24,128]{2,1,0:T(8,128)S(1)} %collective-permute-done.r0, f32[4,24,128]{2,1,0:T(8,128)S(1)} %collective-permute-done.1.r1, ...), custom_call_target="tpu_custom_call" | custom-call | flops 2000000 | bytes 4000000 | tf_op jit(solution)/shard_map/own/pallas_call | solution.py:342
  42.8 3.1 %collective-permute-done.5.from_x = f32[160,128]{1,0:T(8,128)S(1)} collective-permute-done((f32[160,128]{1,0:T(8,128)S(1)}, f32[160,128]{1,0:T(8,128)S(1)}, u32[]{:S(2)}, u32[]{:S(2)}) %collective-permute-start.5) | collective-permute-done | bytes 81952 | tf_op jit(solution)/shard_map/ppermute | solution.py:382
  45.8 5.4 %collective-permute-done.4.from_y = f32[168,128]{1,0:T(8,128)S(1)} collective-permute-done((f32[168,128]{1,0:T(8,128)S(1)}, f32[168,128]{1,0:T(8,128)S(1)}, u32[]{:S(2)}, u32[]{:S(2)}) %collective-permute-start.4) | collective-permute-done | bytes 86048 | tf_op jit(solution)/shard_map/ppermute | solution.py:382
  51.2 1.4 %place.1 = f32[5,3,4096]{2,1,0:T(4,128)} custom-call(s32[1,128]{1,0:T(1,128)S(1)} %get-tuple-element.12.numbers, f32[168,128]{1,0:T(8,128)S(1)} %collective-permute-done.4.from_y, f32[160,128]{1,0:T(8,128)S(1)} %collective-permute-done.5.from_x, f32[160,128]{1,0:T(8,128)S(1)} %own.1), custom_call_target="tpu_custom_call" | custom-call | tf_op jit(solution)/shard_map/place/pallas_call | solution.py:359
Async XLA Ops:
  3.8 26.0 %collective-permute-start = (f32[4,24,128]{2,1,0:T(8,128)S(1)}, f32[4,24,128]{2,1,0:T(8,128)S(1)}, u32[]{:S(2)}, u32[]{:S(2)}) collective-permute-start(f32[4,24,128]{2,1,0:T(8,128)S(1)} %get-tuple-element.15), channel_id=1, source_target_pairs={{0,31},{1,2},{2,1},{3,4},{4,3},{5,6},{6,5},{7,8},{8,7},{9,10},{10,... | collective-permute-start | bytes 147464 | tf_op jit(solution)/shard_map/ppermute | solution.py:377
  8.4 21.4 %collective-permute-start.1 = (f32[4,24,128]{2,1,0:T(8,128)S(1)}, f32[4,24,128]{2,1,0:T(8,128)S(1)}, u32[]{:S(2)}, u32[]{:S(2)}) collective-permute-start(f32[4,24,128]{2,1,0:T(8,128)S(1)} %get-tuple-element.16), channel_id=1, source_target_pairs={{0,480},{32,64},{64,32},{96,128},{128,96},{160,192},{192,160},{224... | collective-permute-start | bytes 147464 | tf_op jit(solution)/shard_map/ppermute | solution.py:377
  16.8 13.0 %collective-permute-start.2 = (f32[4,24,128]{2,1,0:T(8,128)S(1)}, f32[4,24,128]{2,1,0:T(8,128)S(1)}, u32[]{:S(2)}, u32[]{:S(2)}) collective-permute-start(f32[4,24,128]{2,1,0:T(8,128)S(1)} %get-tuple-element.17), channel_id=1, source_target_pairs={{0,32},{32,0},{64,96},{96,64},{128,160},{160,128},{192,224},{224,1... | collective-permute-start | bytes 147464 | tf_op jit(solution)/shard_map/ppermute | solution.py:377
  18.8 11.9 %collective-permute-start.3 = (f32[4,24,128]{2,1,0:T(8,128)S(1)}, f32[4,24,128]{2,1,0:T(8,128)S(1)}, u32[]{:S(2)}, u32[]{:S(2)}) collective-permute-start(f32[4,24,128]{2,1,0:T(8,128)S(1)} %get-tuple-element.18), channel_id=1, source_target_pairs={{0,1},{1,0},{2,3},{3,2},{4,5},{5,4},{6,7},{7,6},{8,9},{9,8},{10,11... | collective-permute-start | bytes 147464 | tf_op jit(solution)/shard_map/ppermute | solution.py:377
  31.9 19.4 %collective-permute-start.4 = (f32[168,128]{1,0:T(8,128)S(1)}, f32[168,128]{1,0:T(8,128)S(1)}, u32[]{:S(2)}, u32[]{:S(2)}) collective-permute-start(f32[168,128]{1,0:T(8,128)S(1)} %to_y.1.rest_0_), channel_id=1, source_target_pairs={{0,16},{1,17},{2,18},{3,19},{4,20},{5,21},{6,22},{7,23},{8,24},{9,... | collective-permute-start | bytes 258056 | tf_op jit(solution)/shard_map/ppermute | solution.py:382
  39.1 6.7 %collective-permute-start.5 = (f32[160,128]{1,0:T(8,128)S(1)}, f32[160,128]{1,0:T(8,128)S(1)}, u32[]{:S(2)}, u32[]{:S(2)}) collective-permute-start(f32[160,128]{1,0:T(8,128)S(1)} %to_x.1.rest_0_), channel_id=1, source_target_pairs={{0,256},{32,288},{64,320},{96,352},{128,384},{160,416},{192,448},{... | collective-permute-start | bytes 245768 | tf_op jit(solution)/shard_map/ppermute | solution.py:382

commit v3 on v2

--- a/solution.py
+++ b/solution.py
@@ -74,7 +74,7 @@
 
 
 def pack_kernel(
-    send_x, send_y, cells_in, layout_in, levels_in, ghost_src_in, face_out_in, *rest
+    cells_in, layout_in, levels_in, ghost_src_in, face_out_in, *rest
 ):
     numbers, sweep, table, *messages = rest[:7]
     cells, layout, levels, ghost_src, face_out, cells_sem, small_sem = rest[7:]
@@ -141,7 +141,7 @@
             messages[m][k] = table[face_out[0, one_list, k]]
     codes = [layout[0, j] for j in range(3)]
     kept = functools.reduce(jnp.maximum, [jnp.where(c < 4, c, 0) for c in codes])
-    listed = {0: send_x[0, 0], 1: send_y[0, 0], 2: kept}
+    listed = {2: kept}
     listed.update({3 + j: codes[j] for j in range(3)})
     listed.update({8 + j: levels[j] for j in range(4)})
     listed.update({12 + s * 6 + f: ghost_src[0, s, f] for s in range(4) for f in range(6)})
@@ -172,15 +172,37 @@
     return jnp.where(level == 0, STEP, jnp.where(level == 1, STEP * 2, STEP * 4))
 
 
-def update_kernel(which_block, more, numbers, sweep, table, r0, r1, r2, r3, *rest):
-    out, remote, ghost, change = rest[-4:]
+def upper_half():
+    return lax.axis_index("by") >= lax.axis_size("by") // 2
+
+
+def update_kernel(which, half, extra, handed, counts, sends, numbers, sweep, table, *rest):
+    received, rest = rest[: sum(counts)], rest[sum(counts) :]
+    out, copies = rest[-4 - handed], rest[-3 - handed : -3]
+    for source, target in zip(rest, copies):
+        target[...] = source[...]
+
+    def body():
+        update_body(which, counts, sends, numbers, sweep, table, received, out, *rest[-3:])
+        if extra:
+            out[BLOCK_ROWS : BLOCK_ROWS + extra, :] = jnp.zeros((extra, 128), jnp.float32)
+
+    if half is None:
+        body()
+    else:
+        pl.when(upper_half() == half)(body)
+
+
+def update_body(which, counts, sends, numbers, sweep, table, received, out, remote, ghost, change):
     turns = Turns()
     odd_x, odd_y = parities()
-    s = numbers[0, which_block]
+    s = numbers[0, 2] if which == 2 else sends[0, 0]
     ratio = step_of(numbers[0, 8 + s])
-    for m, received in enumerate((r0, r1, r2, r3)):
+    first = 0
+    for m, count in enumerate(counts):
         for k in range(4):
-            remote[m * 4 + k] = received[k]
+            remote[m * 4 + k] = sum(array[k] for array in received[first : first + count])
+        first += count
     for face in range(6):
         direction, high = face // 2, face % 2
         code = numbers[0, 12 + s * 6 + face]
@@ -242,9 +264,6 @@
         if i < B:
             left_face = fluxes_of([a + b for a, b in zip(centre, half)])
 
-    if more:
-        out[BLOCK_ROWS : BLOCK_ROWS + 8, :] = jnp.zeros((8, 128), jnp.float32)
-
     def in_place(ref, start):
         return ref[pl.ds(start, 8, stride=8), :]
 
@@ -279,7 +298,7 @@
                 out[row : row + 8, :] = initial - scale * total
 
 
-def place_kernel(numbers, from_y, from_x, own, out, slots, staged, sems):
+def place_kernel(numbers, from_y0, from_y1, from_x0, from_x1, own, out, slots, staged, sems):
     codes = [numbers[0, 3 + j] for j in range(3)]
     at_x = jnp.where(codes[1] == 4, 1, jnp.where(codes[2] == 4, 2, 0))
     at_y = jnp.where(codes[1] == 5, 1, jnp.where(codes[2] == 5, 2, 0))
@@ -287,10 +306,13 @@
     empty = codes[0] + codes[1] + codes[2] == 8
     copies = []
     for f in range(5):
-        for source, at in ((own, at_own), (from_x, at_x), (from_y, at_y)):
-            v = source[f * 2 * B : (f + 1) * 2 * B, :]
-            if source is own:
-                v = jnp.where(empty, 0.0, v)
+        one = pl.ds(f * 2 * B, 2 * B)
+        values = (
+            (jnp.where(empty, 0.0, own[one, :]), at_own),
+            (from_x0[one, :] + from_x1[one, :], at_x),
+            (from_y0[one, :] + from_y1[one, :], at_y),
+        )
+        for v, at in values:
             slots[pl.ds(pl.multiple_of(at * BLOCK_ROWS + f * 2 * B, 2 * B), 2 * B), :] = v
         for t in range(2 * B):
             row = f * 2 * B + (t % 2) * B + t // 2
@@ -316,7 +338,7 @@
     return pltpu.with_memory_space_constraint(array, pltpu.HBM)
 
 
-def pack(send_x, send_y, cells, *small):
+def pack(cells, *small):
     return pl.pallas_call(
         pack_kernel,
         out_shape=(
@@ -325,7 +347,7 @@
             struct(24, FACE_ROWS, 128),
         )
         + (struct(4, FACE_ROWS, 128),) * 4,
-        in_specs=[SMEM, SMEM, HBM] + [HBM] * len(small),
+        in_specs=[HBM] * (1 + len(small)),
         out_specs=(VMEM,) * 7,
         scratch_shapes=[
             pltpu.VMEM(cells.shape, jnp.float32),
@@ -335,31 +357,33 @@
         ],
         compiler_params=pltpu.CompilerParams(vmem_limit_bytes=LIMIT),
         name="pack",
-    )(send_x, send_y, *[in_hbm(array) for array in (cells, *small)])
-
-
-def update(name, which_block, more, numbers, sweep, table, received, *after):
+    )(*[in_hbm(array) for array in (cells, *small)])
+
+
+def update(name, which, half, extra, sends, numbers, sweep, table, received, handed=(), after=()):
+    counts = tuple(len(arrays) for arrays in received)
+    flat = [array for arrays in received for array in arrays]
+    message = struct(BLOCK_ROWS + extra, 128)
     return pl.pallas_call(
-        functools.partial(update_kernel, which_block, more),
-        out_shape=struct(BLOCK_ROWS + (8 if more else 0), 128),
-        in_specs=[SMEM] + [VMEM] * 6 + [ANY] * len(after),
-        out_specs=VMEM,
+        functools.partial(update_kernel, which, half, extra, len(handed), counts),
+        out_shape=(message, *[struct(*array.shape) for array in handed]) if handed else message,
+        in_specs=[SMEM] * 2 + [VMEM] * (2 + len(flat) + len(handed)) + [ANY] * len(after),
+        out_specs=(VMEM,) * (1 + len(handed)) if handed else VMEM,
         scratch_shapes=[
             pltpu.VMEM((16, FACE_ROWS, 128), jnp.float32),
             pltpu.VMEM((5 * GHOST_ROWS, 128), jnp.float32),
             pltpu.VMEM((SWEEP_ROWS, 128), jnp.float32),
         ],
         compiler_params=pltpu.CompilerParams(vmem_limit_bytes=LIMIT),
-        cost_estimate=pl.CostEstimate(flops=2_000_000, bytes_accessed=4_000_000, transcendentals=40_000),
         name=name,
-    )(numbers, sweep.reshape(4, SWEEP_ROWS, 128), table, *received, *after)
+    )(sends, numbers, sweep.reshape(4, SWEEP_ROWS, 128), table, *flat, *handed, *after)
 
 
 def place(numbers, from_y, from_x, own):
     return pl.pallas_call(
         place_kernel,
         out_shape=struct(5, 3, B * B * B),
-        in_specs=[SMEM] + [VMEM] * 3,
+        in_specs=[SMEM] + [VMEM] * 5,
         out_specs=HBM,
         scratch_shapes=[
             pltpu.VMEM((3 * BLOCK_ROWS, 128), jnp.float32),
@@ -368,36 +392,61 @@
         ],
         compiler_params=pltpu.CompilerParams(vmem_limit_bytes=LIMIT),
         name="place",
-    )(numbers, from_y, from_x, own)
-
-
-def with_pair(values, axis, odd):
-    count = lax.axis_size(axis)
-    mate = [((i + odd) ^ 1) - odd for i in range(count)]
-    return lax.ppermute(values, axis, [(i, j % count) for i, j in enumerate(mate)])
-
-
-def with_partner(values, axis):
-    count = lax.axis_size(axis)
-    return lax.ppermute(values, axis, [(i, i ^ (count // 2)) for i in range(count)])
+    )(numbers, *from_y, *from_x, own)
+
+
+def exchange(values, move, sends):
+    count_x, count_y = lax.axis_size("bx"), lax.axis_size("by")
+    pairs = []
+    for i in range(count_x):
+        for j in range(count_y):
+            to_i, to_j = move(i, j)
+            to_i, to_j = to_i % count_x, to_j % count_y
+            if sends(j, to_j):
+                pairs.append((i * count_y + j, to_i * count_y + to_j))
+    return lax.ppermute(values, ("bx", "by"), pairs)
 
 
 def on_device(cells_in, block_levels, send_x, send_y, layout, face_out, ghost_src):
+    half_x, half_y = lax.axis_size("bx") // 2, lax.axis_size("by") // 2
+    pairings = (
+        lambda i, j: (i, ((j + 1) ^ 1) - 1),
+        lambda i, j: (((i + 1) ^ 1) - 1, j),
+        lambda i, j: (i ^ 1, j),
+        lambda i, j: (i, j ^ 1),
+    )
+
+    def upper(j, to_j):
+        return j >= half_y or to_j >= half_y
+
+    def lower(j, to_j):
+        return not upper(j, to_j)
+
+    def by_partner(i, j):
+        return i, j ^ half_y
+
+    def bx_partner(i, j):
+        return i ^ half_x, j
+
     numbers, sweep, table, *messages = pack(
-        send_x, send_y, cells_in.transpose(1, 0, 2), layout, block_levels, ghost_src, face_out
+        cells_in.transpose(1, 0, 2), layout, block_levels, ghost_src, face_out
     )
-    received = [
-        with_pair(messages[0], "by", 1),
-        with_pair(messages[1], "bx", 1),
-        with_pair(messages[2], "bx", 0),
-        with_pair(messages[3], "by", 0),
-    ]
-    common = (numbers, sweep, table, received)
-    to_y = update("to_y", 1, True, *common)
-    from_y = with_partner(to_y, "by")
-    to_x = update("to_x", 0, False, *common, to_y)
-    from_x = with_partner(to_x, "bx")
-    own = update("own", 2, False, *common, to_x)
+    common = (numbers, sweep, table)
+    early = [exchange(m, pairing, upper) for m, pairing in zip(messages, pairings)]
+    y_upper, *messages = update(
+        "y_upper", 1, True, 8, send_y, *common, [[r] for r in early], handed=messages
+    )
+    y_from_upper = exchange(y_upper, by_partner, lambda j, to_j: j >= half_y)
+    late = [exchange(m, pairing, lower) for m, pairing in zip(messages, pairings)]
+    lower_faces = [[early[0], late[0]], [late[1]], [late[2]], [late[3]]]
+    x_lower = update("x_lower", 0, False, 16, send_x, *common, lower_faces, after=(y_upper,))
+    x_from_lower = exchange(x_lower, bx_partner, lower)
+    y_lower = update("y_lower", 1, False, 8, send_y, *common, lower_faces, after=(x_lower,))
+    y_from_lower = exchange(y_lower, by_partner, lambda j, to_j: j < half_y)
+    x_upper = update("x_upper", 0, True, 0, send_x, *common, [[r] for r in early], after=(y_lower, y_from_upper))
+    x_from_upper = exchange(x_upper, bx_partner, upper)
+    own = update("own", 2, None, 0, send_x, *common, [list(p) for p in zip(early, late)], after=(x_upper,))
+    from_y, from_x = (y_from_upper, y_from_lower), (x_from_upper, x_from_lower)
     return place(numbers, from_y, from_x, own).transpose(1, 0, 2)
 
 

time: 53 us -> 50.9 us (0.960)
  the two profiles are of different devices: /device:TPU:1 before, /device:TPU:448 now
where the time goes in v3:
time: 50.9 us; the launch traced here: 50.5 us
  starting transfers between devices  27.4 us (54%)
  waiting for transfers between devices  13 us (26%)
  Pallas kernels  8.62 us (17%)
  between operations  1.49 us (3%)
    ppermute x12, starting transfers between devices, exchange(): return lax.ppermute(values, ('bx', 'by'), pairs)  27.4 us
    ppermute x12, waiting for transfers between devices, exchange(): return lax.ppermute(values, ('bx', 'by'), pairs)  13 us
    pallas_call x5, Pallas kernels, update(): pl.pallas_call(functools.partial(update_kernel, which, half, extra, len(h...  4.7 us
    pallas_call x1, Pallas kernels, pack(): pl.pallas_call(pack_kernel, out_shape=(jax.ShapeDtypeStruct((1, 128), jnp...  2.47 us
    pallas_call x1, Pallas kernels, place(): pl.pallas_call(place_kernel, out_shape=struct(5, 3, B * B * B), in_specs=...  1.44 us
  transfers between devices with their start and end apart: 12, of which 3 were waited for; matrix products, arithmetic and copies ran while one was open for 0% of the time, Pallas kernels for 7%

profile of v3, /device:TPU:448, one launch (start us, length us, event | category | flops | bytes accessed | tf_op | source)
XLA Modules:
  0.0 50.5 jit_solution(4762502025249178487)
XLA Ops:
  0.0 2.5 %pack.1 = (s32[1,128]{1,0:T(1,128)S(1)}, f32[2560,128]{1,0:T(8,128)S(1)}, f32[24,24,128]{2,1,0:T(8,128)S(1)}, f32[4,24,128]{2,1,0:T(8,128)S(1)}, f32[4,24,128]{2...) custom-call(f32[5,4,4096]{2,1,0:T(4,128)} %bitcast.8, s32[1,3]{1,0:T(1,128)} %layout_in.1, ...), custom_call_target="tpu_custom_call" | custom-call | tf_op jit(solution)/shard_map/pack/pallas_call | solution.py:342
  2.5 7.3 %collective-permute-start = (f32[4,24,128]{2,1,0:T(8,128)S(1)}, f32[4,24,128]{2,1,0:T(8,128)S(1)}, u32[]{:S(2)}, u32[]{:S(2)}) collective-permute-start(f32[4,24,128]{2,1,0:T(8,128)S(1)} %get-tuple-element.20.rest_4_), channel_id=1, source_target_pairs={{0,31},{15,16},{16,15},{17,18},{18,17},{19,20},{20,19},{21,22},{22... | collective-permute-start | bytes 147464 | tf_op jit(solution)/shard_map/ppermute | solution.py:407
  9.8 2.9 %collective-permute-start.1 = (f32[4,24,128]{2,1,0:T(8,128)S(1)}, f32[4,24,128]{2,1,0:T(8,128)S(1)}, u32[]{:S(2)}, u32[]{:S(2)}) collective-permute-start(f32[4,24,128]{2,1,0:T(8,128)S(1)} %get-tuple-element.21.rest_5_), channel_id=1, source_target_pairs={{16,496},{17,497},{18,498},{19,499},{20,500},{21,501},{22,502},{23... | collective-permute-start | bytes 147464 | tf_op jit(solution)/shard_map/ppermute | solution.py:407
  12.8 4.7 %collective-permute-start.2 = (f32[4,24,128]{2,1,0:T(8,128)S(1)}, f32[4,24,128]{2,1,0:T(8,128)S(1)}, u32[]{:S(2)}, u32[]{:S(2)}) collective-permute-start(f32[4,24,128]{2,1,0:T(8,128)S(1)} %get-tuple-element.22.rest_6_), channel_id=1, source_target_pairs={{16,48},{17,49},{18,50},{19,51},{20,52},{21,53},{22,54},{23,55},{2... | collective-permute-start | bytes 147464 | tf_op jit(solution)/shard_map/ppermute | solution.py:407
  17.5 1.9 %collective-permute-start.3 = (f32[4,24,128]{2,1,0:T(8,128)S(1)}, f32[4,24,128]{2,1,0:T(8,128)S(1)}, u32[]{:S(2)}, u32[]{:S(2)}) collective-permute-start(f32[4,24,128]{2,1,0:T(8,128)S(1)} %get-tuple-element.23.rest_7_), channel_id=1, source_target_pairs={{16,17},{17,16},{18,19},{19,18},{20,21},{21,20},{22,23},{23,22},{2... | collective-permute-start | bytes 147464 | tf_op jit(solution)/shard_map/ppermute | solution.py:407
  20.1 0.0 collective-permute-done.rest_0_
  20.1 0.0 collective-permute-done.1.rest_1_.rest_2_
  20.1 0.0 collective-permute-done.2.rest_2_.rest_4_
  20.1 0.5 %collective-permute-done.3.rest_3_.rest_6_ = f32[4,24,128]{2,1,0:T(8,128)S(1)} collective-permute-done((f32[4,24,128]{2,1,0:T(8,128)S(1)}, f32[4,24,128]{2,1,0:T(8,128)S(1)}, u32[]{:S(2)}, u32[]{:S(2)}) %collective-permute-start.3) | collective-permute-done | bytes 49184 | tf_op jit(solution)/shard_map/ppermute | solution.py:407
  20.6 1.2 %y_upper.1 = (f32[168,128]{1,0:T(8,128)S(1)}, f32[4,24,128]{2,1,0:T(8,128)S(1)}, f32[4,24,128]{2,1,0:T(8,128)S(1)}, f32[4,24,128]{2,1,0:T(8,128)S(1)}, f32[4,24,128]{2,1,0:T(8,128)S(1)}) custom-call(s32[1,1]{1,0:T(1,128)S(6)} %copy.9.sends, s32[1,128]{1,0:T(1,128)S(1)} %get-tuple-element.17.numbers, f32[4,640,128]{2,1,0:T(8,128)S(1)} %bitcast.3, ...), custom_call_target="tpu_custom_call" | custom-call | tf_op jit(solution)/shard_map/y_upper/pallas_call | solution.py:367
  21.8 1.3 %collective-permute-start.4 = (f32[168,128]{1,0:T(8,128)S(1)}, f32[168,128]{1,0:T(8,128)S(1)}, u32[]{:S(2)}, u32[]{:S(2)}) collective-permute-start(f32[168,128]{1,0:T(8,128)S(1)} %get-tuple-element.24.rest_5_), channel_id=1, source_target_pairs={{16,0},{17,1},{18,2},{19,3},{20,4},{21,5},{22,6},{23,7},{24,8},{25... | collective-permute-start | bytes 258056 | tf_op jit(solution)/shard_map/ppermute | solution.py:407
  23.1 0.7 %collective-permute-start.5 = (f32[4,24,128]{2,1,0:T(8,128)S(1)}, f32[4,24,128]{2,1,0:T(8,128)S(1)}, u32[]{:S(2)}, u32[]{:S(2)}) collective-permute-start(f32[4,24,128]{2,1,0:T(8,128)S(1)} %get-tuple-element.25), channel_id=1, source_target_pairs={{1,2},{2,1},{3,4},{4,3},{5,6},{6,5},{7,8},{8,7},{9,10},{10,9},{11,... | collective-permute-start | bytes 147464 | tf_op jit(solution)/shard_map/ppermute | solution.py:407
  23.8 0.7 %collective-permute-start.6 = (f32[4,24,128]{2,1,0:T(8,128)S(1)}, f32[4,24,128]{2,1,0:T(8,128)S(1)}, u32[]{:S(2)}, u32[]{:S(2)}) collective-permute-start(f32[4,24,128]{2,1,0:T(8,128)S(1)} %get-tuple-element.26), channel_id=1, source_target_pairs={{0,480},{1,481},{2,482},{3,483},{4,484},{5,485},{6,486},{7,487},{8... | collective-permute-start | bytes 147464 | tf_op jit(solution)/shard_map/ppermute | solution.py:407
  24.5 0.7 %collective-permute-start.7 = (f32[4,24,128]{2,1,0:T(8,128)S(1)}, f32[4,24,128]{2,1,0:T(8,128)S(1)}, u32[]{:S(2)}, u32[]{:S(2)}) collective-permute-start(f32[4,24,128]{2,1,0:T(8,128)S(1)} %get-tuple-element.27), channel_id=1, source_target_pairs={{0,32},{1,33},{2,34},{3,35},{4,36},{5,37},{6,38},{7,39},{8,40},{9,... | collective-permute-start | bytes 147464 | tf_op jit(solution)/shard_map/ppermute | solution.py:407
  25.2 0.7 %collective-permute-start.8 = (f32[4,24,128]{2,1,0:T(8,128)S(1)}, f32[4,24,128]{2,1,0:T(8,128)S(1)}, u32[]{:S(2)}, u32[]{:S(2)}) collective-permute-start(f32[4,24,128]{2,1,0:T(8,128)S(1)} %get-tuple-element.28), channel_id=1, source_target_pairs={{0,1},{1,0},{2,3},{3,2},{4,5},{5,4},{6,7},{7,6},{8,9},{9,8},{10,11... | collective-permute-start | bytes 147464 | tf_op jit(solution)/shard_map/ppermute | solution.py:407
  26.5 0.0 collective-permute-done.5.rest_1_
  26.5 0.0 collective-permute-done.6.rest_2_.rest_3_
  26.5 0.0 collective-permute-done.7.rest_3_.rest_5_
  26.5 0.0 collective-permute-done.8.rest_4_.rest_7_
  26.5 0.6 %x_lower.1.rest_5_ = f32[176,128]{1,0:T(8,128)S(1)} custom-call(s32[1,1]{1,0:T(1,128)S(6)} %copy.8.sends, s32[1,128]{1,0:T(1,128)S(1)} %get-tuple-element.17.numbers, f32[4,640,128]{2,1,0:T(8,128)S(1)} %bitcast.4, f32[24,24,128]{2,1,0:T(8,128)S(1)} %get-tuple-element.19.table, f32[4,24,128]{2,1,0:T(8,128)S(1)} %collective-permute-done.rest_0_, ...), custom_call_target="tpu_custom_call" | custom-call | tf_op jit(solution)/shard_map/x_lower/pallas_call | solution.py:367
  27.1 0.7 %collective-permute-start.11 = (f32[176,128]{1,0:T(8,128)S(1)}, f32[176,128]{1,0:T(8,128)S(1)}, u32[]{:S(2)}, u32[]{:S(2)}) collective-permute-start(f32[176,128]{1,0:T(8,128)S(1)} %x_lower.1.rest_5_), channel_id=1, source_target_pairs={{0,256},{1,257},{2,258},{3,259},{4,260},{5,261},{6,262},{7,263},{8... | collective-permute-start | bytes 270344 | tf_op jit(solution)/shard_map/ppermute | solution.py:407
  27.8 0.6 %y_lower.1.rest_4_ = f32[168,128]{1,0:T(8,128)S(1)} custom-call(s32[1,1]{1,0:T(1,128)S(6)} %copy.9.sends, s32[1,128]{1,0:T(1,128)S(1)} %get-tuple-element.17.numbers, f32[4,640,128]{2,1,0:T(8,128)S(1)} %bitcast.5, f32[24,24,128]{2,1,0:T(8,128)S(1)} %get-tuple-element.19.table, f32[4,24,128]{2,1,0:T(8,128)S(1)} %collective-permute-done.rest_0_, ...), custom_call_target="tpu_custom_call" | custom-call | tf_op jit(solution)/shard_map/y_lower/pallas_call | solution.py:367
  28.3 1.3 %collective-permute-start.9 = (f32[168,128]{1,0:T(8,128)S(1)}, f32[168,128]{1,0:T(8,128)S(1)}, u32[]{:S(2)}, u32[]{:S(2)}) collective-permute-start(f32[168,128]{1,0:T(8,128)S(1)} %y_lower.1.rest_4_), channel_id=1, source_target_pairs={{0,16},{1,17},{2,18},{3,19},{4,20},{5,21},{6,22},{7,23},{8,24},{9,... | collective-permute-start | bytes 258056 | tf_op jit(solution)/shard_map/ppermute | solution.py:407
  29.6 0.1 collective-permute-done.4.rest_5_.from_y0
  29.7 1.2 %x_upper.1.rest_8_ = f32[160,128]{1,0:T(8,128)S(1)} custom-call(s32[1,1]{1,0:T(1,128)S(6)} %copy.8.sends, s32[1,128]{1,0:T(1,128)S(1)} %get-tuple-element.17.numbers, f32[4,640,128]{2,1,0:T(8,128)S(1)} %bitcast.6, f32[24,24,128]{2,1,0:T(8,128)S(1)} %get-tuple-element.19.table, f32[4,24,128]{2,1,0:T(8,128)S(1)} %collective-permute-done.rest_0_, ...), custom_call_target="tpu_custom_call" | custom-call | tf_op jit(solution)/shard_map/x_upper/pallas_call | solution.py:367
  30.9 4.5 %collective-permute-start.10 = (f32[160,128]{1,0:T(8,128)S(1)}, f32[160,128]{1,0:T(8,128)S(1)}, u32[]{:S(2)}, u32[]{:S(2)}) collective-permute-start(f32[160,128]{1,0:T(8,128)S(1)} %x_upper.1.rest_8_), channel_id=1, source_target_pairs={{16,272},{17,273},{18,274},{19,275},{20,276},{21,277},{22,278},{23... | collective-permute-start | bytes 245768 | tf_op jit(solution)/shard_map/ppermute | solution.py:407
  35.5 1.2 %own.1 = f32[160,128]{1,0:T(8,128)S(1)} custom-call(s32[1,1]{1,0:T(1,128)S(6)} %copy.8.sends, s32[1,128]{1,0:T(1,128)S(1)} %get-tuple-element.17.numbers, f32[4,640,128]{2,1,0:T(8,128)S(1)} %bitcast.7, f32[24,24,128]{2,1,0:T(8,128)S(1)} %get-tuple-element.19.table, f32[4,24,128]{2,1,0:T(8,128)S(1)} %collective-permute-done.rest_0_, ...), custom_call_target="tpu_custom_call" | custom-call | tf_op jit(solution)/shard_map/own/pallas_call | solution.py:367
  36.7 12.4 %collective-permute-done.9.from_y1 = f32[168,128]{1,0:T(8,128)S(1)} collective-permute-done((f32[168,128]{1,0:T(8,128)S(1)}, f32[168,128]{1,0:T(8,128)S(1)}, u32[]{:S(2)}, u32[]{:S(2)}) %collective-permute-start.9) | collective-permute-done | bytes 86048 | tf_op jit(solution)/shard_map/ppermute | solution.py:407
  49.1 0.0 collective-permute-done.11.from_x1
  49.1 0.0 collective-permute-done.10.from_x0
  49.1 1.4 %place.1 = f32[5,3,4096]{2,1,0:T(4,128)} custom-call(s32[1,128]{1,0:T(1,128)S(1)} %get-tuple-element.17.numbers, f32[168,128]{1,0:T(8,128)S(1)} %collective-permute-done.4.rest_5_.from_y0, f32[168,128]{1,0:T(8,128)S(1)} %collective-permute-done.9.from_y1, f32[160,128]{1,0:T(8,128)S(1)} %collective-permute-done.10.from_x0, ...), custom_call_target="tpu_custom_call" | custom-call | tf_op jit(solution)/shard_map/place/pallas_call | solution.py:383
Async XLA Ops:
  2.5 17.6 %collective-permute-start = (f32[4,24,128]{2,1,0:T(8,128)S(1)}, f32[4,24,128]{2,1,0:T(8,128)S(1)}, u32[]{:S(2)}, u32[]{:S(2)}) collective-permute-start(f32[4,24,128]{2,1,0:T(8,128)S(1)} %get-tuple-element.20.rest_4_), channel_id=1, source_target_pairs={{0,31},{15,16},{16,15},{17,18},{18,17},{19,20},{20,19},{21,22},{22... | collective-permute-start | bytes 147464 | tf_op jit(solution)/shard_map/ppermute | solution.py:407
  9.8 10.3 %collective-permute-start.1 = (f32[4,24,128]{2,1,0:T(8,128)S(1)}, f32[4,24,128]{2,1,0:T(8,128)S(1)}, u32[]{:S(2)}, u32[]{:S(2)}) collective-permute-start(f32[4,24,128]{2,1,0:T(8,128)S(1)} %get-tuple-element.21.rest_5_), channel_id=1, source_target_pairs={{16,496},{17,497},{18,498},{19,499},{20,500},{21,501},{22,502},{23... | collective-permute-start | bytes 147464 | tf_op jit(solution)/shard_map/ppermute | solution.py:407
  12.8 7.3 %collective-permute-start.2 = (f32[4,24,128]{2,1,0:T(8,128)S(1)}, f32[4,24,128]{2,1,0:T(8,128)S(1)}, u32[]{:S(2)}, u32[]{:S(2)}) collective-permute-start(f32[4,24,128]{2,1,0:T(8,128)S(1)} %get-tuple-element.22.rest_6_), channel_id=1, source_target_pairs={{16,48},{17,49},{18,50},{19,51},{20,52},{21,53},{22,54},{23,55},{2... | collective-permute-start | bytes 147464 | tf_op jit(solution)/shard_map/ppermute | solution.py:407
  17.5 3.1 %collective-permute-start.3 = (f32[4,24,128]{2,1,0:T(8,128)S(1)}, f32[4,24,128]{2,1,0:T(8,128)S(1)}, u32[]{:S(2)}, u32[]{:S(2)}) collective-permute-start(f32[4,24,128]{2,1,0:T(8,128)S(1)} %get-tuple-element.23.rest_7_), channel_id=1, source_target_pairs={{16,17},{17,16},{18,19},{19,18},{20,21},{21,20},{22,23},{23,22},{2... | collective-permute-start | bytes 147464 | tf_op jit(solution)/shard_map/ppermute | solution.py:407
  21.8 7.9 %collective-permute-start.4 = (f32[168,128]{1,0:T(8,128)S(1)}, f32[168,128]{1,0:T(8,128)S(1)}, u32[]{:S(2)}, u32[]{:S(2)}) collective-permute-start(f32[168,128]{1,0:T(8,128)S(1)} %get-tuple-element.24.rest_5_), channel_id=1, source_target_pairs={{16,0},{17,1},{18,2},{19,3},{20,4},{21,5},{22,6},{23,7},{24,8},{25... | collective-permute-start | bytes 258056 | tf_op jit(solution)/shard_map/ppermute | solution.py:407
  23.1 3.3 %collective-permute-start.5 = (f32[4,24,128]{2,1,0:T(8,128)S(1)}, f32[4,24,128]{2,1,0:T(8,128)S(1)}, u32[]{:S(2)}, u32[]{:S(2)}) collective-permute-start(f32[4,24,128]{2,1,0:T(8,128)S(1)} %get-tuple-element.25), channel_id=1, source_target_pairs={{1,2},{2,1},{3,4},{4,3},{5,6},{6,5},{7,8},{8,7},{9,10},{10,9},{11,... | collective-permute-start | bytes 147464 | tf_op jit(solution)/shard_map/ppermute | solution.py:407
  23.8 2.7 %collective-permute-start.6 = (f32[4,24,128]{2,1,0:T(8,128)S(1)}, f32[4,24,128]{2,1,0:T(8,128)S(1)}, u32[]{:S(2)}, u32[]{:S(2)}) collective-permute-start(f32[4,24,128]{2,1,0:T(8,128)S(1)} %get-tuple-element.26), channel_id=1, source_target_pairs={{0,480},{1,481},{2,482},{3,483},{4,484},{5,485},{6,486},{7,487},{8... | collective-permute-start | bytes 147464 | tf_op jit(solution)/shard_map/ppermute | solution.py:407
  24.5 2.0 %collective-permute-start.7 = (f32[4,24,128]{2,1,0:T(8,128)S(1)}, f32[4,24,128]{2,1,0:T(8,128)S(1)}, u32[]{:S(2)}, u32[]{:S(2)}) collective-permute-start(f32[4,24,128]{2,1,0:T(8,128)S(1)} %get-tuple-element.27), channel_id=1, source_target_pairs={{0,32},{1,33},{2,34},{3,35},{4,36},{5,37},{6,38},{7,39},{8,40},{9,... | collective-permute-start | bytes 147464 | tf_op jit(solution)/shard_map/ppermute | solution.py:407
  25.2 1.4 %collective-permute-start.8 = (f32[4,24,128]{2,1,0:T(8,128)S(1)}, f32[4,24,128]{2,1,0:T(8,128)S(1)}, u32[]{:S(2)}, u32[]{:S(2)}) collective-permute-start(f32[4,24,128]{2,1,0:T(8,128)S(1)} %get-tuple-element.28), channel_id=1, source_target_pairs={{0,1},{1,0},{2,3},{3,2},{4,5},{5,4},{6,7},{7,6},{8,9},{9,8},{10,11... | collective-permute-start | bytes 147464 | tf_op jit(solution)/shard_map/ppermute | solution.py:407
  27.1 22.0 %collective-permute-start.11 = (f32[176,128]{1,0:T(8,128)S(1)}, f32[176,128]{1,0:T(8,128)S(1)}, u32[]{:S(2)}, u32[]{:S(2)}) collective-permute-start(f32[176,128]{1,0:T(8,128)S(1)} %x_lower.1.rest_5_), channel_id=1, source_target_pairs={{0,256},{1,257},{2,258},{3,259},{4,260},{5,261},{6,262},{7,263},{8... | collective-permute-start | bytes 270344 | tf_op jit(solution)/shard_map/ppermute | solution.py:407
  28.3 20.7 %collective-permute-start.9 = (f32[168,128]{1,0:T(8,128)S(1)}, f32[168,128]{1,0:T(8,128)S(1)}, u32[]{:S(2)}, u32[]{:S(2)}) collective-permute-start(f32[168,128]{1,0:T(8,128)S(1)} %y_lower.1.rest_4_), channel_id=1, source_target_pairs={{0,16},{1,17},{2,18},{3,19},{4,20},{5,21},{6,22},{7,23},{8,24},{9,... | collective-permute-start | bytes 258056 | tf_op jit(solution)/shard_map/ppermute | solution.py:407
  30.9 18.1 %collective-permute-start.10 = (f32[160,128]{1,0:T(8,128)S(1)}, f32[160,128]{1,0:T(8,128)S(1)}, u32[]{:S(2)}, u32[]{:S(2)}) collective-permute-start(f32[160,128]{1,0:T(8,128)S(1)} %x_upper.1.rest_8_), channel_id=1, source_target_pairs={{16,272},{17,273},{18,274},{19,275},{20,276},{21,277},{22,278},{23... | collective-permute-start | bytes 245768 | tf_op jit(solution)/shard_map/ppermute | solution.py:407

commit v4 on v3

--- a/solution.py
+++ b/solution.py
@@ -176,33 +176,32 @@
     return lax.axis_index("by") >= lax.axis_size("by") // 2
 
 
-def update_kernel(which, half, extra, handed, counts, sends, numbers, sweep, table, *rest):
+def update_kernel(half, blocks, counts, handed, send_x, send_y, numbers, sweep, table, *rest):
     received, rest = rest[: sum(counts)], rest[sum(counts) :]
-    out, copies = rest[-4 - handed], rest[-3 - handed : -3]
-    for source, target in zip(rest, copies):
+    scratch = rest[-3:]
+    outs = rest[-3 - len(blocks) - handed : -3 - handed]
+    for source, target in zip(rest[:handed], rest[-3 - handed : -3]):
         target[...] = source[...]
 
-    def body():
-        update_body(which, counts, sends, numbers, sweep, table, received, out, *rest[-3:])
-        if extra:
-            out[BLOCK_ROWS : BLOCK_ROWS + extra, :] = jnp.zeros((extra, 128), jnp.float32)
-
-    if half is None:
-        body()
-    else:
-        pl.when(upper_half() == half)(body)
-
-
-def update_body(which, counts, sends, numbers, sweep, table, received, out, remote, ghost, change):
+    @pl.when(upper_half() == half)
+    def _():
+        remote = scratch[0]
+        first = 0
+        for m, count in enumerate(counts):
+            for k in range(4):
+                remote[m * 4 + k] = sum(array[k] for array in received[first : first + count])
+            first += count
+        for (which, extra), out in zip(blocks, outs):
+            s = (send_x[0, 0], send_y[0, 0], numbers[0, 2])[which]
+            update_body(s, numbers, sweep, table, out, *scratch)
+            if extra:
+                out[BLOCK_ROWS : BLOCK_ROWS + extra, :] = jnp.zeros((extra, 128), jnp.float32)
+
+
+def update_body(s, numbers, sweep, table, out, remote, ghost, change):
     turns = Turns()
     odd_x, odd_y = parities()
-    s = numbers[0, 2] if which == 2 else sends[0, 0]
     ratio = step_of(numbers[0, 8 + s])
-    first = 0
-    for m, count in enumerate(counts):
-        for k in range(4):
-            remote[m * 4 + k] = sum(array[k] for array in received[first : first + count])
-        first += count
     for face in range(6):
         direction, high = face // 2, face % 2
         code = numbers[0, 12 + s * 6 + face]
@@ -298,17 +297,18 @@
                 out[row : row + 8, :] = initial - scale * total
 
 
-def place_kernel(numbers, from_y0, from_y1, from_x0, from_x1, own, out, slots, staged, sems):
+def place_kernel(numbers, from_y0, from_y1, from_x0, from_x1, own0, own1, out, slots, staged, sems):
     codes = [numbers[0, 3 + j] for j in range(3)]
     at_x = jnp.where(codes[1] == 4, 1, jnp.where(codes[2] == 4, 2, 0))
     at_y = jnp.where(codes[1] == 5, 1, jnp.where(codes[2] == 5, 2, 0))
     at_own = 3 - at_x - at_y
+    upper = upper_half()
     empty = codes[0] + codes[1] + codes[2] == 8
     copies = []
     for f in range(5):
         one = pl.ds(f * 2 * B, 2 * B)
         values = (
-            (jnp.where(empty, 0.0, own[one, :]), at_own),
+            (jnp.where(empty, 0.0, jnp.where(upper, own0[one, :], own1[one, :])), at_own),
             (from_x0[one, :] + from_x1[one, :], at_x),
             (from_y0[one, :] + from_y1[one, :], at_y),
         )
@@ -360,15 +360,17 @@
     )(*[in_hbm(array) for array in (cells, *small)])
 
 
-def update(name, which, half, extra, sends, numbers, sweep, table, received, handed=(), after=()):
+def update(name, half, blocks, send_x, send_y, numbers, sweep, table, received, handed=(), after=()):
     counts = tuple(len(arrays) for arrays in received)
     flat = [array for arrays in received for array in arrays]
-    message = struct(BLOCK_ROWS + extra, 128)
     return pl.pallas_call(
-        functools.partial(update_kernel, which, half, extra, len(handed), counts),
-        out_shape=(message, *[struct(*array.shape) for array in handed]) if handed else message,
-        in_specs=[SMEM] * 2 + [VMEM] * (2 + len(flat) + len(handed)) + [ANY] * len(after),
-        out_specs=(VMEM,) * (1 + len(handed)) if handed else VMEM,
+        functools.partial(update_kernel, half, blocks, counts, len(handed)),
+        out_shape=(
+            *[struct(BLOCK_ROWS + extra, 128) for _, extra in blocks],
+            *[struct(*array.shape) for array in handed],
+        ),
+        in_specs=[SMEM] * 3 + [VMEM] * (2 + len(flat) + len(handed)) + [ANY] * len(after),
+        out_specs=(VMEM,) * (len(blocks) + len(handed)),
         scratch_shapes=[
             pltpu.VMEM((16, FACE_ROWS, 128), jnp.float32),
             pltpu.VMEM((5 * GHOST_ROWS, 128), jnp.float32),
@@ -376,14 +378,14 @@
         ],
         compiler_params=pltpu.CompilerParams(vmem_limit_bytes=LIMIT),
         name=name,
-    )(sends, numbers, sweep.reshape(4, SWEEP_ROWS, 128), table, *flat, *handed, *after)
+    )(send_x, send_y, numbers, sweep.reshape(4, SWEEP_ROWS, 128), table, *flat, *handed, *after)
 
 
 def place(numbers, from_y, from_x, own):
     return pl.pallas_call(
         place_kernel,
         out_shape=struct(5, 3, B * B * B),
-        in_specs=[SMEM] + [VMEM] * 5,
+        in_specs=[SMEM] + [VMEM] * 6,
         out_specs=HBM,
         scratch_shapes=[
             pltpu.VMEM((3 * BLOCK_ROWS, 128), jnp.float32),
@@ -392,7 +394,7 @@
         ],
         compiler_params=pltpu.CompilerParams(vmem_limit_bytes=LIMIT),
         name="place",
-    )(numbers, *from_y, *from_x, own)
+    )(numbers, *from_y, *from_x, *own)
 
 
 def exchange(values, move, sends):
@@ -431,23 +433,24 @@
     numbers, sweep, table, *messages = pack(
         cells_in.transpose(1, 0, 2), layout, block_levels, ghost_src, face_out
     )
-    common = (numbers, sweep, table)
+    common = (send_x, send_y, numbers, sweep, table)
     early = [exchange(m, pairing, upper) for m, pairing in zip(messages, pairings)]
-    y_upper, *messages = update(
-        "y_upper", 1, True, 8, send_y, *common, [[r] for r in early], handed=messages
-    )
+    upper_faces = [[r] for r in early]
+    y_upper, *messages = update("upper", True, ((1, 8),), *common, upper_faces, handed=messages)
     y_from_upper = exchange(y_upper, by_partner, lambda j, to_j: j >= half_y)
     late = [exchange(m, pairing, lower) for m, pairing in zip(messages, pairings)]
     lower_faces = [[early[0], late[0]], [late[1]], [late[2]], [late[3]]]
-    x_lower = update("x_lower", 0, False, 16, send_x, *common, lower_faces, after=(y_upper,))
+    x_lower, y_lower, own_lower = update(
+        "lower", False, ((0, 16), (1, 8), (2, 0)), *common, lower_faces, after=(y_upper,)
+    )
     x_from_lower = exchange(x_lower, bx_partner, lower)
-    y_lower = update("y_lower", 1, False, 8, send_y, *common, lower_faces, after=(x_lower,))
     y_from_lower = exchange(y_lower, by_partner, lambda j, to_j: j < half_y)
-    x_upper = update("x_upper", 0, True, 0, send_x, *common, [[r] for r in early], after=(y_lower, y_from_upper))
+    x_upper, own_upper = update(
+        "rest", True, ((0, 0), (2, 0)), *common, upper_faces, after=(y_lower, y_from_upper)
+    )
     x_from_upper = exchange(x_upper, bx_partner, upper)
-    own = update("own", 2, None, 0, send_x, *common, [list(p) for p in zip(early, late)], after=(x_upper,))
     from_y, from_x = (y_from_upper, y_from_lower), (x_from_upper, x_from_lower)
-    return place(numbers, from_y, from_x, own).transpose(1, 0, 2)
+    return place(numbers, from_y, from_x, (own_upper, own_lower)).transpose(1, 0, 2)
 
 
 def solution(mesh):

time: 50.9 us -> 52.4 us (1.029)
  the two profiles are of different devices: /device:TPU:448 before, /device:TPU:32 now
where the time goes in v4:
time: 52.4 us; the launch traced here: 52.1 us
  starting transfers between devices  33.2 us (63%)
  Pallas kernels  9.81 us (19%)
  waiting for transfers between devices  7.57 us (14%)
  between operations  1.48 us (3%)
    ppermute x12, starting transfers between devices, exchange(): return lax.ppermute(values, ('bx', 'by'), pairs)  33.2 us
    ppermute x12, waiting for transfers between devices, exchange(): return lax.ppermute(values, ('bx', 'by'), pairs)  7.57 us
    pallas_call x3, Pallas kernels, update(): pl.pallas_call(functools.partial(update_kernel, half, blocks, counts, len...  5.91 us
    pallas_call x1, Pallas kernels, pack(): pl.pallas_call(pack_kernel, out_shape=(jax.ShapeDtypeStruct((1, 128), jnp...  2.47 us
    pallas_call x1, Pallas kernels, place(): pl.pallas_call(place_kernel, out_shape=struct(5, 3, B * B * B), in_specs=...  1.43 us
  transfers between devices with their start and end apart: 12, of which 3 were waited for; matrix products, arithmetic and copies ran while one was open for 0% of the time, Pallas kernels for 10%

profile of v4, /device:TPU:32, one launch (start us, length us, event | category | flops | bytes accessed | tf_op | source)
XLA Modules:
  0.0 52.1 jit_solution(6646127317699531985)
XLA Ops:
  0.0 2.5 %pack.1 = (s32[1,128]{1,0:T(1,128)S(1)}, f32[2560,128]{1,0:T(8,128)S(1)}, f32[24,24,128]{2,1,0:T(8,128)S(1)}, f32[4,24,128]{2,1,0:T(8,128)S(1)}, f32[4,24,128]{2...) custom-call(f32[5,4,4096]{2,1,0:T(4,128)} %bitcast.6, s32[1,3]{1,0:T(1,128)} %layout_in.1, ...), custom_call_target="tpu_custom_call" | custom-call | tf_op jit(solution)/shard_map/pack/pallas_call | solution.py:342
  2.5 13.7 %collective-permute-start = (f32[4,24,128]{2,1,0:T(8,128)S(1)}, f32[4,24,128]{2,1,0:T(8,128)S(1)}, u32[]{:S(2)}, u32[]{:S(2)}) collective-permute-start(f32[4,24,128]{2,1,0:T(8,128)S(1)} %get-tuple-element.25.rest_4_), channel_id=1, source_target_pairs={{0,31},{15,16},{16,15},{17,18},{18,17},{19,20},{20,19},{21,22},{22... | collective-permute-start | bytes 147464 | tf_op jit(solution)/shard_map/ppermute | solution.py:409
  16.2 0.7 %collective-permute-start.1 = (f32[4,24,128]{2,1,0:T(8,128)S(1)}, f32[4,24,128]{2,1,0:T(8,128)S(1)}, u32[]{:S(2)}, u32[]{:S(2)}) collective-permute-start(f32[4,24,128]{2,1,0:T(8,128)S(1)} %get-tuple-element.26.rest_5_), channel_id=1, source_target_pairs={{16,496},{17,497},{18,498},{19,499},{20,500},{21,501},{22,502},{23... | collective-permute-start | bytes 147464 | tf_op jit(solution)/shard_map/ppermute | solution.py:409
  16.9 0.7 %collective-permute-start.2 = (f32[4,24,128]{2,1,0:T(8,128)S(1)}, f32[4,24,128]{2,1,0:T(8,128)S(1)}, u32[]{:S(2)}, u32[]{:S(2)}) collective-permute-start(f32[4,24,128]{2,1,0:T(8,128)S(1)} %get-tuple-element.27.rest_6_), channel_id=1, source_target_pairs={{16,48},{17,49},{18,50},{19,51},{20,52},{21,53},{22,54},{23,55},{2... | collective-permute-start | bytes 147464 | tf_op jit(solution)/shard_map/ppermute | solution.py:409
  17.6 0.7 %collective-permute-start.3 = (f32[4,24,128]{2,1,0:T(8,128)S(1)}, f32[4,24,128]{2,1,0:T(8,128)S(1)}, u32[]{:S(2)}, u32[]{:S(2)}) collective-permute-start(f32[4,24,128]{2,1,0:T(8,128)S(1)} %get-tuple-element.28.rest_7_), channel_id=1, source_target_pairs={{16,17},{17,16},{18,19},{19,18},{20,21},{21,20},{22,23},{23,22},{2... | collective-permute-start | bytes 147464 | tf_op jit(solution)/shard_map/ppermute | solution.py:409
  19.5 0.0 collective-permute-done.rest_0_
  19.5 0.0 collective-permute-done.1.rest_1_
  19.5 0.0 collective-permute-done.2.rest_2_
  19.6 0.0 collective-permute-done.3.rest_3_
  19.6 0.6 %upper.1 = (f32[168,128]{1,0:T(8,128)S(1)}, f32[4,24,128]{2,1,0:T(8,128)S(1)}, f32[4,24,128]{2,1,0:T(8,128)S(1)}, f32[4,24,128]{2,1,0:T(8,128)S(1)}, f32[4,24,128]{2,1,0:T(8,128)S(1)}) custom-call(s32[1,1]{1,0:T(1,128)S(6)} %copy.8.send_x, s32[1,1]{1,0:T(1,128)S(6)} %copy.9.send_y, s32[1,128]{1,0:T(1,128)S(1)} %get-tuple-element.22.numbers, ...), custom_call_target="tpu_custom_call" | custom-call | tf_op jit(solution)/shard_map/upper/pallas_call | solution.py:366
  20.1 1.3 %collective-permute-start.4 = (f32[168,128]{1,0:T(8,128)S(1)}, f32[168,128]{1,0:T(8,128)S(1)}, u32[]{:S(2)}, u32[]{:S(2)}) collective-permute-start(f32[168,128]{1,0:T(8,128)S(1)} %get-tuple-element.29.rest_5_), channel_id=1, source_target_pairs={{16,0},{17,1},{18,2},{19,3},{20,4},{21,5},{22,6},{23,7},{24,8},{25... | collective-permute-start | bytes 258056 | tf_op jit(solution)/shard_map/ppermute | solution.py:409
  21.4 0.7 %collective-permute-start.5 = (f32[4,24,128]{2,1,0:T(8,128)S(1)}, f32[4,24,128]{2,1,0:T(8,128)S(1)}, u32[]{:S(2)}, u32[]{:S(2)}) collective-permute-start(f32[4,24,128]{2,1,0:T(8,128)S(1)} %get-tuple-element.30), channel_id=1, source_target_pairs={{1,2},{2,1},{3,4},{4,3},{5,6},{6,5},{7,8},{8,7},{9,10},{10,9},{11,... | collective-permute-start | bytes 147464 | tf_op jit(solution)/shard_map/ppermute | solution.py:409
  22.1 2.9 %collective-permute-start.6 = (f32[4,24,128]{2,1,0:T(8,128)S(1)}, f32[4,24,128]{2,1,0:T(8,128)S(1)}, u32[]{:S(2)}, u32[]{:S(2)}) collective-permute-start(f32[4,24,128]{2,1,0:T(8,128)S(1)} %get-tuple-element.31), channel_id=1, source_target_pairs={{0,480},{1,481},{2,482},{3,483},{4,484},{5,485},{6,486},{7,487},{8... | collective-permute-start | bytes 147464 | tf_op jit(solution)/shard_map/ppermute | solution.py:409
  25.0 6.0 %collective-permute-start.7 = (f32[4,24,128]{2,1,0:T(8,128)S(1)}, f32[4,24,128]{2,1,0:T(8,128)S(1)}, u32[]{:S(2)}, u32[]{:S(2)}) collective-permute-start(f32[4,24,128]{2,1,0:T(8,128)S(1)} %get-tuple-element.32), channel_id=1, source_target_pairs={{0,32},{1,33},{2,34},{3,35},{4,36},{5,37},{6,38},{7,39},{8,40},{9,... | collective-permute-start | bytes 147464 | tf_op jit(solution)/shard_map/ppermute | solution.py:409
  31.1 1.9 %collective-permute-start.8 = (f32[4,24,128]{2,1,0:T(8,128)S(1)}, f32[4,24,128]{2,1,0:T(8,128)S(1)}, u32[]{:S(2)}, u32[]{:S(2)}) collective-permute-start(f32[4,24,128]{2,1,0:T(8,128)S(1)} %get-tuple-element.33), channel_id=1, source_target_pairs={{0,1},{1,0},{2,3},{3,2},{4,5},{5,4},{6,7},{7,6},{8,9},{9,8},{10,11... | collective-permute-start | bytes 147464 | tf_op jit(solution)/shard_map/ppermute | solution.py:409
  33.0 0.0 collective-permute-done.5.rest_1_
  33.0 0.0 collective-permute-done.6.rest_2_
  33.0 0.7 %collective-permute-done.7.rest_3_ = f32[4,24,128]{2,1,0:T(8,128)S(1)} collective-permute-done((f32[4,24,128]{2,1,0:T(8,128)S(1)}, f32[4,24,128]{2,1,0:T(8,128)S(1)}, u32[]{:S(2)}, u32[]{:S(2)}) %collective-permute-start.7) | collective-permute-done | bytes 49184 | tf_op jit(solution)/shard_map/ppermute | solution.py:409
  33.7 0.5 collective-permute-done.8.rest_4_
  34.2 4.8 %lower.1 = (f32[176,128]{1,0:T(8,128)S(1)}, f32[168,128]{1,0:T(8,128)S(1)}, f32[160,128]{1,0:T(8,128)S(1)}) custom-call(s32[1,1]{1,0:T(1,128)S(6)} %copy.8.send_x, s32[1,1]{1,0:T(1,128)S(6)} %copy.9.send_y, s32[1,128]{1,0:T(1,128)S(1)} %get-tuple-element.22.numbers, f32[4,640,128]{2,1,0:T(8,128)S(1)} %bitcast.4, f32[24,24,128]{2,1,0:T(8,128)S(1)} %get-tuple-element.24.table, ...), custom_call_target="tpu_custom_call" | custom-call | tf_op jit(solution)/shard_map/lower/pallas_call | solution.py:366
  39.0 2.7 %collective-permute-start.11 = (f32[176,128]{1,0:T(8,128)S(1)}, f32[176,128]{1,0:T(8,128)S(1)}, u32[]{:S(2)}, u32[]{:S(2)}) collective-permute-start(f32[176,128]{1,0:T(8,128)S(1)} %get-tuple-element.36), channel_id=1, source_target_pairs={{0,256},{1,257},{2,258},{3,259},{4,260},{5,261},{6,262},{7,263},{8... | collective-permute-start | bytes 270344 | tf_op jit(solution)/shard_map/ppermute | solution.py:409
  41.7 1.3 %collective-permute-start.9 = (f32[168,128]{1,0:T(8,128)S(1)}, f32[168,128]{1,0:T(8,128)S(1)}, u32[]{:S(2)}, u32[]{:S(2)}) collective-permute-start(f32[168,128]{1,0:T(8,128)S(1)} %get-tuple-element.34.rest_4_), channel_id=1, source_target_pairs={{0,16},{1,17},{2,18},{3,19},{4,20},{5,21},{6,22},{7,23},{8,24},{9,... | collective-permute-start | bytes 258056 | tf_op jit(solution)/shard_map/ppermute | solution.py:409
  43.0 0.0 collective-permute-done.4.rest_5_.from_y0
  43.0 0.6 %rest.1 = (f32[160,128]{1,0:T(8,128)S(1)}, f32[160,128]{1,0:T(8,128)S(1)}) custom-call(s32[1,1]{1,0:T(1,128)S(6)} %copy.8.send_x, s32[1,1]{1,0:T(1,128)S(6)} %copy.9.send_y, s32[1,128]{1,0:T(1,128)S(1)} %get-tuple-element.22.numbers, f32[4,640,128]{2,1,0:T(8,128)S(1)} %bitcast.5, f32[24,24,128]{2,1,0:T(8,128)S(1)} %get-tuple-element.24.table, ...), custom_call_target="tpu_custom_call" | custom-call | tf_op jit(solution)/shard_map/rest/pallas_call | solution.py:366
  43.6 0.7 %collective-permute-start.10 = (f32[160,128]{1,0:T(8,128)S(1)}, f32[160,128]{1,0:T(8,128)S(1)}, u32[]{:S(2)}, u32[]{:S(2)}) collective-permute-start(f32[160,128]{1,0:T(8,128)S(1)} %get-tuple-element.35), channel_id=1, source_target_pairs={{16,272},{17,273},{18,274},{19,275},{20,276},{21,277},{22,278},{23... | collective-permute-start | bytes 245768 | tf_op jit(solution)/shard_map/ppermute | solution.py:409
  44.3 6.4 %collective-permute-done.9.from_y1 = f32[168,128]{1,0:T(8,128)S(1)} collective-permute-done((f32[168,128]{1,0:T(8,128)S(1)}, f32[168,128]{1,0:T(8,128)S(1)}, u32[]{:S(2)}, u32[]{:S(2)}) %collective-permute-start.9) | collective-permute-done | bytes 86048 | tf_op jit(solution)/shard_map/ppermute | solution.py:409
  50.6 0.0 collective-permute-done.11.from_x1
  50.6 0.0 collective-permute-done.10.from_x0
  50.6 1.4 %place.1 = f32[5,3,4096]{2,1,0:T(4,128)} custom-call(s32[1,128]{1,0:T(1,128)S(1)} %get-tuple-element.22.numbers, f32[168,128]{1,0:T(8,128)S(1)} %collective-permute-done.4.rest_5_.from_y0, f32[168,128]{1,0:T(8,128)S(1)} %collective-permute-done.9.from_y1, f32[160,128]{1,0:T(8,128)S(1)} %collective-permute-done.10.from_x0, ...), custom_call_target="tpu_custom_call" | custom-call | tf_op jit(solution)/shard_map/place/pallas_call | solution.py:385
Async XLA Ops:
  2.5 17.0 %collective-permute-start = (f32[4,24,128]{2,1,0:T(8,128)S(1)}, f32[4,24,128]{2,1,0:T(8,128)S(1)}, u32[]{:S(2)}, u32[]{:S(2)}) collective-permute-start(f32[4,24,128]{2,1,0:T(8,128)S(1)} %get-tuple-element.25.rest_4_), channel_id=1, source_target_pairs={{0,31},{15,16},{16,15},{17,18},{18,17},{19,20},{20,19},{21,22},{22... | collective-permute-start | bytes 147464 | tf_op jit(solution)/shard_map/ppermute | solution.py:409
  16.2 3.3 %collective-permute-start.1 = (f32[4,24,128]{2,1,0:T(8,128)S(1)}, f32[4,24,128]{2,1,0:T(8,128)S(1)}, u32[]{:S(2)}, u32[]{:S(2)}) collective-permute-start(f32[4,24,128]{2,1,0:T(8,128)S(1)} %get-tuple-element.26.rest_5_), channel_id=1, source_target_pairs={{16,496},{17,497},{18,498},{19,499},{20,500},{21,501},{22,502},{23... | collective-permute-start | bytes 147464 | tf_op jit(solution)/shard_map/ppermute | solution.py:409
  16.9 2.7 %collective-permute-start.2 = (f32[4,24,128]{2,1,0:T(8,128)S(1)}, f32[4,24,128]{2,1,0:T(8,128)S(1)}, u32[]{:S(2)}, u32[]{:S(2)}) collective-permute-start(f32[4,24,128]{2,1,0:T(8,128)S(1)} %get-tuple-element.27.rest_6_), channel_id=1, source_target_pairs={{16,48},{17,49},{18,50},{19,51},{20,52},{21,53},{22,54},{23,55},{2... | collective-permute-start | bytes 147464 | tf_op jit(solution)/shard_map/ppermute | solution.py:409
  17.6 2.0 %collective-permute-start.3 = (f32[4,24,128]{2,1,0:T(8,128)S(1)}, f32[4,24,128]{2,1,0:T(8,128)S(1)}, u32[]{:S(2)}, u32[]{:S(2)}) collective-permute-start(f32[4,24,128]{2,1,0:T(8,128)S(1)} %get-tuple-element.28.rest_7_), channel_id=1, source_target_pairs={{16,17},{17,16},{18,19},{19,18},{20,21},{21,20},{22,23},{23,22},{2... | collective-permute-start | bytes 147464 | tf_op jit(solution)/shard_map/ppermute | solution.py:409
  20.1 22.9 %collective-permute-start.4 = (f32[168,128]{1,0:T(8,128)S(1)}, f32[168,128]{1,0:T(8,128)S(1)}, u32[]{:S(2)}, u32[]{:S(2)}) collective-permute-start(f32[168,128]{1,0:T(8,128)S(1)} %get-tuple-element.29.rest_5_), channel_id=1, source_target_pairs={{16,0},{17,1},{18,2},{19,3},{20,4},{21,5},{22,6},{23,7},{24,8},{25... | collective-permute-start | bytes 258056 | tf_op jit(solution)/shard_map/ppermute | solution.py:409
  21.4 11.6 %collective-permute-start.5 = (f32[4,24,128]{2,1,0:T(8,128)S(1)}, f32[4,24,128]{2,1,0:T(8,128)S(1)}, u32[]{:S(2)}, u32[]{:S(2)}) collective-permute-start(f32[4,24,128]{2,1,0:T(8,128)S(1)} %get-tuple-element.30), channel_id=1, source_target_pairs={{1,2},{2,1},{3,4},{4,3},{5,6},{6,5},{7,8},{8,7},{9,10},{10,9},{11,... | collective-permute-start | bytes 147464 | tf_op jit(solution)/shard_map/ppermute | solution.py:409
  22.1 10.9 %collective-permute-start.6 = (f32[4,24,128]{2,1,0:T(8,128)S(1)}, f32[4,24,128]{2,1,0:T(8,128)S(1)}, u32[]{:S(2)}, u32[]{:S(2)}) collective-permute-start(f32[4,24,128]{2,1,0:T(8,128)S(1)} %get-tuple-element.31), channel_id=1, source_target_pairs={{0,480},{1,481},{2,482},{3,483},{4,484},{5,485},{6,486},{7,487},{8... | collective-permute-start | bytes 147464 | tf_op jit(solution)/shard_map/ppermute | solution.py:409
  25.0 8.7 %collective-permute-start.7 = (f32[4,24,128]{2,1,0:T(8,128)S(1)}, f32[4,24,128]{2,1,0:T(8,128)S(1)}, u32[]{:S(2)}, u32[]{:S(2)}) collective-permute-start(f32[4,24,128]{2,1,0:T(8,128)S(1)} %get-tuple-element.32), channel_id=1, source_target_pairs={{0,32},{1,33},{2,34},{3,35},{4,36},{5,37},{6,38},{7,39},{8,40},{9,... | collective-permute-start | bytes 147464 | tf_op jit(solution)/shard_map/ppermute | solution.py:409
  31.1 3.1 %collective-permute-start.8 = (f32[4,24,128]{2,1,0:T(8,128)S(1)}, f32[4,24,128]{2,1,0:T(8,128)S(1)}, u32[]{:S(2)}, u32[]{:S(2)}) collective-permute-start(f32[4,24,128]{2,1,0:T(8,128)S(1)} %get-tuple-element.33), channel_id=1, source_target_pairs={{0,1},{1,0},{2,3},{3,2},{4,5},{5,4},{6,7},{7,6},{8,9},{9,8},{10,11... | collective-permute-start | bytes 147464 | tf_op jit(solution)/shard_map/ppermute | solution.py:409
  39.0 11.6 %collective-permute-start.11 = (f32[176,128]{1,0:T(8,128)S(1)}, f32[176,128]{1,0:T(8,128)S(1)}, u32[]{:S(2)}, u32[]{:S(2)}) collective-permute-start(f32[176,128]{1,0:T(8,128)S(1)} %get-tuple-element.36), channel_id=1, source_target_pairs={{0,256},{1,257},{2,258},{3,259},{4,260},{5,261},{6,262},{7,263},{8... | collective-permute-start | bytes 270344 | tf_op jit(solution)/shard_map/ppermute | solution.py:409
  41.7 8.9 %collective-permute-start.9 = (f32[168,128]{1,0:T(8,128)S(1)}, f32[168,128]{1,0:T(8,128)S(1)}, u32[]{:S(2)}, u32[]{:S(2)}) collective-permute-start(f32[168,128]{1,0:T(8,128)S(1)} %get-tuple-element.34.rest_4_), channel_id=1, source_target_pairs={{0,16},{1,17},{2,18},{3,19},{4,20},{5,21},{6,22},{7,23},{8,24},{9,... | collective-permute-start | bytes 258056 | tf_op jit(solution)/shard_map/ppermute | solution.py:409
  43.6 7.0 %collective-permute-start.10 = (f32[160,128]{1,0:T(8,128)S(1)}, f32[160,128]{1,0:T(8,128)S(1)}, u32[]{:S(2)}, u32[]{:S(2)}) collective-permute-start(f32[160,128]{1,0:T(8,128)S(1)} %get-tuple-element.35), channel_id=1, source_target_pairs={{16,272},{17,273},{18,274},{19,275},{20,276},{21,277},{22,278},{23... | collective-permute-start | bytes 245768 | tf_op jit(solution)/shard_map/ppermute | solution.py:409

commit v5 on v4

--- a/solution.py
+++ b/solution.py
@@ -183,8 +183,7 @@
     for source, target in zip(rest[:handed], rest[-3 - handed : -3]):
         target[...] = source[...]
 
-    @pl.when(upper_half() == half)
-    def _():
+    def body():
         remote = scratch[0]
         first = 0
         for m, count in enumerate(counts):
@@ -196,6 +195,11 @@
             update_body(s, numbers, sweep, table, out, *scratch)
             if extra:
                 out[BLOCK_ROWS : BLOCK_ROWS + extra, :] = jnp.zeros((extra, 128), jnp.float32)
+
+    if half is None:
+        body()
+    else:
+        pl.when(upper_half() == half)(body)
 
 
 def update_body(s, numbers, sweep, table, out, remote, ghost, change):
@@ -297,18 +301,17 @@
                 out[row : row + 8, :] = initial - scale * total
 
 
-def place_kernel(numbers, from_y0, from_y1, from_x0, from_x1, own0, own1, out, slots, staged, sems):
+def place_kernel(numbers, from_y0, from_y1, from_x0, from_x1, own, out, slots, staged, sems):
     codes = [numbers[0, 3 + j] for j in range(3)]
     at_x = jnp.where(codes[1] == 4, 1, jnp.where(codes[2] == 4, 2, 0))
     at_y = jnp.where(codes[1] == 5, 1, jnp.where(codes[2] == 5, 2, 0))
     at_own = 3 - at_x - at_y
-    upper = upper_half()
     empty = codes[0] + codes[1] + codes[2] == 8
     copies = []
     for f in range(5):
         one = pl.ds(f * 2 * B, 2 * B)
         values = (
-            (jnp.where(empty, 0.0, jnp.where(upper, own0[one, :], own1[one, :])), at_own),
+            (jnp.where(empty, 0.0, own[one, :]), at_own),
             (from_x0[one, :] + from_x1[one, :], at_x),
             (from_y0[one, :] + from_y1[one, :], at_y),
         )
@@ -385,7 +388,7 @@
     return pl.pallas_call(
         place_kernel,
         out_shape=struct(5, 3, B * B * B),
-        in_specs=[SMEM] + [VMEM] * 6,
+        in_specs=[SMEM] + [VMEM] * 5,
         out_specs=HBM,
         scratch_shapes=[
             pltpu.VMEM((3 * BLOCK_ROWS, 128), jnp.float32),
@@ -394,7 +397,7 @@
         ],
         compiler_params=pltpu.CompilerParams(vmem_limit_bytes=LIMIT),
         name="place",
-    )(numbers, *from_y, *from_x, *own)
+    )(numbers, *from_y, *from_x, own)
 
 
 def exchange(values, move, sends):
@@ -424,6 +427,9 @@
     def lower(j, to_j):
         return not upper(j, to_j)
 
+    def anyone(j, to_j):
+        return True
+
     def by_partner(i, j):
         return i, j ^ half_y
 
@@ -434,23 +440,30 @@
         cells_in.transpose(1, 0, 2), layout, block_levels, ghost_src, face_out
     )
     common = (send_x, send_y, numbers, sweep, table)
-    early = [exchange(m, pairing, upper) for m, pairing in zip(messages, pairings)]
+    early = [
+        exchange(m, pairing, sends)
+        for m, pairing, sends in zip(messages, pairings, (anyone, upper, upper, upper))
+    ]
     upper_faces = [[r] for r in early]
-    y_upper, *messages = update("upper", True, ((1, 8),), *common, upper_faces, handed=messages)
+    y_upper, *messages = update(
+        "y_upper", True, ((1, 8),), *common, upper_faces, handed=messages[1:]
+    )
     y_from_upper = exchange(y_upper, by_partner, lambda j, to_j: j >= half_y)
-    late = [exchange(m, pairing, lower) for m, pairing in zip(messages, pairings)]
-    lower_faces = [[early[0], late[0]], [late[1]], [late[2]], [late[3]]]
-    x_lower, y_lower, own_lower = update(
-        "lower", False, ((0, 16), (1, 8), (2, 0)), *common, lower_faces, after=(y_upper,)
+    late = [exchange(m, pairing, lower) for m, pairing in zip(messages, pairings[1:])]
+    lower_faces = [[r] for r in (early[0], *late)]
+    x_lower, y_lower = update(
+        "lower", False, ((0, 16), (1, 8)), *common, lower_faces, after=(y_upper,)
     )
     x_from_lower = exchange(x_lower, bx_partner, lower)
     y_from_lower = exchange(y_lower, by_partner, lambda j, to_j: j < half_y)
-    x_upper, own_upper = update(
-        "rest", True, ((0, 0), (2, 0)), *common, upper_faces, after=(y_lower, y_from_upper)
+    (x_upper,) = update(
+        "x_upper", True, ((0, 0),), *common, upper_faces, after=(y_lower, y_from_upper)
     )
     x_from_upper = exchange(x_upper, bx_partner, upper)
+    all_faces = [[early[0]], *[list(pair) for pair in zip(early[1:], late)]]
+    (own,) = update("own", None, ((2, 0),), *common, all_faces, after=(x_upper,))
     from_y, from_x = (y_from_upper, y_from_lower), (x_from_upper, x_from_lower)
-    return place(numbers, from_y, from_x, (own_upper, own_lower)).transpose(1, 0, 2)
+    return place(numbers, from_y, from_x, own).transpose(1, 0, 2)
 
 
 def solution(mesh):

time: 52.4 us -> 50.4 us (0.962)
  the two profiles are of different devices: /device:TPU:32 before, /device:TPU:33 now
where the time goes in v5:
time: 50.4 us; the launch traced here: 50.1 us
  starting transfers between devices  33.5 us (66%)
  Pallas kernels  9.07 us (18%)
  waiting for transfers between devices  6.07 us (12%)
  between operations  1.47 us (3%)
    ppermute x11, starting transfers between devices, exchange(): return lax.ppermute(values, ('bx', 'by'), pairs)  33.5 us
    ppermute x11, waiting for transfers between devices, exchange(): return lax.ppermute(values, ('bx', 'by'), pairs)  6.07 us
    pallas_call x4, Pallas kernels, update(): pl.pallas_call(functools.partial(update_kernel, half, blocks, counts, len...  5.16 us
    pallas_call x1, Pallas kernels, pack(): pl.pallas_call(pack_kernel, out_shape=(jax.ShapeDtypeStruct((1, 128), jnp...  2.47 us
    pallas_call x1, Pallas kernels, place(): pl.pallas_call(place_kernel, out_shape=struct(5, 3, B * B * B), in_specs=...  1.45 us
  transfers between devices with their start and end apart: 11, of which 2 were waited for; matrix products, arithmetic and copies ran while one was open for 0% of the time, Pallas kernels for 9%

profile of v5, /device:TPU:33, one launch (start us, length us, event | category | flops | bytes accessed | tf_op | source)
XLA Modules:
  0.0 50.1 jit_solution(4156257493727053173)
XLA Ops:
  0.0 2.5 %pack.1 = (s32[1,128]{1,0:T(1,128)S(1)}, f32[2560,128]{1,0:T(8,128)S(1)}, f32[24,24,128]{2,1,0:T(8,128)S(1)}, f32[4,24,128]{2,1,0:T(8,128)S(1)}, f32[4,24,128]{2...) custom-call(f32[5,4,4096]{2,1,0:T(4,128)} %bitcast.7, s32[1,3]{1,0:T(1,128)} %layout_in.1, ...), custom_call_target="tpu_custom_call" | custom-call | tf_op jit(solution)/shard_map/pack/pallas_call | solution.py:345
  2.5 3.8 %collective-permute-start = (f32[4,24,128]{2,1,0:T(8,128)S(1)}, f32[4,24,128]{2,1,0:T(8,128)S(1)}, u32[]{:S(2)}, u32[]{:S(2)}) collective-permute-start(f32[4,24,128]{2,1,0:T(8,128)S(1)} %get-tuple-element.21), channel_id=1, source_target_pairs={{0,31},{1,2},{2,1},{3,4},{4,3},{5,6},{6,5},{7,8},{8,7},{9,10},{10,... | collective-permute-start | bytes 147464 | tf_op jit(solution)/shard_map/ppermute | solution.py:412
  6.3 0.7 %collective-permute-start.1 = (f32[4,24,128]{2,1,0:T(8,128)S(1)}, f32[4,24,128]{2,1,0:T(8,128)S(1)}, u32[]{:S(2)}, u32[]{:S(2)}) collective-permute-start(f32[4,24,128]{2,1,0:T(8,128)S(1)} %get-tuple-element.22.rest_4_), channel_id=1, source_target_pairs={{16,496},{17,497},{18,498},{19,499},{20,500},{21,501},{22,502},{23... | collective-permute-start | bytes 147464 | tf_op jit(solution)/shard_map/ppermute | solution.py:412
  6.9 0.7 %collective-permute-start.2 = (f32[4,24,128]{2,1,0:T(8,128)S(1)}, f32[4,24,128]{2,1,0:T(8,128)S(1)}, u32[]{:S(2)}, u32[]{:S(2)}) collective-permute-start(f32[4,24,128]{2,1,0:T(8,128)S(1)} %get-tuple-element.23.rest_5_), channel_id=1, source_target_pairs={{16,48},{17,49},{18,50},{19,51},{20,52},{21,53},{22,54},{23,55},{2... | collective-permute-start | bytes 147464 | tf_op jit(solution)/shard_map/ppermute | solution.py:412
  7.6 0.7 %collective-permute-start.3 = (f32[4,24,128]{2,1,0:T(8,128)S(1)}, f32[4,24,128]{2,1,0:T(8,128)S(1)}, u32[]{:S(2)}, u32[]{:S(2)}) collective-permute-start(f32[4,24,128]{2,1,0:T(8,128)S(1)} %get-tuple-element.24.rest_6_), channel_id=1, source_target_pairs={{16,17},{17,16},{18,19},{19,18},{20,21},{21,20},{22,23},{23,22},{2... | collective-permute-start | bytes 147464 | tf_op jit(solution)/shard_map/ppermute | solution.py:412
  9.6 0.0 collective-permute-done.rest_0_
  9.6 0.0 collective-permute-done.1.rest_1_
  9.6 0.0 collective-permute-done.2.rest_2_.rest_3_
  9.6 0.0 collective-permute-done.3.rest_3_.rest_5_
  9.6 0.6 %y_upper.1 = (f32[168,128]{1,0:T(8,128)S(1)}, f32[4,24,128]{2,1,0:T(8,128)S(1)}, f32[4,24,128]{2,1,0:T(8,128)S(1)}, f32[4,24,128]{2,1,0:T(8,128)S(1)}) custom-call(s32[1,1]{1,0:T(1,128)S(6)} %copy.8.send_x, s32[1,1]{1,0:T(1,128)S(6)} %copy.9.send_y, s32[1,128]{1,0:T(1,128)S(1)} %get-tuple-element.18.numbers, f32[4,640,128]{2,1,0:T(8,128)S(1)} %bitcast.3, ...), custom_call_target="tpu_custom_call" | custom-call | tf_op jit(solution)/shard_map/y_upper/pallas_call | solution.py:369
  10.2 1.3 %collective-permute-start.4 = (f32[168,128]{1,0:T(8,128)S(1)}, f32[168,128]{1,0:T(8,128)S(1)}, u32[]{:S(2)}, u32[]{:S(2)}) collective-permute-start(f32[168,128]{1,0:T(8,128)S(1)} %get-tuple-element.25.rest_4_), channel_id=1, source_target_pairs={{16,0},{17,1},{18,2},{19,3},{20,4},{21,5},{22,6},{23,7},{24,8},{25... | collective-permute-start | bytes 258056 | tf_op jit(solution)/shard_map/ppermute | solution.py:412
  11.5 3.5 %collective-permute-start.5 = (f32[4,24,128]{2,1,0:T(8,128)S(1)}, f32[4,24,128]{2,1,0:T(8,128)S(1)}, u32[]{:S(2)}, u32[]{:S(2)}) collective-permute-start(f32[4,24,128]{2,1,0:T(8,128)S(1)} %get-tuple-element.26), channel_id=1, source_target_pairs={{0,480},{1,481},{2,482},{3,483},{4,484},{5,485},{6,486},{7,487},{8... | collective-permute-start | bytes 147464 | tf_op jit(solution)/shard_map/ppermute | solution.py:412
  15.0 6.6 %collective-permute-start.6 = (f32[4,24,128]{2,1,0:T(8,128)S(1)}, f32[4,24,128]{2,1,0:T(8,128)S(1)}, u32[]{:S(2)}, u32[]{:S(2)}) collective-permute-start(f32[4,24,128]{2,1,0:T(8,128)S(1)} %get-tuple-element.27), channel_id=1, source_target_pairs={{0,32},{1,33},{2,34},{3,35},{4,36},{5,37},{6,38},{7,39},{8,40},{9,... | collective-permute-start | bytes 147464 | tf_op jit(solution)/shard_map/ppermute | solution.py:412
  21.7 11.3 %collective-permute-start.7 = (f32[4,24,128]{2,1,0:T(8,128)S(1)}, f32[4,24,128]{2,1,0:T(8,128)S(1)}, u32[]{:S(2)}, u32[]{:S(2)}) collective-permute-start(f32[4,24,128]{2,1,0:T(8,128)S(1)} %get-tuple-element.28), channel_id=1, source_target_pairs={{0,1},{1,0},{2,3},{3,2},{4,5},{5,4},{6,7},{7,6},{8,9},{9,8},{10,11... | collective-permute-start | bytes 147464 | tf_op jit(solution)/shard_map/ppermute | solution.py:412
  33.0 0.0 collective-permute-done.5.rest_1_.rest_2_
  33.0 0.0 collective-permute-done.6.rest_2_.rest_4_
  33.0 0.8 %collective-permute-done.7.rest_3_.rest_6_ = f32[4,24,128]{2,1,0:T(8,128)S(1)} collective-permute-done((f32[4,24,128]{2,1,0:T(8,128)S(1)}, f32[4,24,128]{2,1,0:T(8,128)S(1)}, u32[]{:S(2)}, u32[]{:S(2)}) %collective-permute-start.7) | collective-permute-done | bytes 49184 | tf_op jit(solution)/shard_map/ppermute | solution.py:412
  33.8 2.8 %lower.1 = (f32[176,128]{1,0:T(8,128)S(1)}, f32[168,128]{1,0:T(8,128)S(1)}) custom-call(s32[1,1]{1,0:T(1,128)S(6)} %copy.8.send_x, s32[1,1]{1,0:T(1,128)S(6)} %copy.9.send_y, s32[1,128]{1,0:T(1,128)S(1)} %get-tuple-element.18.numbers, f32[4,640,128]{2,1,0:T(8,128)S(1)} %bitcast.4, f32[24,24,128]{2,1,0:T(8,128)S(1)} %get-tuple-element.20.table, ...), custom_call_target="tpu_custom_call" | custom-call | tf_op jit(solution)/shard_map/lower/pallas_call | solution.py:369
  36.7 2.4 %collective-permute-start.10 = (f32[176,128]{1,0:T(8,128)S(1)}, f32[176,128]{1,0:T(8,128)S(1)}, u32[]{:S(2)}, u32[]{:S(2)}) collective-permute-start(f32[176,128]{1,0:T(8,128)S(1)} %get-tuple-element.30), channel_id=1, source_target_pairs={{0,256},{1,257},{2,258},{3,259},{4,260},{5,261},{6,262},{7,263},{8... | collective-permute-start | bytes 270344 | tf_op jit(solution)/shard_map/ppermute | solution.py:412
  39.1 1.8 %collective-permute-start.8 = (f32[168,128]{1,0:T(8,128)S(1)}, f32[168,128]{1,0:T(8,128)S(1)}, u32[]{:S(2)}, u32[]{:S(2)}) collective-permute-start(f32[168,128]{1,0:T(8,128)S(1)} %get-tuple-element.29.rest_4_), channel_id=1, source_target_pairs={{0,16},{1,17},{2,18},{3,19},{4,20},{5,21},{6,22},{7,23},{8,24},{9,... | collective-permute-start | bytes 258056 | tf_op jit(solution)/shard_map/ppermute | solution.py:412
  41.0 0.0 collective-permute-done.4.rest_5_.from_y0
  41.0 0.6 %x_upper.1.rest_7_ = f32[160,128]{1,0:T(8,128)S(1)} custom-call(s32[1,1]{1,0:T(1,128)S(6)} %copy.8.send_x, s32[1,1]{1,0:T(1,128)S(6)} %copy.9.send_y, s32[1,128]{1,0:T(1,128)S(1)} %get-tuple-element.18.numbers, f32[4,640,128]{2,1,0:T(8,128)S(1)} %bitcast.5, f32[24,24,128]{2,1,0:T(8,128)S(1)} %get-tuple-element.20.table, ...), custom_call_target="tpu_custom_call" | custom-call | tf_op jit(solution)/shard_map/x_upper/pallas_call | solution.py:369
  41.5 0.7 %collective-permute-start.9 = (f32[160,128]{1,0:T(8,128)S(1)}, f32[160,128]{1,0:T(8,128)S(1)}, u32[]{:S(2)}, u32[]{:S(2)}) collective-permute-start(f32[160,128]{1,0:T(8,128)S(1)} %x_upper.1.rest_7_), channel_id=1, source_target_pairs={{16,272},{17,273},{18,274},{19,275},{20,276},{21,277},{22,278},{23... | collective-permute-start | bytes 245768 | tf_op jit(solution)/shard_map/ppermute | solution.py:412
  42.2 1.2 %own.1 = f32[160,128]{1,0:T(8,128)S(1)} custom-call(s32[1,1]{1,0:T(1,128)S(6)} %copy.8.send_x, s32[1,1]{1,0:T(1,128)S(6)} %copy.9.send_y, s32[1,128]{1,0:T(1,128)S(1)} %get-tuple-element.18.numbers, f32[4,640,128]{2,1,0:T(8,128)S(1)} %bitcast.6, f32[24,24,128]{2,1,0:T(8,128)S(1)} %get-tuple-element.20.table, f32[4,24,128]{2,1,0:T(8,128)S(1)} %collective-permute-done.rest_0_, ...), custom_call_target="tpu_custom_call" | custom-call | tf_op jit(solution)/shard_map/own/pallas_call | solution.py:369
  43.4 5.2 %collective-permute-done.8.from_y1 = f32[168,128]{1,0:T(8,128)S(1)} collective-permute-done((f32[168,128]{1,0:T(8,128)S(1)}, f32[168,128]{1,0:T(8,128)S(1)}, u32[]{:S(2)}, u32[]{:S(2)}) %collective-permute-start.8) | collective-permute-done | bytes 86048 | tf_op jit(solution)/shard_map/ppermute | solution.py:412
  48.6 0.0 collective-permute-done.10.from_x1
  48.6 0.0 collective-permute-done.9.from_x0
  48.6 1.4 %place.1 = f32[5,3,4096]{2,1,0:T(4,128)} custom-call(s32[1,128]{1,0:T(1,128)S(1)} %get-tuple-element.18.numbers, f32[168,128]{1,0:T(8,128)S(1)} %collective-permute-done.4.rest_5_.from_y0, f32[168,128]{1,0:T(8,128)S(1)} %collective-permute-done.8.from_y1, f32[160,128]{1,0:T(8,128)S(1)} %collective-permute-done.9.from_x0, ...), custom_call_target="tpu_custom_call" | custom-call | tf_op jit(solution)/shard_map/place/pallas_call | solution.py:388
Async XLA Ops:
  2.5 7.1 %collective-permute-start = (f32[4,24,128]{2,1,0:T(8,128)S(1)}, f32[4,24,128]{2,1,0:T(8,128)S(1)}, u32[]{:S(2)}, u32[]{:S(2)}) collective-permute-start(f32[4,24,128]{2,1,0:T(8,128)S(1)} %get-tuple-element.21), channel_id=1, source_target_pairs={{0,31},{1,2},{2,1},{3,4},{4,3},{5,6},{6,5},{7,8},{8,7},{9,10},{10,... | collective-permute-start | bytes 147464 | tf_op jit(solution)/shard_map/ppermute | solution.py:412
  6.3 3.3 %collective-permute-start.1 = (f32[4,24,128]{2,1,0:T(8,128)S(1)}, f32[4,24,128]{2,1,0:T(8,128)S(1)}, u32[]{:S(2)}, u32[]{:S(2)}) collective-permute-start(f32[4,24,128]{2,1,0:T(8,128)S(1)} %get-tuple-element.22.rest_4_), channel_id=1, source_target_pairs={{16,496},{17,497},{18,498},{19,499},{20,500},{21,501},{22,502},{23... | collective-permute-start | bytes 147464 | tf_op jit(solution)/shard_map/ppermute | solution.py:412
  6.9 2.7 %collective-permute-start.2 = (f32[4,24,128]{2,1,0:T(8,128)S(1)}, f32[4,24,128]{2,1,0:T(8,128)S(1)}, u32[]{:S(2)}, u32[]{:S(2)}) collective-permute-start(f32[4,24,128]{2,1,0:T(8,128)S(1)} %get-tuple-element.23.rest_5_), channel_id=1, source_target_pairs={{16,48},{17,49},{18,50},{19,51},{20,52},{21,53},{22,54},{23,55},{2... | collective-permute-start | bytes 147464 | tf_op jit(solution)/shard_map/ppermute | solution.py:412
  7.6 2.0 %collective-permute-start.3 = (f32[4,24,128]{2,1,0:T(8,128)S(1)}, f32[4,24,128]{2,1,0:T(8,128)S(1)}, u32[]{:S(2)}, u32[]{:S(2)}) collective-permute-start(f32[4,24,128]{2,1,0:T(8,128)S(1)} %get-tuple-element.24.rest_6_), channel_id=1, source_target_pairs={{16,17},{17,16},{18,19},{19,18},{20,21},{21,20},{22,23},{23,22},{2... | collective-permute-start | bytes 147464 | tf_op jit(solution)/shard_map/ppermute | solution.py:412
  10.2 30.8 %collective-permute-start.4 = (f32[168,128]{1,0:T(8,128)S(1)}, f32[168,128]{1,0:T(8,128)S(1)}, u32[]{:S(2)}, u32[]{:S(2)}) collective-permute-start(f32[168,128]{1,0:T(8,128)S(1)} %get-tuple-element.25.rest_4_), channel_id=1, source_target_pairs={{16,0},{17,1},{18,2},{19,3},{20,4},{21,5},{22,6},{23,7},{24,8},{25... | collective-permute-start | bytes 258056 | tf_op jit(solution)/shard_map/ppermute | solution.py:412
  11.5 21.5 %collective-permute-start.5 = (f32[4,24,128]{2,1,0:T(8,128)S(1)}, f32[4,24,128]{2,1,0:T(8,128)S(1)}, u32[]{:S(2)}, u32[]{:S(2)}) collective-permute-start(f32[4,24,128]{2,1,0:T(8,128)S(1)} %get-tuple-element.26), channel_id=1, source_target_pairs={{0,480},{1,481},{2,482},{3,483},{4,484},{5,485},{6,486},{7,487},{8... | collective-permute-start | bytes 147464 | tf_op jit(solution)/shard_map/ppermute | solution.py:412
  15.0 18.0 %collective-permute-start.6 = (f32[4,24,128]{2,1,0:T(8,128)S(1)}, f32[4,24,128]{2,1,0:T(8,128)S(1)}, u32[]{:S(2)}, u32[]{:S(2)}) collective-permute-start(f32[4,24,128]{2,1,0:T(8,128)S(1)} %get-tuple-element.27), channel_id=1, source_target_pairs={{0,32},{1,33},{2,34},{3,35},{4,36},{5,37},{6,38},{7,39},{8,40},{9,... | collective-permute-start | bytes 147464 | tf_op jit(solution)/shard_map/ppermute | solution.py:412
  21.7 12.2 %collective-permute-start.7 = (f32[4,24,128]{2,1,0:T(8,128)S(1)}, f32[4,24,128]{2,1,0:T(8,128)S(1)}, u32[]{:S(2)}, u32[]{:S(2)}) collective-permute-start(f32[4,24,128]{2,1,0:T(8,128)S(1)} %get-tuple-element.28), channel_id=1, source_target_pairs={{0,1},{1,0},{2,3},{3,2},{4,5},{5,4},{6,7},{7,6},{8,9},{9,8},{10,11... | collective-permute-start | bytes 147464 | tf_op jit(solution)/shard_map/ppermute | solution.py:412
  36.7 12.0 %collective-permute-start.10 = (f32[176,128]{1,0:T(8,128)S(1)}, f32[176,128]{1,0:T(8,128)S(1)}, u32[]{:S(2)}, u32[]{:S(2)}) collective-permute-start(f32[176,128]{1,0:T(8,128)S(1)} %get-tuple-element.30), channel_id=1, source_target_pairs={{0,256},{1,257},{2,258},{3,259},{4,260},{5,261},{6,262},{7,263},{8... | collective-permute-start | bytes 270344 | tf_op jit(solution)/shard_map/ppermute | solution.py:412
  39.1 9.5 %collective-permute-start.8 = (f32[168,128]{1,0:T(8,128)S(1)}, f32[168,128]{1,0:T(8,128)S(1)}, u32[]{:S(2)}, u32[]{:S(2)}) collective-permute-start(f32[168,128]{1,0:T(8,128)S(1)} %get-tuple-element.29.rest_4_), channel_id=1, source_target_pairs={{0,16},{1,17},{2,18},{3,19},{4,20},{5,21},{6,22},{7,23},{8,24},{9,... | collective-permute-start | bytes 258056 | tf_op jit(solution)/shard_map/ppermute | solution.py:412
  41.5 7.1 %collective-permute-start.9 = (f32[160,128]{1,0:T(8,128)S(1)}, f32[160,128]{1,0:T(8,128)S(1)}, u32[]{:S(2)}, u32[]{:S(2)}) collective-permute-start(f32[160,128]{1,0:T(8,128)S(1)} %x_upper.1.rest_7_), channel_id=1, source_target_pairs={{16,272},{17,273},{18,274},{19,275},{20,276},{21,277},{22,278},{23... | collective-permute-start | bytes 245768 | tf_op jit(solution)/shard_map/ppermute | solution.py:412

commit v6 on v5

--- a/solution.py
+++ b/solution.py
@@ -141,15 +141,13 @@
             messages[m][k] = table[face_out[0, one_list, k]]
     codes = [layout[0, j] for j in range(3)]
     kept = functools.reduce(jnp.maximum, [jnp.where(c < 4, c, 0) for c in codes])
-    listed = {2: kept}
+    listed = {}
     listed.update({3 + j: codes[j] for j in range(3)})
     listed.update({8 + j: levels[j] for j in range(4)})
     listed.update({12 + s * 6 + f: ghost_src[0, s, f] for s in range(4) for f in range(6)})
-    lane = lanes((1, 128))
-    row = jnp.zeros((1, 128), jnp.int32)
-    for i, number in listed.items():
-        row = jnp.where(lane == i, number, row)
-    numbers[...] = row
+    for i in range(3, 40):
+        numbers[0, i] = listed.get(i, 0)
+    numbers[0, 2] = kept
 
 
 def limited(left, right):
@@ -345,13 +343,13 @@
     return pl.pallas_call(
         pack_kernel,
         out_shape=(
-            jax.ShapeDtypeStruct((1, 128), jnp.int32),
+            pltpu.SMEM((1, 40), jnp.int32),
             struct(4 * SWEEP_ROWS, 128),
             struct(24, FACE_ROWS, 128),
         )
         + (struct(4, FACE_ROWS, 128),) * 4,
         in_specs=[HBM] * (1 + len(small)),
-        out_specs=(VMEM,) * 7,
+        out_specs=(SMEM,) + (VMEM,) * 6,
         scratch_shapes=[
             pltpu.VMEM(cells.shape, jnp.float32),
             *[pltpu.SMEM(array.shape, jnp.int32) for array in small],
@@ -446,15 +444,14 @@
     ]
     upper_faces = [[r] for r in early]
     y_upper, *messages = update(
-        "y_upper", True, ((1, 8),), *common, upper_faces, handed=messages[1:]
+        "y_upper", True, ((1, 0),), *common, upper_faces, handed=messages[1:]
     )
     y_from_upper = exchange(y_upper, by_partner, lambda j, to_j: j >= half_y)
     late = [exchange(m, pairing, lower) for m, pairing in zip(messages, pairings[1:])]
     lower_faces = [[r] for r in (early[0], *late)]
-    x_lower, y_lower = update(
-        "lower", False, ((0, 16), (1, 8)), *common, lower_faces, after=(y_upper,)
-    )
+    (x_lower,) = update("x_lower", False, ((0, 8),), *common, lower_faces, after=(y_upper,))
     x_from_lower = exchange(x_lower, bx_partner, lower)
+    (y_lower,) = update("y_lower", False, ((1, 0),), *common, lower_faces, after=(x_lower,))
     y_from_lower = exchange(y_lower, by_partner, lambda j, to_j: j < half_y)
     (x_upper,) = update(
         "x_upper", True, ((0, 0),), *common, upper_faces, after=(y_lower, y_from_upper)

time: 50.4 us -> 47.5 us (0.942)
  the two profiles are of different devices: /device:TPU:33 before, /device:TPU:448 now
where the time goes in v6:
time: 47.5 us; the launch traced here: 47.2 us
  starting transfers between devices  26.4 us (56%)
  waiting for transfers between devices  13.9 us (29%)
  Pallas kernels  5.4 us (11%)
  between operations  1.48 us (3%)
    ppermute x11, starting transfers between devices, exchange(): return lax.ppermute(values, ('bx', 'by'), pairs)  26.4 us
    ppermute x11, waiting for transfers between devices, exchange(): return lax.ppermute(values, ('bx', 'by'), pairs)  13.9 us
    pallas_call x1, Pallas kernels, pack(): pl.pallas_call(pack_kernel, out_shape=(pltpu.SMEM((1, 40), jnp.int32), st...  2.49 us
    pallas_call x5, Pallas kernels, update(): pl.pallas_call(functools.partial(update_kernel, half, blocks, counts, len...  2.02 us
  transfers between devices with their start and end apart: 11, of which 2 were waited for; matrix products, arithmetic and copies ran while one was open for 0% of the time, Pallas kernels for 3%

profile of v6, /device:TPU:448, one launch (start us, length us, event | category | flops | bytes accessed | tf_op | source)
XLA Modules:
  0.0 47.2 jit_solution(11767165495565638877)
XLA Ops:
  0.0 2.5 %pack.1 = (s32[1,40]{1,0:T(1,128)S(4)}, f32[2560,128]{1,0:T(8,128)S(1)}, f32[24,24,128]{2,1,0:T(8,128)S(1)}, f32[4,24,128]{2,1,0:T(8,128)S(1)}, f32[4,24,128]{2,...) custom-call(f32[5,4,4096]{2,1,0:T(4,128)} %bitcast.8, s32[1,3]{1,0:T(1,128)} %layout_in.1, ...), custom_call_target="tpu_custom_call" | custom-call | tf_op jit(solution)/shard_map/pack/pallas_call | solution.py:343
  2.5 7.3 %collective-permute-start = (f32[4,24,128]{2,1,0:T(8,128)S(1)}, f32[4,24,128]{2,1,0:T(8,128)S(1)}, u32[]{:S(2)}, u32[]{:S(2)}) collective-permute-start(f32[4,24,128]{2,1,0:T(8,128)S(1)} %get-tuple-element.19), channel_id=1, source_target_pairs={{0,31},{1,2},{2,1},{3,4},{4,3},{5,6},{6,5},{7,8},{8,7},{9,10},{10,... | collective-permute-start | bytes 147464 | tf_op jit(solution)/shard_map/ppermute | solution.py:410
  9.9 2.9 %collective-permute-start.1 = (f32[4,24,128]{2,1,0:T(8,128)S(1)}, f32[4,24,128]{2,1,0:T(8,128)S(1)}, u32[]{:S(2)}, u32[]{:S(2)}) collective-permute-start(f32[4,24,128]{2,1,0:T(8,128)S(1)} %get-tuple-element.20.rest_4_), channel_id=1, source_target_pairs={{16,496},{17,497},{18,498},{19,499},{20,500},{21,501},{22,502},{23... | collective-permute-start | bytes 147464 | tf_op jit(solution)/shard_map/ppermute | solution.py:410
  12.8 4.7 %collective-permute-start.2 = (f32[4,24,128]{2,1,0:T(8,128)S(1)}, f32[4,24,128]{2,1,0:T(8,128)S(1)}, u32[]{:S(2)}, u32[]{:S(2)}) collective-permute-start(f32[4,24,128]{2,1,0:T(8,128)S(1)} %get-tuple-element.21.rest_5_), channel_id=1, source_target_pairs={{16,48},{17,49},{18,50},{19,51},{20,52},{21,53},{22,54},{23,55},{2... | collective-permute-start | bytes 147464 | tf_op jit(solution)/shard_map/ppermute | solution.py:410
  17.5 1.9 %collective-permute-start.3 = (f32[4,24,128]{2,1,0:T(8,128)S(1)}, f32[4,24,128]{2,1,0:T(8,128)S(1)}, u32[]{:S(2)}, u32[]{:S(2)}) collective-permute-start(f32[4,24,128]{2,1,0:T(8,128)S(1)} %get-tuple-element.22.rest_6_), channel_id=1, source_target_pairs={{16,17},{17,16},{18,19},{19,18},{20,21},{21,20},{22,23},{23,22},{2... | collective-permute-start | bytes 147464 | tf_op jit(solution)/shard_map/ppermute | solution.py:410
  20.7 0.0 collective-permute-done.rest_0_
  20.8 0.0 collective-permute-done.1.rest_1_
  20.8 0.0 collective-permute-done.2.rest_2_.rest_3_
  20.8 0.0 collective-permute-done.3.rest_3_.rest_5_
  20.8 0.7 %y_upper.1 = (f32[160,128]{1,0:T(8,128)S(1)}, f32[4,24,128]{2,1,0:T(8,128)S(1)}, f32[4,24,128]{2,1,0:T(8,128)S(1)}, f32[4,24,128]{2,1,0:T(8,128)S(1)}) custom-call(s32[1,1]{1,0:T(1,128)S(6)} %copy.8.send_x, s32[1,1]{1,0:T(1,128)S(6)} %copy.9.send_y, s32[1,40]{1,0:T(1,128)S(4)} %get-tuple-element.16.numbers, f32[4,640,128]{2,1,0:T(8,128)S(1)} %bitcast.3, ...), custom_call_target="tpu_custom_call" | custom-call | tf_op jit(solution)/shard_map/y_upper/pallas_call | solution.py:367
  21.5 1.3 %collective-permute-start.4 = (f32[160,128]{1,0:T(8,128)S(1)}, f32[160,128]{1,0:T(8,128)S(1)}, u32[]{:S(2)}, u32[]{:S(2)}) collective-permute-start(f32[160,128]{1,0:T(8,128)S(1)} %get-tuple-element.23.rest_4_), channel_id=1, source_target_pairs={{16,0},{17,1},{18,2},{19,3},{20,4},{21,5},{22,6},{23,7},{24,8},{25... | collective-permute-start | bytes 245768 | tf_op jit(solution)/shard_map/ppermute | solution.py:410
  22.8 0.7 %collective-permute-start.5 = (f32[4,24,128]{2,1,0:T(8,128)S(1)}, f32[4,24,128]{2,1,0:T(8,128)S(1)}, u32[]{:S(2)}, u32[]{:S(2)}) collective-permute-start(f32[4,24,128]{2,1,0:T(8,128)S(1)} %get-tuple-element.24), channel_id=1, source_target_pairs={{0,480},{1,481},{2,482},{3,483},{4,484},{5,485},{6,486},{7,487},{8... | collective-permute-start | bytes 147464 | tf_op jit(solution)/shard_map/ppermute | solution.py:410
  23.4 0.7 %collective-permute-start.6 = (f32[4,24,128]{2,1,0:T(8,128)S(1)}, f32[4,24,128]{2,1,0:T(8,128)S(1)}, u32[]{:S(2)}, u32[]{:S(2)}) collective-permute-start(f32[4,24,128]{2,1,0:T(8,128)S(1)} %get-tuple-element.25), channel_id=1, source_target_pairs={{0,32},{1,33},{2,34},{3,35},{4,36},{5,37},{6,38},{7,39},{8,40},{9,... | collective-permute-start | bytes 147464 | tf_op jit(solution)/shard_map/ppermute | solution.py:410
  24.1 0.7 %collective-permute-start.7 = (f32[4,24,128]{2,1,0:T(8,128)S(1)}, f32[4,24,128]{2,1,0:T(8,128)S(1)}, u32[]{:S(2)}, u32[]{:S(2)}) collective-permute-start(f32[4,24,128]{2,1,0:T(8,128)S(1)} %get-tuple-element.26), channel_id=1, source_target_pairs={{0,1},{1,0},{2,3},{3,2},{4,5},{5,4},{6,7},{7,6},{8,9},{9,8},{10,11... | collective-permute-start | bytes 147464 | tf_op jit(solution)/shard_map/ppermute | solution.py:410
  24.8 0.0 collective-permute-done.5.rest_1_.rest_2_
  24.8 0.0 collective-permute-done.6.rest_2_.rest_4_
  24.8 0.0 collective-permute-done.7.rest_3_.rest_6_
  24.8 0.7 %collective-permute-start.10 = (f32[168,128]{1,0:T(8,128)S(1)}, f32[168,128]{1,0:T(8,128)S(1)}, u32[]{:S(2)}, u32[]{:S(2)}) collective-permute-start(f32[168,128]{1,0:T(8,128)S(1)} %x_lower.1.rest_4_), channel_id=1, source_target_pairs={{0,256},{1,257},{2,258},{3,259},{4,260},{5,261},{6,262},{7,263},{8... | collective-permute-start | bytes 258056 | tf_op jit(solution)/shard_map/ppermute | solution.py:410
  25.5 1.3 %collective-permute-start.8 = (f32[160,128]{1,0:T(8,128)S(1)}, f32[160,128]{1,0:T(8,128)S(1)}, u32[]{:S(2)}, u32[]{:S(2)}) collective-permute-start(f32[160,128]{1,0:T(8,128)S(1)} %y_lower.1.rest_4_), channel_id=1, source_target_pairs={{0,16},{1,17},{2,18},{3,19},{4,20},{5,21},{6,22},{7,23},{8,24},{9,... | collective-permute-start | bytes 245768 | tf_op jit(solution)/shard_map/ppermute | solution.py:410
  26.8 2.7 %collective-permute-done.4.rest_5_.from_y0 = f32[160,128]{1,0:T(8,128)S(1)} collective-permute-done((f32[160,128]{1,0:T(8,128)S(1)}, f32[160,128]{1,0:T(8,128)S(1)}, u32[]{:S(2)}, u32[]{:S(2)}) %collective-permute-start.4) | collective-permute-done | bytes 81952 | tf_op jit(solution)/shard_map/ppermute | solution.py:410
  29.6 0.6 %x_upper.1.rest_7_ = f32[160,128]{1,0:T(8,128)S(1)} custom-call(s32[1,1]{1,0:T(1,128)S(6)} %copy.8.send_x, s32[1,1]{1,0:T(1,128)S(6)} %copy.9.send_y, s32[1,40]{1,0:T(1,128)S(4)} %get-tuple-element.16.numbers, f32[4,640,128]{2,1,0:T(8,128)S(1)} %bitcast.6, f32[24,24,128]{2,1,0:T(8,128)S(1)} %get-tuple-element.18.table, ...), custom_call_target="tpu_custom_call" | custom-call | tf_op jit(solution)/shard_map/x_upper/pallas_call | solution.py:367
  30.2 4.2 %collective-permute-start.9 = (f32[160,128]{1,0:T(8,128)S(1)}, f32[160,128]{1,0:T(8,128)S(1)}, u32[]{:S(2)}, u32[]{:S(2)}) collective-permute-start(f32[160,128]{1,0:T(8,128)S(1)} %x_upper.1.rest_7_), channel_id=1, source_target_pairs={{16,272},{17,273},{18,274},{19,275},{20,276},{21,277},{22,278},{23... | collective-permute-start | bytes 245768 | tf_op jit(solution)/shard_map/ppermute | solution.py:410
  34.5 0.7 %own.1 = f32[160,128]{1,0:T(8,128)S(1)} custom-call(s32[1,1]{1,0:T(1,128)S(6)} %copy.8.send_x, s32[1,1]{1,0:T(1,128)S(6)} %copy.9.send_y, s32[1,40]{1,0:T(1,128)S(4)} %get-tuple-element.16.numbers, f32[4,640,128]{2,1,0:T(8,128)S(1)} %bitcast.7, f32[24,24,128]{2,1,0:T(8,128)S(1)} %get-tuple-element.18.table, f32[4,24,128]{2,1,0:T(8,128)S(1)} %collective-permute-done.rest_0_, ...), custom_call_target="tpu_custom_call" | custom-call | tf_op jit(solution)/shard_map/own/pallas_call | solution.py:367
  35.1 11.1 %collective-permute-done.8.from_y1 = f32[160,128]{1,0:T(8,128)S(1)} collective-permute-done((f32[160,128]{1,0:T(8,128)S(1)}, f32[160,128]{1,0:T(8,128)S(1)}, u32[]{:S(2)}, u32[]{:S(2)}) %collective-permute-start.8) | collective-permute-done | bytes 81952 | tf_op jit(solution)/shard_map/ppermute | solution.py:410
  46.2 0.0 collective-permute-done.10.from_x1
  46.3 0.0 collective-permute-done.9.from_x0
  46.3 0.9 %place.1 = f32[5,3,4096]{2,1,0:T(4,128)} custom-call(s32[1,40]{1,0:T(1,128)S(4)} %get-tuple-element.16.numbers, f32[160,128]{1,0:T(8,128)S(1)} %collective-permute-done.4.rest_5_.from_y0, f32[160,128]{1,0:T(8,128)S(1)} %collective-permute-done.8.from_y1, f32[160,128]{1,0:T(8,128)S(1)} %collective-permute-done.9.from_x0, ...), custom_call_target="tpu_custom_call" | custom-call | tf_op jit(solution)/shard_map/place/pallas_call | solution.py:386
  (2 shorter events, 0.0 us)
Async XLA Ops:
  2.5 18.3 %collective-permute-start = (f32[4,24,128]{2,1,0:T(8,128)S(1)}, f32[4,24,128]{2,1,0:T(8,128)S(1)}, u32[]{:S(2)}, u32[]{:S(2)}) collective-permute-start(f32[4,24,128]{2,1,0:T(8,128)S(1)} %get-tuple-element.19), channel_id=1, source_target_pairs={{0,31},{1,2},{2,1},{3,4},{4,3},{5,6},{6,5},{7,8},{8,7},{9,10},{10,... | collective-permute-start | bytes 147464 | tf_op jit(solution)/shard_map/ppermute | solution.py:410
  9.9 10.9 %collective-permute-start.1 = (f32[4,24,128]{2,1,0:T(8,128)S(1)}, f32[4,24,128]{2,1,0:T(8,128)S(1)}, u32[]{:S(2)}, u32[]{:S(2)}) collective-permute-start(f32[4,24,128]{2,1,0:T(8,128)S(1)} %get-tuple-element.20.rest_4_), channel_id=1, source_target_pairs={{16,496},{17,497},{18,498},{19,499},{20,500},{21,501},{22,502},{23... | collective-permute-start | bytes 147464 | tf_op jit(solution)/shard_map/ppermute | solution.py:410
  12.8 8.0 %collective-permute-start.2 = (f32[4,24,128]{2,1,0:T(8,128)S(1)}, f32[4,24,128]{2,1,0:T(8,128)S(1)}, u32[]{:S(2)}, u32[]{:S(2)}) collective-permute-start(f32[4,24,128]{2,1,0:T(8,128)S(1)} %get-tuple-element.21.rest_5_), channel_id=1, source_target_pairs={{16,48},{17,49},{18,50},{19,51},{20,52},{21,53},{22,54},{23,55},{2... | collective-permute-start | bytes 147464 | tf_op jit(solution)/shard_map/ppermute | solution.py:410
  17.5 3.3 %collective-permute-start.3 = (f32[4,24,128]{2,1,0:T(8,128)S(1)}, f32[4,24,128]{2,1,0:T(8,128)S(1)}, u32[]{:S(2)}, u32[]{:S(2)}) collective-permute-start(f32[4,24,128]{2,1,0:T(8,128)S(1)} %get-tuple-element.22.rest_6_), channel_id=1, source_target_pairs={{16,17},{17,16},{18,19},{19,18},{20,21},{21,20},{22,23},{23,22},{2... | collective-permute-start | bytes 147464 | tf_op jit(solution)/shard_map/ppermute | solution.py:410
  21.5 8.1 %collective-permute-start.4 = (f32[160,128]{1,0:T(8,128)S(1)}, f32[160,128]{1,0:T(8,128)S(1)}, u32[]{:S(2)}, u32[]{:S(2)}) collective-permute-start(f32[160,128]{1,0:T(8,128)S(1)} %get-tuple-element.23.rest_4_), channel_id=1, source_target_pairs={{16,0},{17,1},{18,2},{19,3},{20,4},{21,5},{22,6},{23,7},{24,8},{25... | collective-permute-start | bytes 245768 | tf_op jit(solution)/shard_map/ppermute | solution.py:410
  22.8 2.0 %collective-permute-start.5 = (f32[4,24,128]{2,1,0:T(8,128)S(1)}, f32[4,24,128]{2,1,0:T(8,128)S(1)}, u32[]{:S(2)}, u32[]{:S(2)}) collective-permute-start(f32[4,24,128]{2,1,0:T(8,128)S(1)} %get-tuple-element.24), channel_id=1, source_target_pairs={{0,480},{1,481},{2,482},{3,483},{4,484},{5,485},{6,486},{7,487},{8... | collective-permute-start | bytes 147464 | tf_op jit(solution)/shard_map/ppermute | solution.py:410
  23.4 1.4 %collective-permute-start.6 = (f32[4,24,128]{2,1,0:T(8,128)S(1)}, f32[4,24,128]{2,1,0:T(8,128)S(1)}, u32[]{:S(2)}, u32[]{:S(2)}) collective-permute-start(f32[4,24,128]{2,1,0:T(8,128)S(1)} %get-tuple-element.25), channel_id=1, source_target_pairs={{0,32},{1,33},{2,34},{3,35},{4,36},{5,37},{6,38},{7,39},{8,40},{9,... | collective-permute-start | bytes 147464 | tf_op jit(solution)/shard_map/ppermute | solution.py:410
  24.1 0.7 %collective-permute-start.7 = (f32[4,24,128]{2,1,0:T(8,128)S(1)}, f32[4,24,128]{2,1,0:T(8,128)S(1)}, u32[]{:S(2)}, u32[]{:S(2)}) collective-permute-start(f32[4,24,128]{2,1,0:T(8,128)S(1)} %get-tuple-element.26), channel_id=1, source_target_pairs={{0,1},{1,0},{2,3},{3,2},{4,5},{5,4},{6,7},{7,6},{8,9},{9,8},{10,11... | collective-permute-start | bytes 147464 | tf_op jit(solution)/shard_map/ppermute | solution.py:410
  24.8 21.4 %collective-permute-start.10 = (f32[168,128]{1,0:T(8,128)S(1)}, f32[168,128]{1,0:T(8,128)S(1)}, u32[]{:S(2)}, u32[]{:S(2)}) collective-permute-start(f32[168,128]{1,0:T(8,128)S(1)} %x_lower.1.rest_4_), channel_id=1, source_target_pairs={{0,256},{1,257},{2,258},{3,259},{4,260},{5,261},{6,262},{7,263},{8... | collective-permute-start | bytes 258056 | tf_op jit(solution)/shard_map/ppermute | solution.py:410
  25.5 20.7 %collective-permute-start.8 = (f32[160,128]{1,0:T(8,128)S(1)}, f32[160,128]{1,0:T(8,128)S(1)}, u32[]{:S(2)}, u32[]{:S(2)}) collective-permute-start(f32[160,128]{1,0:T(8,128)S(1)} %y_lower.1.rest_4_), channel_id=1, source_target_pairs={{0,16},{1,17},{2,18},{3,19},{4,20},{5,21},{6,22},{7,23},{8,24},{9,... | collective-permute-start | bytes 245768 | tf_op jit(solution)/shard_map/ppermute | solution.py:410
  30.2 16.1 %collective-permute-start.9 = (f32[160,128]{1,0:T(8,128)S(1)}, f32[160,128]{1,0:T(8,128)S(1)}, u32[]{:S(2)}, u32[]{:S(2)}) collective-permute-start(f32[160,128]{1,0:T(8,128)S(1)} %x_upper.1.rest_7_), channel_id=1, source_target_pairs={{16,272},{17,273},{18,274},{19,275},{20,276},{21,277},{22,278},{23... | collective-permute-start | bytes 245768 | tf_op jit(solution)/shard_map/ppermute | solution.py:410

commit v7 on v6

--- a/solution.py
+++ b/solution.py
@@ -50,23 +50,19 @@
         self.back_half = ((row - group) % 8) * 16 + (inner + 8) % 16
         source_group = (group + row) % 8
         self.skew_z = (inner % 8) * 16 + (inner // 8) * 8 + source_group
+        self.skew_z_half = (inner % 8) * 16 + (1 - inner // 8) * 8 + source_group
         z_low, z_high = inner % 8, inner // 8
         self.back_z = ((row - z_low) % 8) * 16 + z_high * 8 + group
+        self.back_z_half = ((row - z_low) % 8) * 16 + (1 - z_high) * 8 + group
 
     def turn(self, v):
         return take(take(take(v, self.skew, 1), self.shift, 0), self.back, 1)
 
-    def to_z(self, v0, v1):
-        t0 = take(take(v0, self.skew_z, 1), self.shift, 0)
-        t1 = take(take(v1, self.skew_z, 1), self.shift, 0)
-        first = jnp.where(self.low, take(t0, self.back, 1), take(t1, self.back_half, 1))
-        second = jnp.where(self.low, take(t0, self.back_half, 1), take(t1, self.back, 1))
-        return first, second
-
     def from_z(self, first, second):
-        t0 = jnp.where(self.low, take(first, self.skew, 1), take(second, self.skew_half, 1))
-        t1 = jnp.where(self.low, take(first, self.skew_half, 1), take(second, self.skew, 1))
-        return tuple(take(take(t, self.shift, 0), self.back_z, 1) for t in (t0, t1))
+        a, b = take(first, self.skew, 1), take(second, self.skew_half, 1)
+        t0 = take(jnp.where(self.low, a, b), self.shift, 0)
+        t1 = take(jnp.where(self.low, b, a), self.shift, 0)
+        return take(t0, self.back_z, 1), take(t1, self.back_z_half, 1)
 
 
 def parities():
@@ -106,18 +102,27 @@
             sweep[pl.ds(row, 4, stride=SWEEP_ROWS), :] = cells[
                 field, :, t * 128 : (t + 1) * 128
             ]
-        for first in range(0, 4 * SWEEP_ROWS, SWEEP_ROWS):
-            for xh in range(2):
-                v = [
-                    sweep[pl.ds(first + base + HALF * xh * 8 + h, 8, stride=8), :]
-                    for h in range(2)
-                ]
-                for h in range(2):
-                    start = first + to_y + HALF * h * 8 + 2 + xh
-                    sweep[pl.ds(start, 8, stride=8), :] = turns.turn(v[h])
-                for zh, value in enumerate(turns.to_z(v[0], v[1])):
-                    start = first + to_z + HALF * zh * 8 + 4 + xh
-                    sweep[pl.ds(start, 8, stride=8), :] = value
+        places = [(s * SWEEP_ROWS, xh) for s in range(4) for xh in range(2)]
+        v = [
+            sweep[pl.ds(first + base + HALF * xh * 8 + h, 8, stride=8), :]
+            for first, xh in places
+            for h in range(2)
+        ]
+        y = [take(a, turns.skew, 1) for a in v]
+        z = [take(a, (turns.skew_z, turns.skew_z_half)[k % 2], 1) for k, a in enumerate(v)]
+        y = [take(a, turns.shift, 0) for a in y]
+        z = [take(a, turns.shift, 0) for a in z]
+        y = [take(a, turns.back, 1) for a in y]
+        pairs = list(zip(z[::2], z[1::2]))
+        ones = [take(jnp.where(turns.low, a, b), turns.back, 1) for a, b in pairs]
+        twos = [take(jnp.where(turns.low, b, a), turns.back_half, 1) for a, b in pairs]
+        for k, (first, xh) in enumerate(places):
+            for h in range(2):
+                start = first + to_y + HALF * h * 8 + 2 + xh
+                sweep[pl.ds(start, 8, stride=8), :] = y[2 * k + h]
+            for zh, value in enumerate((ones[k], twos[k])):
+                start = first + to_z + HALF * zh * 8 + 4 + xh
+                sweep[pl.ds(start, 8, stride=8), :] = value
     for s in range(4):
         for face in range(6):
             direction, high = face // 2, face % 2

time: 47.5 us -> 47.3 us (level)
  no operation moved by 1% of the time
where the time goes in v7:
time: 47.3 us; the launch traced here: 47 us
  starting transfers between devices  26.4 us (56%)
  waiting for transfers between devices  13.9 us (29%)
  Pallas kernels  5.2 us (11%)
  between operations  1.47 us (3%)
    ppermute x11, starting transfers between devices, exchange(): return lax.ppermute(values, ('bx', 'by'), pairs)  26.4 us
    ppermute x11, waiting for transfers between devices, exchange(): return lax.ppermute(values, ('bx', 'by'), pairs)  13.9 us
    pallas_call x1, Pallas kernels, pack(): pl.pallas_call(pack_kernel, out_shape=(pltpu.SMEM((1, 40), jnp.int32), st...  2.32 us
    pallas_call x5, Pallas kernels, update(): pl.pallas_call(functools.partial(update_kernel, half, blocks, counts, len...  1.98 us
  transfers between devices with their start and end apart: 11, of which 2 were waited for; matrix products, arithmetic and copies ran while one was open for 0% of the time, Pallas kernels for 3%

profile of v7, /device:TPU:448, one launch (start us, length us, event | category | flops | bytes accessed | tf_op | source)
XLA Modules:
  0.0 47.0 jit_solution(10296207486830752125)
XLA Ops:
  0.0 2.3 %pack.1 = (s32[1,40]{1,0:T(1,128)S(4)}, f32[2560,128]{1,0:T(8,128)S(1)}, f32[24,24,128]{2,1,0:T(8,128)S(1)}, f32[4,24,128]{2,1,0:T(8,128)S(1)}, f32[4,24,128]{2,...) custom-call(f32[5,4,4096]{2,1,0:T(4,128)} %bitcast.8, s32[1,3]{1,0:T(1,128)} %layout_in.1, ...), custom_call_target="tpu_custom_call" | custom-call | tf_op jit(solution)/shard_map/pack/pallas_call | solution.py:348
  2.3 7.3 %collective-permute-start = (f32[4,24,128]{2,1,0:T(8,128)S(1)}, f32[4,24,128]{2,1,0:T(8,128)S(1)}, u32[]{:S(2)}, u32[]{:S(2)}) collective-permute-start(f32[4,24,128]{2,1,0:T(8,128)S(1)} %get-tuple-element.19), channel_id=1, source_target_pairs={{0,31},{1,2},{2,1},{3,4},{4,3},{5,6},{6,5},{7,8},{8,7},{9,10},{10,... | collective-permute-start | bytes 147464 | tf_op jit(solution)/shard_map/ppermute | solution.py:415
  9.7 2.9 %collective-permute-start.1 = (f32[4,24,128]{2,1,0:T(8,128)S(1)}, f32[4,24,128]{2,1,0:T(8,128)S(1)}, u32[]{:S(2)}, u32[]{:S(2)}) collective-permute-start(f32[4,24,128]{2,1,0:T(8,128)S(1)} %get-tuple-element.20.rest_4_), channel_id=1, source_target_pairs={{16,496},{17,497},{18,498},{19,499},{20,500},{21,501},{22,502},{23... | collective-permute-start | bytes 147464 | tf_op jit(solution)/shard_map/ppermute | solution.py:415
  12.6 4.7 %collective-permute-start.2 = (f32[4,24,128]{2,1,0:T(8,128)S(1)}, f32[4,24,128]{2,1,0:T(8,128)S(1)}, u32[]{:S(2)}, u32[]{:S(2)}) collective-permute-start(f32[4,24,128]{2,1,0:T(8,128)S(1)} %get-tuple-element.21.rest_5_), channel_id=1, source_target_pairs={{16,48},{17,49},{18,50},{19,51},{20,52},{21,53},{22,54},{23,55},{2... | collective-permute-start | bytes 147464 | tf_op jit(solution)/shard_map/ppermute | solution.py:415
  17.4 1.9 %collective-permute-start.3 = (f32[4,24,128]{2,1,0:T(8,128)S(1)}, f32[4,24,128]{2,1,0:T(8,128)S(1)}, u32[]{:S(2)}, u32[]{:S(2)}) collective-permute-start(f32[4,24,128]{2,1,0:T(8,128)S(1)} %get-tuple-element.22.rest_6_), channel_id=1, source_target_pairs={{16,17},{17,16},{18,19},{19,18},{20,21},{21,20},{22,23},{23,22},{2... | collective-permute-start | bytes 147464 | tf_op jit(solution)/shard_map/ppermute | solution.py:415
  20.6 0.0 collective-permute-done.rest_0_
  20.6 0.0 collective-permute-done.1.rest_1_
  20.6 0.0 collective-permute-done.2.rest_2_.rest_3_
  20.6 0.0 collective-permute-done.3.rest_3_.rest_5_
  20.6 0.7 %y_upper.1 = (f32[160,128]{1,0:T(8,128)S(1)}, f32[4,24,128]{2,1,0:T(8,128)S(1)}, f32[4,24,128]{2,1,0:T(8,128)S(1)}, f32[4,24,128]{2,1,0:T(8,128)S(1)}) custom-call(s32[1,1]{1,0:T(1,128)S(6)} %copy.8.send_x, s32[1,1]{1,0:T(1,128)S(6)} %copy.9.send_y, s32[1,40]{1,0:T(1,128)S(4)} %get-tuple-element.16.numbers, f32[4,640,128]{2,1,0:T(8,128)S(1)} %bitcast.3, ...), custom_call_target="tpu_custom_call" | custom-call | tf_op jit(solution)/shard_map/y_upper/pallas_call | solution.py:372
  21.3 1.3 %collective-permute-start.4 = (f32[160,128]{1,0:T(8,128)S(1)}, f32[160,128]{1,0:T(8,128)S(1)}, u32[]{:S(2)}, u32[]{:S(2)}) collective-permute-start(f32[160,128]{1,0:T(8,128)S(1)} %get-tuple-element.23.rest_4_), channel_id=1, source_target_pairs={{16,0},{17,1},{18,2},{19,3},{20,4},{21,5},{22,6},{23,7},{24,8},{25... | collective-permute-start | bytes 245768 | tf_op jit(solution)/shard_map/ppermute | solution.py:415
  22.6 0.7 %collective-permute-start.5 = (f32[4,24,128]{2,1,0:T(8,128)S(1)}, f32[4,24,128]{2,1,0:T(8,128)S(1)}, u32[]{:S(2)}, u32[]{:S(2)}) collective-permute-start(f32[4,24,128]{2,1,0:T(8,128)S(1)} %get-tuple-element.24), channel_id=1, source_target_pairs={{0,480},{1,481},{2,482},{3,483},{4,484},{5,485},{6,486},{7,487},{8... | collective-permute-start | bytes 147464 | tf_op jit(solution)/shard_map/ppermute | solution.py:415
  23.3 0.7 %collective-permute-start.6 = (f32[4,24,128]{2,1,0:T(8,128)S(1)}, f32[4,24,128]{2,1,0:T(8,128)S(1)}, u32[]{:S(2)}, u32[]{:S(2)}) collective-permute-start(f32[4,24,128]{2,1,0:T(8,128)S(1)} %get-tuple-element.25), channel_id=1, source_target_pairs={{0,32},{1,33},{2,34},{3,35},{4,36},{5,37},{6,38},{7,39},{8,40},{9,... | collective-permute-start | bytes 147464 | tf_op jit(solution)/shard_map/ppermute | solution.py:415
  23.9 0.7 %collective-permute-start.7 = (f32[4,24,128]{2,1,0:T(8,128)S(1)}, f32[4,24,128]{2,1,0:T(8,128)S(1)}, u32[]{:S(2)}, u32[]{:S(2)}) collective-permute-start(f32[4,24,128]{2,1,0:T(8,128)S(1)} %get-tuple-element.26), channel_id=1, source_target_pairs={{0,1},{1,0},{2,3},{3,2},{4,5},{5,4},{6,7},{7,6},{8,9},{9,8},{10,11... | collective-permute-start | bytes 147464 | tf_op jit(solution)/shard_map/ppermute | solution.py:415
  24.6 0.0 collective-permute-done.5.rest_1_.rest_2_
  24.6 0.0 collective-permute-done.6.rest_2_.rest_4_
  24.6 0.0 collective-permute-done.7.rest_3_.rest_6_
  24.7 0.7 %collective-permute-start.10 = (f32[168,128]{1,0:T(8,128)S(1)}, f32[168,128]{1,0:T(8,128)S(1)}, u32[]{:S(2)}, u32[]{:S(2)}) collective-permute-start(f32[168,128]{1,0:T(8,128)S(1)} %x_lower.1.rest_4_), channel_id=1, source_target_pairs={{0,256},{1,257},{2,258},{3,259},{4,260},{5,261},{6,262},{7,263},{8... | collective-permute-start | bytes 258056 | tf_op jit(solution)/shard_map/ppermute | solution.py:415
  25.3 1.3 %collective-permute-start.8 = (f32[160,128]{1,0:T(8,128)S(1)}, f32[160,128]{1,0:T(8,128)S(1)}, u32[]{:S(2)}, u32[]{:S(2)}) collective-permute-start(f32[160,128]{1,0:T(8,128)S(1)} %y_lower.1.rest_4_), channel_id=1, source_target_pairs={{0,16},{1,17},{2,18},{3,19},{4,20},{5,21},{6,22},{7,23},{8,24},{9,... | collective-permute-start | bytes 245768 | tf_op jit(solution)/shard_map/ppermute | solution.py:415
  26.6 2.7 %collective-permute-done.4.rest_5_.from_y0 = f32[160,128]{1,0:T(8,128)S(1)} collective-permute-done((f32[160,128]{1,0:T(8,128)S(1)}, f32[160,128]{1,0:T(8,128)S(1)}, u32[]{:S(2)}, u32[]{:S(2)}) %collective-permute-start.4) | collective-permute-done | bytes 81952 | tf_op jit(solution)/shard_map/ppermute | solution.py:415
  29.4 0.6 %x_upper.1.rest_7_ = f32[160,128]{1,0:T(8,128)S(1)} custom-call(s32[1,1]{1,0:T(1,128)S(6)} %copy.8.send_x, s32[1,1]{1,0:T(1,128)S(6)} %copy.9.send_y, s32[1,40]{1,0:T(1,128)S(4)} %get-tuple-element.16.numbers, f32[4,640,128]{2,1,0:T(8,128)S(1)} %bitcast.6, f32[24,24,128]{2,1,0:T(8,128)S(1)} %get-tuple-element.18.table, ...), custom_call_target="tpu_custom_call" | custom-call | tf_op jit(solution)/shard_map/x_upper/pallas_call | solution.py:372
  30.0 4.2 %collective-permute-start.9 = (f32[160,128]{1,0:T(8,128)S(1)}, f32[160,128]{1,0:T(8,128)S(1)}, u32[]{:S(2)}, u32[]{:S(2)}) collective-permute-start(f32[160,128]{1,0:T(8,128)S(1)} %x_upper.1.rest_7_), channel_id=1, source_target_pairs={{16,272},{17,273},{18,274},{19,275},{20,276},{21,277},{22,278},{23... | collective-permute-start | bytes 245768 | tf_op jit(solution)/shard_map/ppermute | solution.py:415
  34.3 0.7 %own.1 = f32[160,128]{1,0:T(8,128)S(1)} custom-call(s32[1,1]{1,0:T(1,128)S(6)} %copy.8.send_x, s32[1,1]{1,0:T(1,128)S(6)} %copy.9.send_y, s32[1,40]{1,0:T(1,128)S(4)} %get-tuple-element.16.numbers, f32[4,640,128]{2,1,0:T(8,128)S(1)} %bitcast.7, f32[24,24,128]{2,1,0:T(8,128)S(1)} %get-tuple-element.18.table, f32[4,24,128]{2,1,0:T(8,128)S(1)} %collective-permute-done.rest_0_, ...), custom_call_target="tpu_custom_call" | custom-call | tf_op jit(solution)/shard_map/own/pallas_call | solution.py:372
  34.9 11.1 %collective-permute-done.8.from_y1 = f32[160,128]{1,0:T(8,128)S(1)} collective-permute-done((f32[160,128]{1,0:T(8,128)S(1)}, f32[160,128]{1,0:T(8,128)S(1)}, u32[]{:S(2)}, u32[]{:S(2)}) %collective-permute-start.8) | collective-permute-done | bytes 81952 | tf_op jit(solution)/shard_map/ppermute | solution.py:415
  46.1 0.0 collective-permute-done.10.from_x1
  46.1 0.0 collective-permute-done.9.from_x0
  46.1 0.9 %place.1 = f32[5,3,4096]{2,1,0:T(4,128)} custom-call(s32[1,40]{1,0:T(1,128)S(4)} %get-tuple-element.16.numbers, f32[160,128]{1,0:T(8,128)S(1)} %collective-permute-done.4.rest_5_.from_y0, f32[160,128]{1,0:T(8,128)S(1)} %collective-permute-done.8.from_y1, f32[160,128]{1,0:T(8,128)S(1)} %collective-permute-done.9.from_x0, ...), custom_call_target="tpu_custom_call" | custom-call | tf_op jit(solution)/shard_map/place/pallas_call | solution.py:391
  (2 shorter events, 0.0 us)
Async XLA Ops:
  2.3 18.3 %collective-permute-start = (f32[4,24,128]{2,1,0:T(8,128)S(1)}, f32[4,24,128]{2,1,0:T(8,128)S(1)}, u32[]{:S(2)}, u32[]{:S(2)}) collective-permute-start(f32[4,24,128]{2,1,0:T(8,128)S(1)} %get-tuple-element.19), channel_id=1, source_target_pairs={{0,31},{1,2},{2,1},{3,4},{4,3},{5,6},{6,5},{7,8},{8,7},{9,10},{10,... | collective-permute-start | bytes 147464 | tf_op jit(solution)/shard_map/ppermute | solution.py:415
  9.7 10.9 %collective-permute-start.1 = (f32[4,24,128]{2,1,0:T(8,128)S(1)}, f32[4,24,128]{2,1,0:T(8,128)S(1)}, u32[]{:S(2)}, u32[]{:S(2)}) collective-permute-start(f32[4,24,128]{2,1,0:T(8,128)S(1)} %get-tuple-element.20.rest_4_), channel_id=1, source_target_pairs={{16,496},{17,497},{18,498},{19,499},{20,500},{21,501},{22,502},{23... | collective-permute-start | bytes 147464 | tf_op jit(solution)/shard_map/ppermute | solution.py:415
  12.6 8.0 %collective-permute-start.2 = (f32[4,24,128]{2,1,0:T(8,128)S(1)}, f32[4,24,128]{2,1,0:T(8,128)S(1)}, u32[]{:S(2)}, u32[]{:S(2)}) collective-permute-start(f32[4,24,128]{2,1,0:T(8,128)S(1)} %get-tuple-element.21.rest_5_), channel_id=1, source_target_pairs={{16,48},{17,49},{18,50},{19,51},{20,52},{21,53},{22,54},{23,55},{2... | collective-permute-start | bytes 147464 | tf_op jit(solution)/shard_map/ppermute | solution.py:415
  17.4 3.3 %collective-permute-start.3 = (f32[4,24,128]{2,1,0:T(8,128)S(1)}, f32[4,24,128]{2,1,0:T(8,128)S(1)}, u32[]{:S(2)}, u32[]{:S(2)}) collective-permute-start(f32[4,24,128]{2,1,0:T(8,128)S(1)} %get-tuple-element.22.rest_6_), channel_id=1, source_target_pairs={{16,17},{17,16},{18,19},{19,18},{20,21},{21,20},{22,23},{23,22},{2... | collective-permute-start | bytes 147464 | tf_op jit(solution)/shard_map/ppermute | solution.py:415
  21.3 8.1 %collective-permute-start.4 = (f32[160,128]{1,0:T(8,128)S(1)}, f32[160,128]{1,0:T(8,128)S(1)}, u32[]{:S(2)}, u32[]{:S(2)}) collective-permute-start(f32[160,128]{1,0:T(8,128)S(1)} %get-tuple-element.23.rest_4_), channel_id=1, source_target_pairs={{16,0},{17,1},{18,2},{19,3},{20,4},{21,5},{22,6},{23,7},{24,8},{25... | collective-permute-start | bytes 245768 | tf_op jit(solution)/shard_map/ppermute | solution.py:415
  22.6 2.0 %collective-permute-start.5 = (f32[4,24,128]{2,1,0:T(8,128)S(1)}, f32[4,24,128]{2,1,0:T(8,128)S(1)}, u32[]{:S(2)}, u32[]{:S(2)}) collective-permute-start(f32[4,24,128]{2,1,0:T(8,128)S(1)} %get-tuple-element.24), channel_id=1, source_target_pairs={{0,480},{1,481},{2,482},{3,483},{4,484},{5,485},{6,486},{7,487},{8... | collective-permute-start | bytes 147464 | tf_op jit(solution)/shard_map/ppermute | solution.py:415
  23.3 1.4 %collective-permute-start.6 = (f32[4,24,128]{2,1,0:T(8,128)S(1)}, f32[4,24,128]{2,1,0:T(8,128)S(1)}, u32[]{:S(2)}, u32[]{:S(2)}) collective-permute-start(f32[4,24,128]{2,1,0:T(8,128)S(1)} %get-tuple-element.25), channel_id=1, source_target_pairs={{0,32},{1,33},{2,34},{3,35},{4,36},{5,37},{6,38},{7,39},{8,40},{9,... | collective-permute-start | bytes 147464 | tf_op jit(solution)/shard_map/ppermute | solution.py:415
  23.9 0.7 %collective-permute-start.7 = (f32[4,24,128]{2,1,0:T(8,128)S(1)}, f32[4,24,128]{2,1,0:T(8,128)S(1)}, u32[]{:S(2)}, u32[]{:S(2)}) collective-permute-start(f32[4,24,128]{2,1,0:T(8,128)S(1)} %get-tuple-element.26), channel_id=1, source_target_pairs={{0,1},{1,0},{2,3},{3,2},{4,5},{5,4},{6,7},{7,6},{8,9},{9,8},{10,11... | collective-permute-start | bytes 147464 | tf_op jit(solution)/shard_map/ppermute | solution.py:415
  24.7 21.4 %collective-permute-start.10 = (f32[168,128]{1,0:T(8,128)S(1)}, f32[168,128]{1,0:T(8,128)S(1)}, u32[]{:S(2)}, u32[]{:S(2)}) collective-permute-start(f32[168,128]{1,0:T(8,128)S(1)} %x_lower.1.rest_4_), channel_id=1, source_target_pairs={{0,256},{1,257},{2,258},{3,259},{4,260},{5,261},{6,262},{7,263},{8... | collective-permute-start | bytes 258056 | tf_op jit(solution)/shard_map/ppermute | solution.py:415
  25.3 20.7 %collective-permute-start.8 = (f32[160,128]{1,0:T(8,128)S(1)}, f32[160,128]{1,0:T(8,128)S(1)}, u32[]{:S(2)}, u32[]{:S(2)}) collective-permute-start(f32[160,128]{1,0:T(8,128)S(1)} %y_lower.1.rest_4_), channel_id=1, source_target_pairs={{0,16},{1,17},{2,18},{3,19},{4,20},{5,21},{6,22},{7,23},{8,24},{9,... | collective-permute-start | bytes 245768 | tf_op jit(solution)/shard_map/ppermute | solution.py:415
  30.0 16.1 %collective-permute-start.9 = (f32[160,128]{1,0:T(8,128)S(1)}, f32[160,128]{1,0:T(8,128)S(1)}, u32[]{:S(2)}, u32[]{:S(2)}) collective-permute-start(f32[160,128]{1,0:T(8,128)S(1)} %x_upper.1.rest_7_), channel_id=1, source_target_pairs={{16,272},{17,273},{18,274},{19,275},{20,276},{21,277},{22,278},{23... | collective-permute-start | bytes 245768 | tf_op jit(solution)/shard_map/ppermute | solution.py:415

commit v8 on v7

--- a/solution.py
+++ b/solution.py
@@ -304,7 +304,13 @@
                 out[row : row + 8, :] = initial - scale * total
 
 
-def place_kernel(numbers, from_y0, from_y1, from_x0, from_x1, own, out, slots, staged, sems):
+def place_kernel(half, numbers, from_y, from_x, own, *rest):
+    @pl.when(upper_half() == half)
+    def _():
+        place_body(numbers, from_y, from_x, own, *rest[-4:])
+
+
+def place_body(numbers, from_y, from_x, own, out, slots, staged, sems):
     codes = [numbers[0, 3 + j] for j in range(3)]
     at_x = jnp.where(codes[1] == 4, 1, jnp.where(codes[2] == 4, 2, 0))
     at_y = jnp.where(codes[1] == 5, 1, jnp.where(codes[2] == 5, 2, 0))
@@ -315,8 +321,8 @@
         one = pl.ds(f * 2 * B, 2 * B)
         values = (
             (jnp.where(empty, 0.0, own[one, :]), at_own),
-            (from_x0[one, :] + from_x1[one, :], at_x),
-            (from_y0[one, :] + from_y1[one, :], at_y),
+            (from_x[one, :], at_x),
+            (from_y[one, :], at_y),
         )
         for v, at in values:
             slots[pl.ds(pl.multiple_of(at * BLOCK_ROWS + f * 2 * B, 2 * B), 2 * B), :] = v
@@ -387,20 +393,21 @@
     )(send_x, send_y, numbers, sweep.reshape(4, SWEEP_ROWS, 128), table, *flat, *handed, *after)
 
 
-def place(numbers, from_y, from_x, own):
+def place(name, half, numbers, from_y, from_x, own, *before):
     return pl.pallas_call(
-        place_kernel,
+        functools.partial(place_kernel, half),
         out_shape=struct(5, 3, B * B * B),
-        in_specs=[SMEM] + [VMEM] * 5,
+        in_specs=[SMEM] + [VMEM] * 3 + [HBM] * len(before),
         out_specs=HBM,
         scratch_shapes=[
             pltpu.VMEM((3 * BLOCK_ROWS, 128), jnp.float32),
             pltpu.VMEM((5, 3, B * B * B), jnp.float32),
             pltpu.SemaphoreType.DMA((5,)),
         ],
+        input_output_aliases={4: 0} if before else {},
         compiler_params=pltpu.CompilerParams(vmem_limit_bytes=LIMIT),
-        name="place",
-    )(numbers, *from_y, *from_x, own)
+        name=name,
+    )(numbers, from_y, from_x, own, *before)
 
 
 def exchange(values, move, sends):
@@ -464,8 +471,9 @@
     x_from_upper = exchange(x_upper, bx_partner, upper)
     all_faces = [[early[0]], *[list(pair) for pair in zip(early[1:], late)]]
     (own,) = update("own", None, ((2, 0),), *common, all_faces, after=(x_upper,))
-    from_y, from_x = (y_from_upper, y_from_lower), (x_from_upper, x_from_lower)
-    return place(numbers, from_y, from_x, own).transpose(1, 0, 2)
+    out = place("place_lower", False, numbers, y_from_upper, x_from_lower, own)
+    out = place("place_upper", True, numbers, y_from_lower, x_from_upper, own, out)
+    return out.transpose(1, 0, 2)
 
 
 def solution(mesh):

time: 47.3 us -> 47.3 us (level)
    pallas_call x1 -> x2, Pallas kernels: 0.9 us -> 0.95 us  [place(): pl.pallas_call(functools.partial(place_kernel, half), out_shape=struct(5,...]
where the time goes in v8:
time: 47.3 us; the launch traced here: 47 us
  starting transfers between devices  26.4 us (56%)
  waiting for transfers between devices  13.8 us (29%)
  Pallas kernels  5.25 us (11%)
  between operations  1.49 us (3%)
    ppermute x11, starting transfers between devices, exchange(): return lax.ppermute(values, ('bx', 'by'), pairs)  26.4 us
    ppermute x11, waiting for transfers between devices, exchange(): return lax.ppermute(values, ('bx', 'by'), pairs)  13.8 us
    pallas_call x1, Pallas kernels, pack(): pl.pallas_call(pack_kernel, out_shape=(pltpu.SMEM((1, 40), jnp.int32), st...  2.32 us
    pallas_call x5, Pallas kernels, update(): pl.pallas_call(functools.partial(update_kernel, half, blocks, counts, len...  1.98 us
    pallas_call x2, Pallas kernels, place(): pl.pallas_call(functools.partial(place_kernel, half), out_shape=struct(5,...  0.95 us
  transfers between devices with their start and end apart: 11, of which 2 were waited for; matrix products, arithmetic and copies ran while one was open for 0% of the time, Pallas kernels for 3%

profile of v8, /device:TPU:448, one launch (start us, length us, event | category | flops | bytes accessed | tf_op | source)
XLA Modules:
  0.0 47.0 jit_solution(940631110173939450)
XLA Ops:
  0.0 2.3 %pack.1 = (s32[1,40]{1,0:T(1,128)S(4)}, f32[2560,128]{1,0:T(8,128)S(1)}, f32[24,24,128]{2,1,0:T(8,128)S(1)}, f32[4,24,128]{2,1,0:T(8,128)S(1)}, f32[4,24,128]{2,...) custom-call(f32[5,4,4096]{2,1,0:T(4,128)} %bitcast.8, s32[1,3]{1,0:T(1,128)} %layout_in.1, ...), custom_call_target="tpu_custom_call" | custom-call | tf_op jit(solution)/shard_map/pack/pallas_call | solution.py:354
  2.3 7.3 %collective-permute-start = (f32[4,24,128]{2,1,0:T(8,128)S(1)}, f32[4,24,128]{2,1,0:T(8,128)S(1)}, u32[]{:S(2)}, u32[]{:S(2)}) collective-permute-start(f32[4,24,128]{2,1,0:T(8,128)S(1)} %get-tuple-element.19), channel_id=1, source_target_pairs={{0,31},{1,2},{2,1},{3,4},{4,3},{5,6},{6,5},{7,8},{8,7},{9,10},{10,... | collective-permute-start | bytes 147464 | tf_op jit(solution)/shard_map/ppermute | solution.py:422
  9.7 2.9 %collective-permute-start.1 = (f32[4,24,128]{2,1,0:T(8,128)S(1)}, f32[4,24,128]{2,1,0:T(8,128)S(1)}, u32[]{:S(2)}, u32[]{:S(2)}) collective-permute-start(f32[4,24,128]{2,1,0:T(8,128)S(1)} %get-tuple-element.20.rest_4_), channel_id=1, source_target_pairs={{16,496},{17,497},{18,498},{19,499},{20,500},{21,501},{22,502},{23... | collective-permute-start | bytes 147464 | tf_op jit(solution)/shard_map/ppermute | solution.py:422
  12.6 4.7 %collective-permute-start.2 = (f32[4,24,128]{2,1,0:T(8,128)S(1)}, f32[4,24,128]{2,1,0:T(8,128)S(1)}, u32[]{:S(2)}, u32[]{:S(2)}) collective-permute-start(f32[4,24,128]{2,1,0:T(8,128)S(1)} %get-tuple-element.21.rest_5_), channel_id=1, source_target_pairs={{16,48},{17,49},{18,50},{19,51},{20,52},{21,53},{22,54},{23,55},{2... | collective-permute-start | bytes 147464 | tf_op jit(solution)/shard_map/ppermute | solution.py:422
  17.4 1.9 %collective-permute-start.3 = (f32[4,24,128]{2,1,0:T(8,128)S(1)}, f32[4,24,128]{2,1,0:T(8,128)S(1)}, u32[]{:S(2)}, u32[]{:S(2)}) collective-permute-start(f32[4,24,128]{2,1,0:T(8,128)S(1)} %get-tuple-element.22.rest_6_), channel_id=1, source_target_pairs={{16,17},{17,16},{18,19},{19,18},{20,21},{21,20},{22,23},{23,22},{2... | collective-permute-start | bytes 147464 | tf_op jit(solution)/shard_map/ppermute | solution.py:422
  20.6 0.0 collective-permute-done.rest_0_
  20.6 0.0 collective-permute-done.1.rest_1_
  20.6 0.0 collective-permute-done.2.rest_2_.rest_3_
  20.6 0.0 collective-permute-done.3.rest_3_.rest_5_
  20.6 0.7 %y_upper.1 = (f32[160,128]{1,0:T(8,128)S(1)}, f32[4,24,128]{2,1,0:T(8,128)S(1)}, f32[4,24,128]{2,1,0:T(8,128)S(1)}, f32[4,24,128]{2,1,0:T(8,128)S(1)}) custom-call(s32[1,1]{1,0:T(1,128)S(6)} %copy.10.send_x, s32[1,1]{1,0:T(1,128)S(6)} %copy.11.send_y, s32[1,40]{1,0:T(1,128)S(4)} %get-tuple-element.16.numbers, f32[4,640,128]{2,1,0:T(8,128)S(1)} %bitcast.3, ...), custom_call_target="tpu_custom_call" | custom-call | tf_op jit(solution)/shard_map/y_upper/pallas_call | solution.py:378
  21.3 1.3 %collective-permute-start.8 = (f32[160,128]{1,0:T(8,128)S(1)}, f32[160,128]{1,0:T(8,128)S(1)}, u32[]{:S(2)}, u32[]{:S(2)}) collective-permute-start(f32[160,128]{1,0:T(8,128)S(1)} %get-tuple-element.26.rest_4_), channel_id=1, source_target_pairs={{16,0},{17,1},{18,2},{19,3},{20,4},{21,5},{22,6},{23,7},{24,8},{25... | collective-permute-start | bytes 245768 | tf_op jit(solution)/shard_map/ppermute | solution.py:422
  22.6 0.7 %collective-permute-start.4 = (f32[4,24,128]{2,1,0:T(8,128)S(1)}, f32[4,24,128]{2,1,0:T(8,128)S(1)}, u32[]{:S(2)}, u32[]{:S(2)}) collective-permute-start(f32[4,24,128]{2,1,0:T(8,128)S(1)} %get-tuple-element.23), channel_id=1, source_target_pairs={{0,480},{1,481},{2,482},{3,483},{4,484},{5,485},{6,486},{7,487},{8... | collective-permute-start | bytes 147464 | tf_op jit(solution)/shard_map/ppermute | solution.py:422
  23.3 0.7 %collective-permute-start.5 = (f32[4,24,128]{2,1,0:T(8,128)S(1)}, f32[4,24,128]{2,1,0:T(8,128)S(1)}, u32[]{:S(2)}, u32[]{:S(2)}) collective-permute-start(f32[4,24,128]{2,1,0:T(8,128)S(1)} %get-tuple-element.24), channel_id=1, source_target_pairs={{0,32},{1,33},{2,34},{3,35},{4,36},{5,37},{6,38},{7,39},{8,40},{9,... | collective-permute-start | bytes 147464 | tf_op jit(solution)/shard_map/ppermute | solution.py:422
  23.9 0.7 %collective-permute-start.6 = (f32[4,24,128]{2,1,0:T(8,128)S(1)}, f32[4,24,128]{2,1,0:T(8,128)S(1)}, u32[]{:S(2)}, u32[]{:S(2)}) collective-permute-start(f32[4,24,128]{2,1,0:T(8,128)S(1)} %get-tuple-element.25), channel_id=1, source_target_pairs={{0,1},{1,0},{2,3},{3,2},{4,5},{5,4},{6,7},{7,6},{8,9},{9,8},{10,11... | collective-permute-start | bytes 147464 | tf_op jit(solution)/shard_map/ppermute | solution.py:422
  24.6 0.0 collective-permute-done.4.rest_1_.rest_2_
  24.6 0.0 collective-permute-done.5.rest_2_.rest_4_
  24.6 0.0 collective-permute-done.6.rest_3_.rest_6_
  24.7 0.7 %collective-permute-start.10 = (f32[168,128]{1,0:T(8,128)S(1)}, f32[168,128]{1,0:T(8,128)S(1)}, u32[]{:S(2)}, u32[]{:S(2)}) collective-permute-start(f32[168,128]{1,0:T(8,128)S(1)} %x_lower.1.rest_4_), channel_id=1, source_target_pairs={{0,256},{1,257},{2,258},{3,259},{4,260},{5,261},{6,262},{7,263},{8... | collective-permute-start | bytes 258056 | tf_op jit(solution)/shard_map/ppermute | solution.py:422
  25.4 1.3 %collective-permute-start.7 = (f32[160,128]{1,0:T(8,128)S(1)}, f32[160,128]{1,0:T(8,128)S(1)}, u32[]{:S(2)}, u32[]{:S(2)}) collective-permute-start(f32[160,128]{1,0:T(8,128)S(1)} %y_lower.1.rest_4_), channel_id=1, source_target_pairs={{0,16},{1,17},{2,18},{3,19},{4,20},{5,21},{6,22},{7,23},{8,24},{9,... | collective-permute-start | bytes 245768 | tf_op jit(solution)/shard_map/ppermute | solution.py:422
  26.6 2.7 %collective-permute-done.8.rest_5_.from_y = f32[160,128]{1,0:T(8,128)S(1)} collective-permute-done((f32[160,128]{1,0:T(8,128)S(1)}, f32[160,128]{1,0:T(8,128)S(1)}, u32[]{:S(2)}, u32[]{:S(2)}) %collective-permute-start.8) | collective-permute-done | bytes 81952 | tf_op jit(solution)/shard_map/ppermute | solution.py:422
  29.4 0.6 %x_upper.1.rest_7_ = f32[160,128]{1,0:T(8,128)S(1)} custom-call(s32[1,1]{1,0:T(1,128)S(6)} %copy.10.send_x, s32[1,1]{1,0:T(1,128)S(6)} %copy.11.send_y, s32[1,40]{1,0:T(1,128)S(4)} %get-tuple-element.16.numbers, f32[4,640,128]{2,1,0:T(8,128)S(1)} %bitcast.6, f32[24,24,128]{2,1,0:T(8,128)S(1)} %get-tuple-element.18.table, ...), custom_call_target="tpu_custom_call" | custom-call | tf_op jit(solution)/shard_map/x_upper/pallas_call | solution.py:378
  30.0 4.2 %collective-permute-start.9 = (f32[160,128]{1,0:T(8,128)S(1)}, f32[160,128]{1,0:T(8,128)S(1)}, u32[]{:S(2)}, u32[]{:S(2)}) collective-permute-start(f32[160,128]{1,0:T(8,128)S(1)} %x_upper.1.rest_7_), channel_id=1, source_target_pairs={{16,272},{17,273},{18,274},{19,275},{20,276},{21,277},{22,278},{23... | collective-permute-start | bytes 245768 | tf_op jit(solution)/shard_map/ppermute | solution.py:422
  34.3 0.7 %own.1 = f32[160,128]{1,0:T(8,128)S(1)} custom-call(s32[1,1]{1,0:T(1,128)S(6)} %copy.10.send_x, s32[1,1]{1,0:T(1,128)S(6)} %copy.11.send_y, s32[1,40]{1,0:T(1,128)S(4)} %get-tuple-element.16.numbers, f32[4,640,128]{2,1,0:T(8,128)S(1)} %bitcast.7, f32[24,24,128]{2,1,0:T(8,128)S(1)} %get-tuple-element.18.table, ...), custom_call_target="tpu_custom_call" | custom-call | tf_op jit(solution)/shard_map/own/pallas_call | solution.py:378
  34.9 0.0 collective-permute-done.10.from_x
  34.9 0.1 place_lower.1.rest_0_
  35.0 11.1 %collective-permute-done.7.from_y = f32[160,128]{1,0:T(8,128)S(1)} collective-permute-done((f32[160,128]{1,0:T(8,128)S(1)}, f32[160,128]{1,0:T(8,128)S(1)}, u32[]{:S(2)}, u32[]{:S(2)}) %collective-permute-start.7) | collective-permute-done | bytes 81952 | tf_op jit(solution)/shard_map/ppermute | solution.py:422
  46.1 0.0 collective-permute-done.9.from_x
  46.1 0.9 %place_upper.1 = f32[5,3,4096]{2,1,0:T(4,128)} custom-call(s32[1,40]{1,0:T(1,128)S(4)} %get-tuple-element.16.numbers, f32[160,128]{1,0:T(8,128)S(1)} %collective-permute-done.7.from_y, f32[160,128]{1,0:T(8,128)S(1)} %collective-permute-done.9.from_x, f32[160,128]{1,0:T(8,128)S(1)} %own.1, ...), custom_call_target="tpu_custom_call", output_to_operand_aliasing={{}: (4, {})} | custom-call | tf_op jit(solution)/shard_map/place_upper/pallas_call | solution.py:397
  (2 shorter events, 0.0 us)
Async XLA Ops:
  2.3 18.3 %collective-permute-start = (f32[4,24,128]{2,1,0:T(8,128)S(1)}, f32[4,24,128]{2,1,0:T(8,128)S(1)}, u32[]{:S(2)}, u32[]{:S(2)}) collective-permute-start(f32[4,24,128]{2,1,0:T(8,128)S(1)} %get-tuple-element.19), channel_id=1, source_target_pairs={{0,31},{1,2},{2,1},{3,4},{4,3},{5,6},{6,5},{7,8},{8,7},{9,10},{10,... | collective-permute-start | bytes 147464 | tf_op jit(solution)/shard_map/ppermute | solution.py:422
  9.7 10.9 %collective-permute-start.1 = (f32[4,24,128]{2,1,0:T(8,128)S(1)}, f32[4,24,128]{2,1,0:T(8,128)S(1)}, u32[]{:S(2)}, u32[]{:S(2)}) collective-permute-start(f32[4,24,128]{2,1,0:T(8,128)S(1)} %get-tuple-element.20.rest_4_), channel_id=1, source_target_pairs={{16,496},{17,497},{18,498},{19,499},{20,500},{21,501},{22,502},{23... | collective-permute-start | bytes 147464 | tf_op jit(solution)/shard_map/ppermute | solution.py:422
  12.6 8.0 %collective-permute-start.2 = (f32[4,24,128]{2,1,0:T(8,128)S(1)}, f32[4,24,128]{2,1,0:T(8,128)S(1)}, u32[]{:S(2)}, u32[]{:S(2)}) collective-permute-start(f32[4,24,128]{2,1,0:T(8,128)S(1)} %get-tuple-element.21.rest_5_), channel_id=1, source_target_pairs={{16,48},{17,49},{18,50},{19,51},{20,52},{21,53},{22,54},{23,55},{2... | collective-permute-start | bytes 147464 | tf_op jit(solution)/shard_map/ppermute | solution.py:422
  17.4 3.3 %collective-permute-start.3 = (f32[4,24,128]{2,1,0:T(8,128)S(1)}, f32[4,24,128]{2,1,0:T(8,128)S(1)}, u32[]{:S(2)}, u32[]{:S(2)}) collective-permute-start(f32[4,24,128]{2,1,0:T(8,128)S(1)} %get-tuple-element.22.rest_6_), channel_id=1, source_target_pairs={{16,17},{17,16},{18,19},{19,18},{20,21},{21,20},{22,23},{23,22},{2... | collective-permute-start | bytes 147464 | tf_op jit(solution)/shard_map/ppermute | solution.py:422
  21.3 8.1 %collective-permute-start.8 = (f32[160,128]{1,0:T(8,128)S(1)}, f32[160,128]{1,0:T(8,128)S(1)}, u32[]{:S(2)}, u32[]{:S(2)}) collective-permute-start(f32[160,128]{1,0:T(8,128)S(1)} %get-tuple-element.26.rest_4_), channel_id=1, source_target_pairs={{16,0},{17,1},{18,2},{19,3},{20,4},{21,5},{22,6},{23,7},{24,8},{25... | collective-permute-start | bytes 245768 | tf_op jit(solution)/shard_map/ppermute | solution.py:422
  22.6 2.0 %collective-permute-start.4 = (f32[4,24,128]{2,1,0:T(8,128)S(1)}, f32[4,24,128]{2,1,0:T(8,128)S(1)}, u32[]{:S(2)}, u32[]{:S(2)}) collective-permute-start(f32[4,24,128]{2,1,0:T(8,128)S(1)} %get-tuple-element.23), channel_id=1, source_target_pairs={{0,480},{1,481},{2,482},{3,483},{4,484},{5,485},{6,486},{7,487},{8... | collective-permute-start | bytes 147464 | tf_op jit(solution)/shard_map/ppermute | solution.py:422
  23.3 1.4 %collective-permute-start.5 = (f32[4,24,128]{2,1,0:T(8,128)S(1)}, f32[4,24,128]{2,1,0:T(8,128)S(1)}, u32[]{:S(2)}, u32[]{:S(2)}) collective-permute-start(f32[4,24,128]{2,1,0:T(8,128)S(1)} %get-tuple-element.24), channel_id=1, source_target_pairs={{0,32},{1,33},{2,34},{3,35},{4,36},{5,37},{6,38},{7,39},{8,40},{9,... | collective-permute-start | bytes 147464 | tf_op jit(solution)/shard_map/ppermute | solution.py:422
  23.9 0.7 %collective-permute-start.6 = (f32[4,24,128]{2,1,0:T(8,128)S(1)}, f32[4,24,128]{2,1,0:T(8,128)S(1)}, u32[]{:S(2)}, u32[]{:S(2)}) collective-permute-start(f32[4,24,128]{2,1,0:T(8,128)S(1)} %get-tuple-element.25), channel_id=1, source_target_pairs={{0,1},{1,0},{2,3},{3,2},{4,5},{5,4},{6,7},{7,6},{8,9},{9,8},{10,11... | collective-permute-start | bytes 147464 | tf_op jit(solution)/shard_map/ppermute | solution.py:422
  24.7 10.3 %collective-permute-start.10 = (f32[168,128]{1,0:T(8,128)S(1)}, f32[168,128]{1,0:T(8,128)S(1)}, u32[]{:S(2)}, u32[]{:S(2)}) collective-permute-start(f32[168,128]{1,0:T(8,128)S(1)} %x_lower.1.rest_4_), channel_id=1, source_target_pairs={{0,256},{1,257},{2,258},{3,259},{4,260},{5,261},{6,262},{7,263},{8... | collective-permute-start | bytes 258056 | tf_op jit(solution)/shard_map/ppermute | solution.py:422
  25.4 20.7 %collective-permute-start.7 = (f32[160,128]{1,0:T(8,128)S(1)}, f32[160,128]{1,0:T(8,128)S(1)}, u32[]{:S(2)}, u32[]{:S(2)}) collective-permute-start(f32[160,128]{1,0:T(8,128)S(1)} %y_lower.1.rest_4_), channel_id=1, source_target_pairs={{0,16},{1,17},{2,18},{3,19},{4,20},{5,21},{6,22},{7,23},{8,24},{9,... | collective-permute-start | bytes 245768 | tf_op jit(solution)/shard_map/ppermute | solution.py:422
  30.0 16.1 %collective-permute-start.9 = (f32[160,128]{1,0:T(8,128)S(1)}, f32[160,128]{1,0:T(8,128)S(1)}, u32[]{:S(2)}, u32[]{:S(2)}) collective-permute-start(f32[160,128]{1,0:T(8,128)S(1)} %x_upper.1.rest_7_), channel_id=1, source_target_pairs={{16,272},{17,273},{18,274},{19,275},{20,276},{21,277},{22,278},{23... | collective-permute-start | bytes 245768 | tf_op jit(solution)/shard_map/ppermute | solution.py:422

commit v9 on v8

--- a/solution.py
+++ b/solution.py
@@ -461,12 +461,12 @@
     y_from_upper = exchange(y_upper, by_partner, lambda j, to_j: j >= half_y)
     late = [exchange(m, pairing, lower) for m, pairing in zip(messages, pairings[1:])]
     lower_faces = [[r] for r in (early[0], *late)]
-    (x_lower,) = update("x_lower", False, ((0, 8),), *common, lower_faces, after=(y_upper,))
+    (y_lower,) = update("y_lower", False, ((1, 8),), *common, lower_faces, after=(y_upper,))
+    y_from_lower = exchange(y_lower, by_partner, lambda j, to_j: j < half_y)
+    (x_lower,) = update("x_lower", False, ((0, 0),), *common, lower_faces, after=(y_lower,))
     x_from_lower = exchange(x_lower, bx_partner, lower)
-    (y_lower,) = update("y_lower", False, ((1, 0),), *common, lower_faces, after=(x_lower,))
-    y_from_lower = exchange(y_lower, by_partner, lambda j, to_j: j < half_y)
     (x_upper,) = update(
-        "x_upper", True, ((0, 0),), *common, upper_faces, after=(y_lower, y_from_upper)
+        "x_upper", True, ((0, 0),), *common, upper_faces, after=(x_lower, y_from_upper)
     )
     x_from_upper = exchange(x_upper, bx_partner, upper)
     all_faces = [[early[0]], *[list(pair) for pair in zip(early[1:], late)]]

time: 47.3 us -> 48.6 us (1.027)
  the two profiles are of different devices: /device:TPU:448 before, /device:TPU:32 now
where the time goes in v9:
time: 48.6 us; the launch traced here: 48.3 us
  starting transfers between devices  36.4 us (75%)
  Pallas kernels  5.26 us (11%)
  waiting for transfers between devices  5.07 us (10%)
  between operations  1.49 us (3%)
    ppermute x11, starting transfers between devices, exchange(): return lax.ppermute(values, ('bx', 'by'), pairs)  36.4 us
    ppermute x11, waiting for transfers between devices, exchange(): return lax.ppermute(values, ('bx', 'by'), pairs)  5.07 us
    pallas_call x1, Pallas kernels, pack(): pl.pallas_call(pack_kernel, out_shape=(pltpu.SMEM((1, 40), jnp.int32), st...  2.32 us
    pallas_call x5, Pallas kernels, update(): pl.pallas_call(functools.partial(update_kernel, half, blocks, counts, len...  1.98 us
  transfers between devices with their start and end apart: 11, of which 3 were waited for; matrix products, arithmetic and copies ran while one was open for 0% of the time, Pallas kernels for 6%

profile of v9, /device:TPU:32, one launch (start us, length us, event | category | flops | bytes accessed | tf_op | source)
XLA Modules:
  0.0 48.3 jit_solution(11757073057156473230)
XLA Ops:
  0.0 2.3 %pack.1 = (s32[1,40]{1,0:T(1,128)S(4)}, f32[2560,128]{1,0:T(8,128)S(1)}, f32[24,24,128]{2,1,0:T(8,128)S(1)}, f32[4,24,128]{2,1,0:T(8,128)S(1)}, f32[4,24,128]{2,...) custom-call(f32[5,4,4096]{2,1,0:T(4,128)} %bitcast.8, s32[1,3]{1,0:T(1,128)} %layout_in.1, ...), custom_call_target="tpu_custom_call" | custom-call | tf_op jit(solution)/shard_map/pack/pallas_call | solution.py:354
  2.3 13.7 %collective-permute-start = (f32[4,24,128]{2,1,0:T(8,128)S(1)}, f32[4,24,128]{2,1,0:T(8,128)S(1)}, u32[]{:S(2)}, u32[]{:S(2)}) collective-permute-start(f32[4,24,128]{2,1,0:T(8,128)S(1)} %get-tuple-element.19), channel_id=1, source_target_pairs={{0,31},{1,2},{2,1},{3,4},{4,3},{5,6},{6,5},{7,8},{8,7},{9,10},{10,... | collective-permute-start | bytes 147464 | tf_op jit(solution)/shard_map/ppermute | solution.py:422
  16.1 0.7 %collective-permute-start.1 = (f32[4,24,128]{2,1,0:T(8,128)S(1)}, f32[4,24,128]{2,1,0:T(8,128)S(1)}, u32[]{:S(2)}, u32[]{:S(2)}) collective-permute-start(f32[4,24,128]{2,1,0:T(8,128)S(1)} %get-tuple-element.20.rest_4_), channel_id=1, source_target_pairs={{16,496},{17,497},{18,498},{19,499},{20,500},{21,501},{22,502},{23... | collective-permute-start | bytes 147464 | tf_op jit(solution)/shard_map/ppermute | solution.py:422
  16.7 0.7 %collective-permute-start.2 = (f32[4,24,128]{2,1,0:T(8,128)S(1)}, f32[4,24,128]{2,1,0:T(8,128)S(1)}, u32[]{:S(2)}, u32[]{:S(2)}) collective-permute-start(f32[4,24,128]{2,1,0:T(8,128)S(1)} %get-tuple-element.21.rest_5_), channel_id=1, source_target_pairs={{16,48},{17,49},{18,50},{19,51},{20,52},{21,53},{22,54},{23,55},{2... | collective-permute-start | bytes 147464 | tf_op jit(solution)/shard_map/ppermute | solution.py:422
  17.4 0.7 %collective-permute-start.3 = (f32[4,24,128]{2,1,0:T(8,128)S(1)}, f32[4,24,128]{2,1,0:T(8,128)S(1)}, u32[]{:S(2)}, u32[]{:S(2)}) collective-permute-start(f32[4,24,128]{2,1,0:T(8,128)S(1)} %get-tuple-element.22.rest_6_), channel_id=1, source_target_pairs={{16,17},{17,16},{18,19},{19,18},{20,21},{21,20},{22,23},{23,22},{2... | collective-permute-start | bytes 147464 | tf_op jit(solution)/shard_map/ppermute | solution.py:422
  19.4 0.0 collective-permute-done.rest_0_
  19.4 0.0 collective-permute-done.1.rest_1_
  19.4 0.0 collective-permute-done.2.rest_2_.rest_3_
  19.4 0.0 collective-permute-done.3.rest_3_.rest_5_
  19.4 1.3 %collective-permute-start.8 = (f32[160,128]{1,0:T(8,128)S(1)}, f32[160,128]{1,0:T(8,128)S(1)}, u32[]{:S(2)}, u32[]{:S(2)}) collective-permute-start(f32[160,128]{1,0:T(8,128)S(1)} %get-tuple-element.26.rest_4_), channel_id=1, source_target_pairs={{16,0},{17,1},{18,2},{19,3},{20,4},{21,5},{22,6},{23,7},{24,8},{25... | collective-permute-start | bytes 245768 | tf_op jit(solution)/shard_map/ppermute | solution.py:422
  20.7 2.9 %collective-permute-start.4 = (f32[4,24,128]{2,1,0:T(8,128)S(1)}, f32[4,24,128]{2,1,0:T(8,128)S(1)}, u32[]{:S(2)}, u32[]{:S(2)}) collective-permute-start(f32[4,24,128]{2,1,0:T(8,128)S(1)} %get-tuple-element.23), channel_id=1, source_target_pairs={{0,480},{1,481},{2,482},{3,483},{4,484},{5,485},{6,486},{7,487},{8... | collective-permute-start | bytes 147464 | tf_op jit(solution)/shard_map/ppermute | solution.py:422
  23.7 6.0 %collective-permute-start.5 = (f32[4,24,128]{2,1,0:T(8,128)S(1)}, f32[4,24,128]{2,1,0:T(8,128)S(1)}, u32[]{:S(2)}, u32[]{:S(2)}) collective-permute-start(f32[4,24,128]{2,1,0:T(8,128)S(1)} %get-tuple-element.24), channel_id=1, source_target_pairs={{0,32},{1,33},{2,34},{3,35},{4,36},{5,37},{6,38},{7,39},{8,40},{9,... | collective-permute-start | bytes 147464 | tf_op jit(solution)/shard_map/ppermute | solution.py:422
  29.7 1.9 %collective-permute-start.6 = (f32[4,24,128]{2,1,0:T(8,128)S(1)}, f32[4,24,128]{2,1,0:T(8,128)S(1)}, u32[]{:S(2)}, u32[]{:S(2)}) collective-permute-start(f32[4,24,128]{2,1,0:T(8,128)S(1)} %get-tuple-element.25), channel_id=1, source_target_pairs={{0,1},{1,0},{2,3},{3,2},{4,5},{5,4},{6,7},{7,6},{8,9},{9,8},{10,11... | collective-permute-start | bytes 147464 | tf_op jit(solution)/shard_map/ppermute | solution.py:422
  31.6 0.0 collective-permute-done.4.rest_1_.rest_2_
  31.6 1.0 %collective-permute-done.5.rest_2_.rest_4_ = f32[4,24,128]{2,1,0:T(8,128)S(1)} collective-permute-done((f32[4,24,128]{2,1,0:T(8,128)S(1)}, f32[4,24,128]{2,1,0:T(8,128)S(1)}, u32[]{:S(2)}, u32[]{:S(2)}) %collective-permute-start.5) | collective-permute-done | bytes 49184 | tf_op jit(solution)/shard_map/ppermute | solution.py:422
  32.6 0.2 collective-permute-done.6.rest_3_.rest_6_
  32.8 0.6 %y_lower.1.rest_4_ = f32[168,128]{1,0:T(8,128)S(1)} custom-call(s32[1,1]{1,0:T(1,128)S(6)} %copy.10.send_x, s32[1,1]{1,0:T(1,128)S(6)} %copy.11.send_y, s32[1,40]{1,0:T(1,128)S(4)} %get-tuple-element.16.numbers, f32[4,640,128]{2,1,0:T(8,128)S(1)} %bitcast.4, f32[24,24,128]{2,1,0:T(8,128)S(1)} %get-tuple-element.18.table, ...), custom_call_target="tpu_custom_call" | custom-call | tf_op jit(solution)/shard_map/y_lower/pallas_call | solution.py:378
  33.5 5.2 %collective-permute-start.7 = (f32[168,128]{1,0:T(8,128)S(1)}, f32[168,128]{1,0:T(8,128)S(1)}, u32[]{:S(2)}, u32[]{:S(2)}) collective-permute-start(f32[168,128]{1,0:T(8,128)S(1)} %y_lower.1.rest_4_), channel_id=1, source_target_pairs={{0,16},{1,17},{2,18},{3,19},{4,20},{5,21},{6,22},{7,23},{8,24},{9,... | collective-permute-start | bytes 258056 | tf_op jit(solution)/shard_map/ppermute | solution.py:422
  38.7 0.6 %x_lower.1.rest_4_ = f32[160,128]{1,0:T(8,128)S(1)} custom-call(s32[1,1]{1,0:T(1,128)S(6)} %copy.10.send_x, s32[1,1]{1,0:T(1,128)S(6)} %copy.11.send_y, s32[1,40]{1,0:T(1,128)S(4)} %get-tuple-element.16.numbers, f32[4,640,128]{2,1,0:T(8,128)S(1)} %bitcast.5, f32[24,24,128]{2,1,0:T(8,128)S(1)} %get-tuple-element.18.table, ...), custom_call_target="tpu_custom_call" | custom-call | tf_op jit(solution)/shard_map/x_lower/pallas_call | solution.py:378
  39.3 2.7 %collective-permute-start.10 = (f32[160,128]{1,0:T(8,128)S(1)}, f32[160,128]{1,0:T(8,128)S(1)}, u32[]{:S(2)}, u32[]{:S(2)}) collective-permute-start(f32[160,128]{1,0:T(8,128)S(1)} %x_lower.1.rest_4_), channel_id=1, source_target_pairs={{0,256},{1,257},{2,258},{3,259},{4,260},{5,261},{6,262},{7,263},{8... | collective-permute-start | bytes 245768 | tf_op jit(solution)/shard_map/ppermute | solution.py:422
  42.0 0.0 collective-permute-done.8.rest_5_.from_y
  42.1 0.7 %collective-permute-start.9 = (f32[160,128]{1,0:T(8,128)S(1)}, f32[160,128]{1,0:T(8,128)S(1)}, u32[]{:S(2)}, u32[]{:S(2)}) collective-permute-start(f32[160,128]{1,0:T(8,128)S(1)} %x_upper.1.rest_7_), channel_id=1, source_target_pairs={{16,272},{17,273},{18,274},{19,275},{20,276},{21,277},{22,278},{23... | collective-permute-start | bytes 245768 | tf_op jit(solution)/shard_map/ppermute | solution.py:422
  42.7 0.7 %own.1 = f32[160,128]{1,0:T(8,128)S(1)} custom-call(s32[1,1]{1,0:T(1,128)S(6)} %copy.10.send_x, s32[1,1]{1,0:T(1,128)S(6)} %copy.11.send_y, s32[1,40]{1,0:T(1,128)S(4)} %get-tuple-element.16.numbers, f32[4,640,128]{2,1,0:T(8,128)S(1)} %bitcast.7, f32[24,24,128]{2,1,0:T(8,128)S(1)} %get-tuple-element.18.table, ...), custom_call_target="tpu_custom_call" | custom-call | tf_op jit(solution)/shard_map/own/pallas_call | solution.py:378
  43.4 3.9 %collective-permute-done.10.from_x = f32[160,128]{1,0:T(8,128)S(1)} collective-permute-done((f32[160,128]{1,0:T(8,128)S(1)}, f32[160,128]{1,0:T(8,128)S(1)}, u32[]{:S(2)}, u32[]{:S(2)}) %collective-permute-start.10) | collective-permute-done | bytes 81952 | tf_op jit(solution)/shard_map/ppermute | solution.py:422
  47.3 0.9 %place_lower.1.rest_0_ = f32[5,3,4096]{2,1,0:T(4,128)} custom-call(s32[1,40]{1,0:T(1,128)S(4)} %get-tuple-element.16.numbers, f32[160,128]{1,0:T(8,128)S(1)} %collective-permute-done.8.rest_5_.from_y, f32[160,128]{1,0:T(8,128)S(1)} %collective-permute-done.10.from_x, f32[160,128]{1,0:T(8,128)S(1)} %own.1), custom_call_target="tpu_custom_call" | custom-call | tf_op jit(solution)/shard_map/place_lower/pallas_call | solution.py:397
  48.2 0.0 collective-permute-done.7.from_y
  48.2 0.0 collective-permute-done.9.from_x
  48.2 0.1 place_upper.1
  (2 shorter events, 0.0 us)
Async XLA Ops:
  2.3 17.0 %collective-permute-start = (f32[4,24,128]{2,1,0:T(8,128)S(1)}, f32[4,24,128]{2,1,0:T(8,128)S(1)}, u32[]{:S(2)}, u32[]{:S(2)}) collective-permute-start(f32[4,24,128]{2,1,0:T(8,128)S(1)} %get-tuple-element.19), channel_id=1, source_target_pairs={{0,31},{1,2},{2,1},{3,4},{4,3},{5,6},{6,5},{7,8},{8,7},{9,10},{10,... | collective-permute-start | bytes 147464 | tf_op jit(solution)/shard_map/ppermute | solution.py:422
  16.1 3.3 %collective-permute-start.1 = (f32[4,24,128]{2,1,0:T(8,128)S(1)}, f32[4,24,128]{2,1,0:T(8,128)S(1)}, u32[]{:S(2)}, u32[]{:S(2)}) collective-permute-start(f32[4,24,128]{2,1,0:T(8,128)S(1)} %get-tuple-element.20.rest_4_), channel_id=1, source_target_pairs={{16,496},{17,497},{18,498},{19,499},{20,500},{21,501},{22,502},{23... | collective-permute-start | bytes 147464 | tf_op jit(solution)/shard_map/ppermute | solution.py:422
  16.7 2.7 %collective-permute-start.2 = (f32[4,24,128]{2,1,0:T(8,128)S(1)}, f32[4,24,128]{2,1,0:T(8,128)S(1)}, u32[]{:S(2)}, u32[]{:S(2)}) collective-permute-start(f32[4,24,128]{2,1,0:T(8,128)S(1)} %get-tuple-element.21.rest_5_), channel_id=1, source_target_pairs={{16,48},{17,49},{18,50},{19,51},{20,52},{21,53},{22,54},{23,55},{2... | collective-permute-start | bytes 147464 | tf_op jit(solution)/shard_map/ppermute | solution.py:422
  17.4 2.0 %collective-permute-start.3 = (f32[4,24,128]{2,1,0:T(8,128)S(1)}, f32[4,24,128]{2,1,0:T(8,128)S(1)}, u32[]{:S(2)}, u32[]{:S(2)}) collective-permute-start(f32[4,24,128]{2,1,0:T(8,128)S(1)} %get-tuple-element.22.rest_6_), channel_id=1, source_target_pairs={{16,17},{17,16},{18,19},{19,18},{20,21},{21,20},{22,23},{23,22},{2... | collective-permute-start | bytes 147464 | tf_op jit(solution)/shard_map/ppermute | solution.py:422
  19.4 22.6 %collective-permute-start.8 = (f32[160,128]{1,0:T(8,128)S(1)}, f32[160,128]{1,0:T(8,128)S(1)}, u32[]{:S(2)}, u32[]{:S(2)}) collective-permute-start(f32[160,128]{1,0:T(8,128)S(1)} %get-tuple-element.26.rest_4_), channel_id=1, source_target_pairs={{16,0},{17,1},{18,2},{19,3},{20,4},{21,5},{22,6},{23,7},{24,8},{25... | collective-permute-start | bytes 245768 | tf_op jit(solution)/shard_map/ppermute | solution.py:422
  20.7 10.9 %collective-permute-start.4 = (f32[4,24,128]{2,1,0:T(8,128)S(1)}, f32[4,24,128]{2,1,0:T(8,128)S(1)}, u32[]{:S(2)}, u32[]{:S(2)}) collective-permute-start(f32[4,24,128]{2,1,0:T(8,128)S(1)} %get-tuple-element.23), channel_id=1, source_target_pairs={{0,480},{1,481},{2,482},{3,483},{4,484},{5,485},{6,486},{7,487},{8... | collective-permute-start | bytes 147464 | tf_op jit(solution)/shard_map/ppermute | solution.py:422
  23.7 9.0 %collective-permute-start.5 = (f32[4,24,128]{2,1,0:T(8,128)S(1)}, f32[4,24,128]{2,1,0:T(8,128)S(1)}, u32[]{:S(2)}, u32[]{:S(2)}) collective-permute-start(f32[4,24,128]{2,1,0:T(8,128)S(1)} %get-tuple-element.24), channel_id=1, source_target_pairs={{0,32},{1,33},{2,34},{3,35},{4,36},{5,37},{6,38},{7,39},{8,40},{9,... | collective-permute-start | bytes 147464 | tf_op jit(solution)/shard_map/ppermute | solution.py:422
  29.7 3.1 %collective-permute-start.6 = (f32[4,24,128]{2,1,0:T(8,128)S(1)}, f32[4,24,128]{2,1,0:T(8,128)S(1)}, u32[]{:S(2)}, u32[]{:S(2)}) collective-permute-start(f32[4,24,128]{2,1,0:T(8,128)S(1)} %get-tuple-element.25), channel_id=1, source_target_pairs={{0,1},{1,0},{2,3},{3,2},{4,5},{5,4},{6,7},{7,6},{8,9},{9,8},{10,11... | collective-permute-start | bytes 147464 | tf_op jit(solution)/shard_map/ppermute | solution.py:422
  33.5 14.7 %collective-permute-start.7 = (f32[168,128]{1,0:T(8,128)S(1)}, f32[168,128]{1,0:T(8,128)S(1)}, u32[]{:S(2)}, u32[]{:S(2)}) collective-permute-start(f32[168,128]{1,0:T(8,128)S(1)} %y_lower.1.rest_4_), channel_id=1, source_target_pairs={{0,16},{1,17},{2,18},{3,19},{4,20},{5,21},{6,22},{7,23},{8,24},{9,... | collective-permute-start | bytes 258056 | tf_op jit(solution)/shard_map/ppermute | solution.py:422
  39.3 8.0 %collective-permute-start.10 = (f32[160,128]{1,0:T(8,128)S(1)}, f32[160,128]{1,0:T(8,128)S(1)}, u32[]{:S(2)}, u32[]{:S(2)}) collective-permute-start(f32[160,128]{1,0:T(8,128)S(1)} %x_lower.1.rest_4_), channel_id=1, source_target_pairs={{0,256},{1,257},{2,258},{3,259},{4,260},{5,261},{6,262},{7,263},{8... | collective-permute-start | bytes 245768 | tf_op jit(solution)/shard_map/ppermute | solution.py:422
  42.1 6.1 %collective-permute-start.9 = (f32[160,128]{1,0:T(8,128)S(1)}, f32[160,128]{1,0:T(8,128)S(1)}, u32[]{:S(2)}, u32[]{:S(2)}) collective-permute-start(f32[160,128]{1,0:T(8,128)S(1)} %x_upper.1.rest_7_), channel_id=1, source_target_pairs={{16,272},{17,273},{18,274},{19,275},{20,276},{21,277},{22,278},{23... | collective-permute-start | bytes 245768 | tf_op jit(solution)/shard_map/ppermute | solution.py:422

commit v10 on v8

--- a/solution.py
+++ b/solution.py
@@ -141,7 +141,10 @@
                             ]
     for copy in small:
         copy.wait()
-    for m, one_list in enumerate((2 + (1 - odd_y), 1 - odd_x, odd_x, 2 + odd_y)):
+    upper = upper_half()
+    other, same = 1 - odd_x, odd_x
+    second, third = jnp.where(upper, other, same), jnp.where(upper, same, other)
+    for m, one_list in enumerate((2 + (1 - odd_y), second, third, 2 + odd_y)):
         for k in range(4):
             messages[m][k] = table[face_out[0, one_list, k]]
     codes = [layout[0, j] for j in range(3)]
@@ -450,17 +453,23 @@
         cells_in.transpose(1, 0, 2), layout, block_levels, ghost_src, face_out
     )
     common = (send_x, send_y, numbers, sweep, table)
-    early = [
-        exchange(m, pairing, sends)
-        for m, pairing, sends in zip(messages, pairings, (anyone, upper, upper, upper))
-    ]
-    upper_faces = [[r] for r in early]
+    odd_by, odd_bx, even_bx, even_by = pairings
+
+    def mixed(i, j):
+        return (odd_bx if j >= half_y else even_bx)(i, j)
+
+    first = exchange(messages[0], odd_by, anyone)
+    second = exchange(messages[1], mixed, anyone)
+    third = exchange(messages[2], even_bx, upper)
+    fourth = exchange(messages[3], even_by, upper)
+    upper_faces = [[first], [second], [third], [fourth]]
     y_upper, *messages = update(
-        "y_upper", True, ((1, 0),), *common, upper_faces, handed=messages[1:]
+        "y_upper", True, ((1, 0),), *common, upper_faces, handed=messages[2:]
     )
     y_from_upper = exchange(y_upper, by_partner, lambda j, to_j: j >= half_y)
-    late = [exchange(m, pairing, lower) for m, pairing in zip(messages, pairings[1:])]
-    lower_faces = [[r] for r in (early[0], *late)]
+    third = exchange(messages[0], odd_bx, lower)
+    fourth = exchange(messages[1], even_by, lower)
+    lower_faces = [[first], [third], [second], [fourth]]
     (x_lower,) = update("x_lower", False, ((0, 8),), *common, lower_faces, after=(y_upper,))
     x_from_lower = exchange(x_lower, bx_partner, lower)
     (y_lower,) = update("y_lower", False, ((1, 0),), *common, lower_faces, after=(x_lower,))
@@ -469,10 +478,10 @@
         "x_upper", True, ((0, 0),), *common, upper_faces, after=(y_lower, y_from_upper)
     )
     x_from_upper = exchange(x_upper, bx_partner, upper)
-    all_faces = [[early[0]], *[list(pair) for pair in zip(early[1:], late)]]
-    (own,) = update("own", None, ((2, 0),), *common, all_faces, after=(x_upper,))
-    out = place("place_lower", False, numbers, y_from_upper, x_from_lower, own)
-    out = place("place_upper", True, numbers, y_from_lower, x_from_upper, own, out)
+    (own_upper,) = update("own_upper", True, ((2, 0),), *common, upper_faces, after=(x_upper,))
+    (own_lower,) = update("own_lower", False, ((2, 0),), *common, lower_faces, after=(x_upper,))
+    out = place("place_lower", False, numbers, y_from_upper, x_from_lower, own_lower)
+    out = place("place_upper", True, numbers, y_from_lower, x_from_upper, own_upper, out)
     return out.transpose(1, 0, 2)
 
 

time: 47.3 us -> 46.7 us (0.987)
  the two profiles are of different devices: /device:TPU:448 before, /device:TPU:32 now
where the time goes in v10:
time: 46.7 us; the launch traced here: 46.4 us
  starting transfers between devices  32.3 us (69%)
  waiting for transfers between devices  7.37 us (16%)
  Pallas kernels  5.23 us (11%)
  between operations  1.44 us (3%)
    ppermute x10, starting transfers between devices, exchange(): return lax.ppermute(values, ('bx', 'by'), pairs)  32.3 us
    ppermute x10, waiting for transfers between devices, exchange(): return lax.ppermute(values, ('bx', 'by'), pairs)  7.37 us
    pallas_call x1, Pallas kernels, pack(): pl.pallas_call(pack_kernel, out_shape=(pltpu.SMEM((1, 40), jnp.int32), st...  2.32 us
    pallas_call x6, Pallas kernels, update(): pl.pallas_call(functools.partial(update_kernel, half, blocks, counts, len...  1.96 us
    pallas_call x2, Pallas kernels, place(): pl.pallas_call(functools.partial(place_kernel, half), out_shape=struct(5,...  0.95 us
  transfers between devices with their start and end apart: 10, of which 4 were waited for; matrix products, arithmetic and copies ran while one was open for 0% of the time, Pallas kernels for 6%

profile of v10, /device:TPU:32, one launch (start us, length us, event | category | flops | bytes accessed | tf_op | source)
XLA Modules:
  0.0 46.4 jit_solution(17535049689209204084)
XLA Ops:
  0.0 2.3 %pack.1 = (s32[1,40]{1,0:T(1,128)S(4)}, f32[2560,128]{1,0:T(8,128)S(1)}, f32[24,24,128]{2,1,0:T(8,128)S(1)}, f32[4,24,128]{2,1,0:T(8,128)S(1)}, f32[4,24,128]{2,...) custom-call(f32[5,4,4096]{2,1,0:T(4,128)} %bitcast.9, s32[1,3]{1,0:T(1,128)} %layout_in.1, ...), custom_call_target="tpu_custom_call" | custom-call | tf_op jit(solution)/shard_map/pack/pallas_call | solution.py:357
  2.3 13.7 %collective-permute-start = (f32[4,24,128]{2,1,0:T(8,128)S(1)}, f32[4,24,128]{2,1,0:T(8,128)S(1)}, u32[]{:S(2)}, u32[]{:S(2)}) collective-permute-start(f32[4,24,128]{2,1,0:T(8,128)S(1)} %get-tuple-element.18), channel_id=1, source_target_pairs={{0,31},{1,2},{2,1},{3,4},{4,3},{5,6},{6,5},{7,8},{8,7},{9,10},{10,... | collective-permute-start | bytes 147464 | tf_op jit(solution)/shard_map/ppermute | solution.py:425
  16.1 2.9 %collective-permute-start.1 = (f32[4,24,128]{2,1,0:T(8,128)S(1)}, f32[4,24,128]{2,1,0:T(8,128)S(1)}, u32[]{:S(2)}, u32[]{:S(2)}) collective-permute-start(f32[4,24,128]{2,1,0:T(8,128)S(1)} %get-tuple-element.19), channel_id=1, source_target_pairs={{0,32},{1,33},{2,34},{3,35},{4,36},{5,37},{6,38},{7,39},{8,40},{9,... | collective-permute-start | bytes 147464 | tf_op jit(solution)/shard_map/ppermute | solution.py:425
  19.0 0.7 %collective-permute-start.2 = (f32[4,24,128]{2,1,0:T(8,128)S(1)}, f32[4,24,128]{2,1,0:T(8,128)S(1)}, u32[]{:S(2)}, u32[]{:S(2)}) collective-permute-start(f32[4,24,128]{2,1,0:T(8,128)S(1)} %get-tuple-element.20.rest_4_), channel_id=1, source_target_pairs={{16,48},{17,49},{18,50},{19,51},{20,52},{21,53},{22,54},{23,55},{2... | collective-permute-start | bytes 147464 | tf_op jit(solution)/shard_map/ppermute | solution.py:425
  19.7 0.7 %collective-permute-start.3 = (f32[4,24,128]{2,1,0:T(8,128)S(1)}, f32[4,24,128]{2,1,0:T(8,128)S(1)}, u32[]{:S(2)}, u32[]{:S(2)}) collective-permute-start(f32[4,24,128]{2,1,0:T(8,128)S(1)} %get-tuple-element.21.rest_5_), channel_id=1, source_target_pairs={{16,17},{17,16},{18,19},{19,18},{20,21},{21,20},{22,23},{23,22},{2... | collective-permute-start | bytes 147464 | tf_op jit(solution)/shard_map/ppermute | solution.py:425
  21.6 0.0 collective-permute-done.rest_0_
  21.6 0.9 %collective-permute-done.1.rest_1_.rest_2_ = f32[4,24,128]{2,1,0:T(8,128)S(1)} collective-permute-done((f32[4,24,128]{2,1,0:T(8,128)S(1)}, f32[4,24,128]{2,1,0:T(8,128)S(1)}, u32[]{:S(2)}, u32[]{:S(2)}) %collective-permute-start.1) | collective-permute-done | bytes 49184 | tf_op jit(solution)/shard_map/ppermute | solution.py:425
  22.5 0.0 collective-permute-done.2.rest_2_
  22.5 0.0 collective-permute-done.3.rest_3_
  22.6 1.3 %collective-permute-start.7 = (f32[160,128]{1,0:T(8,128)S(1)}, f32[160,128]{1,0:T(8,128)S(1)}, u32[]{:S(2)}, u32[]{:S(2)}) collective-permute-start(f32[160,128]{1,0:T(8,128)S(1)} %get-tuple-element.24.rest_4_), channel_id=1, source_target_pairs={{16,0},{17,1},{18,2},{19,3},{20,4},{21,5},{22,6},{23,7},{24,8},{25... | collective-permute-start | bytes 245768 | tf_op jit(solution)/shard_map/ppermute | solution.py:425
  23.9 2.4 %collective-permute-start.4 = (f32[4,24,128]{2,1,0:T(8,128)S(1)}, f32[4,24,128]{2,1,0:T(8,128)S(1)}, u32[]{:S(2)}, u32[]{:S(2)}) collective-permute-start(f32[4,24,128]{2,1,0:T(8,128)S(1)} %get-tuple-element.22), channel_id=1, source_target_pairs={{0,480},{1,481},{2,482},{3,483},{4,484},{5,485},{6,486},{7,487},{8... | collective-permute-start | bytes 147464 | tf_op jit(solution)/shard_map/ppermute | solution.py:425
  26.3 1.9 %collective-permute-start.5 = (f32[4,24,128]{2,1,0:T(8,128)S(1)}, f32[4,24,128]{2,1,0:T(8,128)S(1)}, u32[]{:S(2)}, u32[]{:S(2)}) collective-permute-start(f32[4,24,128]{2,1,0:T(8,128)S(1)} %get-tuple-element.23), channel_id=1, source_target_pairs={{0,1},{1,0},{2,3},{3,2},{4,5},{5,4},{6,7},{7,6},{8,9},{9,8},{10,11... | collective-permute-start | bytes 147464 | tf_op jit(solution)/shard_map/ppermute | solution.py:425
  28.2 1.6 %collective-permute-done.4.rest_1_ = f32[4,24,128]{2,1,0:T(8,128)S(1)} collective-permute-done((f32[4,24,128]{2,1,0:T(8,128)S(1)}, f32[4,24,128]{2,1,0:T(8,128)S(1)}, u32[]{:S(2)}, u32[]{:S(2)}) %collective-permute-start.4) | collective-permute-done | bytes 49184 | tf_op jit(solution)/shard_map/ppermute | solution.py:425
  29.8 0.0 collective-permute-done.5.rest_3_
  29.9 0.6 %x_lower.1.rest_4_ = f32[168,128]{1,0:T(8,128)S(1)} custom-call(s32[1,1]{1,0:T(1,128)S(6)} %copy.10.send_x, s32[1,1]{1,0:T(1,128)S(6)} %copy.11.send_y, s32[1,40]{1,0:T(1,128)S(4)} %get-tuple-element.15.numbers, f32[4,640,128]{2,1,0:T(8,128)S(1)} %bitcast.4, f32[24,24,128]{2,1,0:T(8,128)S(1)} %get-tuple-element.17.table, ...), custom_call_target="tpu_custom_call" | custom-call | tf_op jit(solution)/shard_map/x_lower/pallas_call | solution.py:381
  30.5 4.5 %collective-permute-start.9 = (f32[168,128]{1,0:T(8,128)S(1)}, f32[168,128]{1,0:T(8,128)S(1)}, u32[]{:S(2)}, u32[]{:S(2)}) collective-permute-start(f32[168,128]{1,0:T(8,128)S(1)} %x_lower.1.rest_4_), channel_id=1, source_target_pairs={{0,256},{1,257},{2,258},{3,259},{4,260},{5,261},{6,262},{7,263},{8... | collective-permute-start | bytes 258056 | tf_op jit(solution)/shard_map/ppermute | solution.py:425
  35.0 0.6 %y_lower.1.rest_4_ = f32[160,128]{1,0:T(8,128)S(1)} custom-call(s32[1,1]{1,0:T(1,128)S(6)} %copy.10.send_x, s32[1,1]{1,0:T(1,128)S(6)} %copy.11.send_y, s32[1,40]{1,0:T(1,128)S(4)} %get-tuple-element.15.numbers, f32[4,640,128]{2,1,0:T(8,128)S(1)} %bitcast.5, f32[24,24,128]{2,1,0:T(8,128)S(1)} %get-tuple-element.17.table, ...), custom_call_target="tpu_custom_call" | custom-call | tf_op jit(solution)/shard_map/y_lower/pallas_call | solution.py:381
  35.7 3.6 %collective-permute-start.6 = (f32[160,128]{1,0:T(8,128)S(1)}, f32[160,128]{1,0:T(8,128)S(1)}, u32[]{:S(2)}, u32[]{:S(2)}) collective-permute-start(f32[160,128]{1,0:T(8,128)S(1)} %y_lower.1.rest_4_), channel_id=1, source_target_pairs={{0,16},{1,17},{2,18},{3,19},{4,20},{5,21},{6,22},{7,23},{8,24},{9,... | collective-permute-start | bytes 245768 | tf_op jit(solution)/shard_map/ppermute | solution.py:425
  39.2 0.3 collective-permute-done.7.rest_5_.from_y
  39.5 0.7 %collective-permute-start.8 = (f32[160,128]{1,0:T(8,128)S(1)}, f32[160,128]{1,0:T(8,128)S(1)}, u32[]{:S(2)}, u32[]{:S(2)}) collective-permute-start(f32[160,128]{1,0:T(8,128)S(1)} %x_upper.1.rest_4_), channel_id=1, source_target_pairs={{16,272},{17,273},{18,274},{19,275},{20,276},{21,277},{22,278},{23... | collective-permute-start | bytes 245768 | tf_op jit(solution)/shard_map/ppermute | solution.py:425
  40.2 0.6 %own_lower.1.own = f32[160,128]{1,0:T(8,128)S(1)} custom-call(s32[1,1]{1,0:T(1,128)S(6)} %copy.10.send_x, s32[1,1]{1,0:T(1,128)S(6)} %copy.11.send_y, s32[1,40]{1,0:T(1,128)S(4)} %get-tuple-element.15.numbers, f32[4,640,128]{2,1,0:T(8,128)S(1)} %bitcast.7, f32[24,24,128]{2,1,0:T(8,128)S(1)} %get-tuple-element.17.table, ...), custom_call_target="tpu_custom_call" | custom-call | tf_op jit(solution)/shard_map/own_lower/pallas_call | solution.py:381
  40.8 0.0 collective-permute-done.9.from_x
  40.9 0.9 %place_lower.1.rest_0_ = f32[5,3,4096]{2,1,0:T(4,128)} custom-call(s32[1,40]{1,0:T(1,128)S(4)} %get-tuple-element.15.numbers, f32[160,128]{1,0:T(8,128)S(1)} %collective-permute-done.7.rest_5_.from_y, f32[168,128]{1,0:T(8,128)S(1)} %collective-permute-done.9.from_x, f32[160,128]{1,0:T(8,128)S(1)} %own_lower.1.own), custom_call_target="tpu_custom_call" | custom-call | tf_op jit(solution)/shard_map/place_lower/pallas_call | solution.py:400
  41.8 4.5 %collective-permute-done.6.from_y = f32[160,128]{1,0:T(8,128)S(1)} collective-permute-done((f32[160,128]{1,0:T(8,128)S(1)}, f32[160,128]{1,0:T(8,128)S(1)}, u32[]{:S(2)}, u32[]{:S(2)}) %collective-permute-start.6) | collective-permute-done | bytes 81952 | tf_op jit(solution)/shard_map/ppermute | solution.py:425
  46.3 0.0 collective-permute-done.8.from_x
  (4 shorter events, 0.1 us)
Async XLA Ops:
  2.3 19.3 %collective-permute-start = (f32[4,24,128]{2,1,0:T(8,128)S(1)}, f32[4,24,128]{2,1,0:T(8,128)S(1)}, u32[]{:S(2)}, u32[]{:S(2)}) collective-permute-start(f32[4,24,128]{2,1,0:T(8,128)S(1)} %get-tuple-element.18), channel_id=1, source_target_pairs={{0,31},{1,2},{2,1},{3,4},{4,3},{5,6},{6,5},{7,8},{8,7},{9,10},{10,... | collective-permute-start | bytes 147464 | tf_op jit(solution)/shard_map/ppermute | solution.py:425
  16.1 6.5 %collective-permute-start.1 = (f32[4,24,128]{2,1,0:T(8,128)S(1)}, f32[4,24,128]{2,1,0:T(8,128)S(1)}, u32[]{:S(2)}, u32[]{:S(2)}) collective-permute-start(f32[4,24,128]{2,1,0:T(8,128)S(1)} %get-tuple-element.19), channel_id=1, source_target_pairs={{0,32},{1,33},{2,34},{3,35},{4,36},{5,37},{6,38},{7,39},{8,40},{9,... | collective-permute-start | bytes 147464 | tf_op jit(solution)/shard_map/ppermute | solution.py:425
  19.0 3.6 %collective-permute-start.2 = (f32[4,24,128]{2,1,0:T(8,128)S(1)}, f32[4,24,128]{2,1,0:T(8,128)S(1)}, u32[]{:S(2)}, u32[]{:S(2)}) collective-permute-start(f32[4,24,128]{2,1,0:T(8,128)S(1)} %get-tuple-element.20.rest_4_), channel_id=1, source_target_pairs={{16,48},{17,49},{18,50},{19,51},{20,52},{21,53},{22,54},{23,55},{2... | collective-permute-start | bytes 147464 | tf_op jit(solution)/shard_map/ppermute | solution.py:425
  19.7 2.9 %collective-permute-start.3 = (f32[4,24,128]{2,1,0:T(8,128)S(1)}, f32[4,24,128]{2,1,0:T(8,128)S(1)}, u32[]{:S(2)}, u32[]{:S(2)}) collective-permute-start(f32[4,24,128]{2,1,0:T(8,128)S(1)} %get-tuple-element.21.rest_5_), channel_id=1, source_target_pairs={{16,17},{17,16},{18,19},{19,18},{20,21},{21,20},{22,23},{23,22},{2... | collective-permute-start | bytes 147464 | tf_op jit(solution)/shard_map/ppermute | solution.py:425
  22.6 16.9 %collective-permute-start.7 = (f32[160,128]{1,0:T(8,128)S(1)}, f32[160,128]{1,0:T(8,128)S(1)}, u32[]{:S(2)}, u32[]{:S(2)}) collective-permute-start(f32[160,128]{1,0:T(8,128)S(1)} %get-tuple-element.24.rest_4_), channel_id=1, source_target_pairs={{16,0},{17,1},{18,2},{19,3},{20,4},{21,5},{22,6},{23,7},{24,8},{25... | collective-permute-start | bytes 245768 | tf_op jit(solution)/shard_map/ppermute | solution.py:425
  23.9 6.0 %collective-permute-start.4 = (f32[4,24,128]{2,1,0:T(8,128)S(1)}, f32[4,24,128]{2,1,0:T(8,128)S(1)}, u32[]{:S(2)}, u32[]{:S(2)}) collective-permute-start(f32[4,24,128]{2,1,0:T(8,128)S(1)} %get-tuple-element.22), channel_id=1, source_target_pairs={{0,480},{1,481},{2,482},{3,483},{4,484},{5,485},{6,486},{7,487},{8... | collective-permute-start | bytes 147464 | tf_op jit(solution)/shard_map/ppermute | solution.py:425
  26.3 3.5 %collective-permute-start.5 = (f32[4,24,128]{2,1,0:T(8,128)S(1)}, f32[4,24,128]{2,1,0:T(8,128)S(1)}, u32[]{:S(2)}, u32[]{:S(2)}) collective-permute-start(f32[4,24,128]{2,1,0:T(8,128)S(1)} %get-tuple-element.23), channel_id=1, source_target_pairs={{0,1},{1,0},{2,3},{3,2},{4,5},{5,4},{6,7},{7,6},{8,9},{9,8},{10,11... | collective-permute-start | bytes 147464 | tf_op jit(solution)/shard_map/ppermute | solution.py:425
  30.5 10.4 %collective-permute-start.9 = (f32[168,128]{1,0:T(8,128)S(1)}, f32[168,128]{1,0:T(8,128)S(1)}, u32[]{:S(2)}, u32[]{:S(2)}) collective-permute-start(f32[168,128]{1,0:T(8,128)S(1)} %x_lower.1.rest_4_), channel_id=1, source_target_pairs={{0,256},{1,257},{2,258},{3,259},{4,260},{5,261},{6,262},{7,263},{8... | collective-permute-start | bytes 258056 | tf_op jit(solution)/shard_map/ppermute | solution.py:425
  35.7 10.7 %collective-permute-start.6 = (f32[160,128]{1,0:T(8,128)S(1)}, f32[160,128]{1,0:T(8,128)S(1)}, u32[]{:S(2)}, u32[]{:S(2)}) collective-permute-start(f32[160,128]{1,0:T(8,128)S(1)} %y_lower.1.rest_4_), channel_id=1, source_target_pairs={{0,16},{1,17},{2,18},{3,19},{4,20},{5,21},{6,22},{7,23},{8,24},{9,... | collective-permute-start | bytes 245768 | tf_op jit(solution)/shard_map/ppermute | solution.py:425
  39.5 6.8 %collective-permute-start.8 = (f32[160,128]{1,0:T(8,128)S(1)}, f32[160,128]{1,0:T(8,128)S(1)}, u32[]{:S(2)}, u32[]{:S(2)}) collective-permute-start(f32[160,128]{1,0:T(8,128)S(1)} %x_upper.1.rest_4_), channel_id=1, source_target_pairs={{16,272},{17,273},{18,274},{19,275},{20,276},{21,277},{22,278},{23... | collective-permute-start | bytes 245768 | tf_op jit(solution)/shard_map/ppermute | solution.py:425
